TPU v7x, 32 devices: a whole 2x2x4 slice. The times are simulated.
32 devices in a mesh: ply: 4 (over x, core), tile: 8 (over z, y).
Axes of the slice: x: 2, y: 2, z: 4, core: 2. Of those that a mesh axis runs over, the one named last changes fastest.
Arguments:
- displacement: float32 [3, 24, 64, 1024], P(None, 'ply', 'tile'), may hold values from -0.2 to 0.2
- angle_index: int32 [24], P('ply'), may hold values from 0 to 3
- bond_table: float32 [4, 14], replicated, may hold values from 5 to 50
- interface_stiffness: float32 [23], replicated, may hold values from 2 to 20
Outputs:
- force_density: float32 [3, 24, 64, 1024], P(None, 'ply', 'tile')
Inputs may be any that keep to these rules, and one draw needn't show every extreme that they name: `angle_index`: each ply's fibre orientation is an index into the rows of bond_table.
All inputs are finite; a program needn't handle non-finite values.
Results may differ from a plain program's by a relative error of at most 0.000058.
Values sent between devices are 32-bit elements; how exact they have to be, the bound alone decides.
No kernel may reach another device: no remote copies, remote signals or barrier semaphores. Data moves between devices by JAX's collectives and lax.ppermute only.
A program may use at most 128 MiB of HBM per device.

v0:
```python
import math

import jax
import jax.numpy as jnp
from jax import lax
from jax.sharding import PartitionSpec as P

bulk_modulus = 40.0


def padded_2(shard, sides, width):
    for axis, dim in sides:
        peers, length = (lax.axis_size(axis), shard.shape[dim])
        up = [(i, (i + 1) % peers) for i in range(peers - 1)]
        down = [(j, i) for i, j in up]
        last = lax.slice_in_dim(shard, length - width, length, axis=dim)
        first = lax.slice_in_dim(shard, 0, width, axis=dim)
        before = lax.ppermute(last, axis, up)
        after = lax.ppermute(first, axis, down)
        shard = jnp.concatenate([before, shard, after], axis=dim)
    return shard


def bond_list():
    halves = []
    for shift_x in range(-3, 4):
        for shift_y in range(-3, 4):
            radius = shift_x * shift_x + shift_y * shift_y
            if 0 < radius <= 9 and (shift_x > 0 or (shift_x == 0 and shift_y > 0)):
                halves.append((shift_x, shift_y))
    result = []
    for shift_x in range(-3, 4):
        for shift_y in range(-3, 4):
            radius = shift_x * shift_x + shift_y * shift_y
            if 0 < radius <= 9:
                if (shift_x, shift_y) in halves:
                    column = halves.index((shift_x, shift_y))
                else:
                    column = halves.index((-shift_x, -shift_y))
                result.append((shift_x, shift_y, math.sqrt(radius), column))
    return result


def inside(x_coord, y_coord, shift_x, shift_y, x_total, y_total):
    x_next = x_coord + shift_x
    y_next = y_coord + shift_y
    return (x_next >= 0) & (x_next < x_total) & (y_next >= 0) & (y_next < y_total)


def weight_sum(x_coord, y_coord, x_total, y_total):
    total = jnp.zeros((x_coord.shape[0], y_coord.shape[1]), jnp.float32)
    for shift_x, shift_y, length, column in bond_list():
        total = total + jnp.where(
            inside(x_coord, y_coord, shift_x, shift_y, x_total, y_total), length, 0.0
        )
    return total


def stretch(anchor, neighbour, shift_x, shift_y, length):
    gap = neighbour - anchor
    sep_x = shift_x + gap[0]
    sep_y = shift_y + gap[1]
    sep_z = gap[2]
    span = jnp.sqrt(sep_x * sep_x + sep_y * sep_y + sep_z * sep_z)
    return (sep_x, sep_y, sep_z, span, span - length)


def bond_terms(theta_here, mass_here, theta_there, mass_there, shear, extension, length):
    first_side = 3.0 * bulk_modulus * theta_here / mass_here + 15.0 * shear * (
        extension - theta_here * length / 3.0
    ) / (mass_here * length)
    second_side = 3.0 * bulk_modulus * theta_there / mass_there + 15.0 * shear * (
        extension - theta_there * length / 3.0
    ) / (mass_there * length)
    return first_side + second_side


def local(displacement, angle_index, bond_table, interface_stiffness):
    comp_count, ply_count, col_count, row_count = displacement.shape
    x_total = col_count * lax.axis_size("tile")
    x_first = lax.axis_index("tile") * col_count
    bond_set = bond_list()
    y_grid = jnp.arange(row_count, dtype=jnp.int32)[None, :]
    y_wide = jnp.arange(-3, row_count + 3, dtype=jnp.int32)[None, :]
    padded = padded_2(displacement, (("tile", 2),), 3)
    margin = 0
    padded = jnp.pad(padded, ((0, 0), (0, 0), (0, 0), (3, 3)))
    border = margin + 3
    span_count = col_count + 2 * margin
    x_region = x_first - margin + jnp.arange(span_count, dtype=jnp.int32)[:, None]
    mass_region = weight_sum(x_region, y_grid, x_total, row_count)
    mass_region = jnp.where(mass_region > 0, mass_region, 1.0)
    anchor = padded[:, :, 3 : 3 + span_count, 3 : 3 + row_count]
    dilation = jnp.zeros((ply_count, span_count, row_count), jnp.float32)
    for shift_x, shift_y, length, column in bond_set:
        neighbour = padded[
            :, :, 3 + shift_x : 3 + shift_x + span_count, 3 + shift_y : 3 + shift_y + row_count
        ]
        stretched = stretch(anchor, neighbour, shift_x, shift_y, length)
        dilation = dilation + jnp.where(
            inside(x_region, y_grid, shift_x, shift_y, x_total, row_count), stretched[4], 0.0
        )
    dilation = 3.0 * dilation / mass_region
    theta_wide = padded_2(dilation, (("tile", 1),), 3)
    theta_wide = jnp.pad(theta_wide, ((0, 0), (0, 0), (3, 3)))
    x_wide = x_first - 3 + jnp.arange(col_count + 6, dtype=jnp.int32)[:, None]
    mass_wide = weight_sum(x_wide, y_wide, x_total, row_count)
    mass_wide = jnp.where(mass_wide > 0, mass_wide, 1.0)
    mass_here = mass_wide[3 : 3 + col_count, 3 : 3 + row_count]
    theta_here = theta_wide[:, 3 : 3 + col_count, 3 : 3 + row_count]
    x_core = x_first + jnp.arange(col_count, dtype=jnp.int32)[:, None]
    selector = (
        angle_index[:, None] == jnp.arange(bond_table.shape[0], dtype=jnp.int32)[None, :]
    ).astype(jnp.float32)
    shear_table = jnp.dot(selector, bond_table, precision=lax.Precision.HIGHEST)
    core = padded[:, :, border : border + col_count, 3 : 3 + row_count]
    force_x = jnp.zeros((ply_count, col_count, row_count), jnp.float32)
    force_y = jnp.zeros((ply_count, col_count, row_count), jnp.float32)
    force_z = jnp.zeros((ply_count, col_count, row_count), jnp.float32)
    for shift_x, shift_y, length, column in bond_set:
        neighbour = padded[
            :,
            :,
            border + shift_x : border + shift_x + col_count,
            3 + shift_y : 3 + shift_y + row_count,
        ]
        sep_x, sep_y, sep_z, span, extension = stretch(core, neighbour, shift_x, shift_y, length)
        theta_there = theta_wide[
            :, 3 + shift_x : 3 + shift_x + col_count, 3 + shift_y : 3 + shift_y + row_count
        ]
        mass_there = mass_wide[
            3 + shift_x : 3 + shift_x + col_count, 3 + shift_y : 3 + shift_y + row_count
        ]
        shear = shear_table[:, column][:, None, None]
        scalar = bond_terms(
            theta_here, mass_here, theta_there, mass_there, shear, extension, length
        )
        scalar = jnp.where(
            inside(x_core, y_grid, shift_x, shift_y, x_total, row_count), scalar / span, 0.0
        )
        force_x = force_x + scalar * sep_x
        force_y = force_y + scalar * sep_y
        force_z = force_z + scalar * sep_z
    zero_end = jnp.zeros((1,), jnp.float32)
    coupling = jnp.concatenate([zero_end, interface_stiffness, zero_end])
    local_coupling = lax.dynamic_slice_in_dim(
        coupling, lax.axis_index("ply") * ply_count, ply_count + 1
    )
    above = local_coupling[1:][None, :, None, None]
    below = local_coupling[:-1][None, :, None, None]
    stacked = padded_2(displacement, (("ply", 1),), 1)
    upper = stacked[:, 2:]
    lower = stacked[:, :-2]
    layered = above * (upper - displacement) + below * (lower - displacement)
    return jnp.stack([force_x, force_y, force_z]) + layered


def solution(mesh):
    placed = (P(None, "ply", "tile", None), P("ply"), P(), P())
    return jax.shard_map(
        local, mesh=mesh, in_specs=placed, out_specs=P(None, "ply", "tile", None), check_vma=False
    )
```

profile of v0, /device:TPU:0, one launch (start us, length us, event | category | flops | bytes accessed | tf_op | source)
XLA Modules:
  0.0 61.0 jit_solution(5106284071565291015)
XLA Ops:
  0.0 0.0 copy-start
  0.0 1.4 %fusion.116 = (f32[3,6,3,1024]{3,2,1,0:T(4,128)S(1)}, f32[3,6,3,1024]{3,2,1,0:T(4,128)S(1)}) fusion(f32[3,6,8,1024]{3,2,1,0:T(8,128)} %param.4), kind=kLoop, calls=%fused_computation.445 | loop fusion | bytes 884736 | tf_op jit(solution)/shard_map/slice | solution.py:16
  1.4 4.9 %collective-permute-start = (f32[3,6,3,1024]{3,2,1,0:T(4,128)S(1)}, f32[3,6,3,1024]{3,2,1,0:T(4,128)S(1)}, u32[]{:S(2)}, u32[]{:S(2)}) collective-permute-start(f32[3,6,3,1024]{3,2,1,0:T(4,128)S(1)} %get-tuple-element.84), channel_id=1, source_target_pairs={{0,1},{1,2},{2,3},{3,4},{4,5},{5,6},{6,7},{8,9},{9,10},{10,11},{11... | collective-permute-start | bytes 663560 | tf_op jit(solution)/shard_map/ppermute | solution.py:18
  6.3 1.3 %collective-permute-start.1 = (f32[3,6,3,1024]{3,2,1,0:T(4,128)S(1)}, f32[3,6,3,1024]{3,2,1,0:T(4,128)S(1)}, u32[]{:S(2)}, u32[]{:S(2)}) collective-permute-start(f32[3,6,3,1024]{3,2,1,0:T(4,128)S(1)} %get-tuple-element.85), channel_id=1, source_target_pairs={{1,0},{2,1},{3,2},{4,3},{5,4},{6,5},{7,6},{9,8},{10,9},{11,10},{12... | collective-permute-start | bytes 663560 | tf_op jit(solution)/shard_map/ppermute | solution.py:19
  7.6 1.6 %fusion.117 = (f32[3,1,8,1024]{3,2,1,0:T(8,128)}, f32[3,1,8,1024]{3,2,1,0:T(8,128)}) fusion(f32[3,6,8,1024]{3,2,1,0:T(8,128)} %param.4), kind=kLoop, calls=%fused_computation.446 | loop fusion | bytes 393216 | tf_op jit(solution)/shard_map/slice | solution.py:17
  9.2 1.3 %collective-permute-start.4 = (f32[3,1,8,1024]{3,2,1,0:T(8,128)}, f32[3,1,8,1024]{3,2,1,0:T(8,128)}, u32[]{:S(2)}, u32[]{:S(2)}) collective-permute-start(f32[3,1,8,1024]{3,2,1,0:T(8,128)} %get-tuple-element.86), channel_id=1, source_target_pairs={{8,0},{16,8},{24,16},{9,1},{17,9},{25,17},{10,2},{18,10},{26,18},{... | collective-permute-start | bytes 294920 | tf_op jit(solution)/shard_map/ppermute | solution.py:19
  10.5 3.7 %collective-permute-start.5 = (f32[3,1,8,1024]{3,2,1,0:T(8,128)}, f32[3,1,8,1024]{3,2,1,0:T(8,128)}, u32[]{:S(2)}, u32[]{:S(2)}) collective-permute-start(f32[3,1,8,1024]{3,2,1,0:T(8,128)} %get-tuple-element.87), channel_id=1, source_target_pairs={{0,8},{8,16},{16,24},{1,9},{9,17},{17,25},{2,10},{10,18},{18,26},{... | collective-permute-start | bytes 294920 | tf_op jit(solution)/shard_map/ppermute | solution.py:18
  14.3 0.9 %broadcast_and_fusion.5 = (pred[8,1024]{1,0:T(8,128)(4,1)S(1)}, pred[8,1024]{1,0:T(8,128)(4,1)}, pred[8,1024]{1,0:T(8,128)(4,1)}, pred[8,1024]{1,0:T(8,128)(4,1)...) fusion(pred[1024]{0:T(1024)(128)(4,1)S(1)} %iota_compare_fusion, ...), kind=kLoop, calls=%fused_computation.370 | loop fusion | flops 393216 | bytes 232504 | tf_op jit(solution)/shard_map/and | solution.py:47
  15.2 0.2 compare_select_fusion.1
  15.5 0.7 %and_and_fusion.8 = pred[8,1024]{1,0:T(8,128)(4,1)} fusion(pred[1024]{0:T(1024)(128)(4,1)S(1)} %get-tuple-element.232, pred[1024]{0:T(1024)(128)(4,1)S(1)} %get-tuple-element.233, pred[8]{0:T(512)(128)(4,1)S(1)} %get-tuple-element.229), kind=kLoop, calls=%fused_computation.322 | loop fusion | flops 16384 | bytes 10248 | tf_op jit(solution)/shard_map/and | solution.py:47
  16.3 0.4 compare_select_fusion
  16.7 0.2 fusion.119
  16.9 0.0 copy-start.44
  16.9 0.0 copy-start.45
  16.9 0.0 copy-start.1
  16.9 0.9 %broadcast_multiply_fusion.26 = (f32[8,1024]{1,0:T(8,128)S(1)}, f32[8,1024]{1,0:T(8,128)S(1)}, f32[8,1024]{1,0:T(8,128)S(1)}, f32[8,1024]{1,0:T(8,128)S(1)}, f32...) fusion(f32[14,1030]{1,0:T(8,128)S(1)} %compare_select_fusion), kind=kLoop, calls=%fused_computation.362 | loop fusion | flops 90112 | bytes 1015808 | tf_op jit(solution)/shard_map/mul | solution.py:74
  17.9 1.1 %fusion.120 = (f32[8,1024]{1,0:T(8,128)}, f32[8,1024]{1,0:T(8,128)}, f32[8,1024]{1,0:T(8,128)}, f32[8,1024]{1,0:T(8,128)}, f32[8,1024]{1,0:T(8,128)}, /*index=5*...) fusion(f32[14,1030]{1,0:T(8,128)S(1)} %compare_select_fusion), kind=kLoop, calls=%fused_computation.449 | loop fusion | bytes 1245184 | tf_op jit(solution)/shard_map/slice | solution.py:131
  19.0 0.7 %slice.1042 = f32[8,1024]{1,0:T(8,128)} slice(f32[14,1030]{1,0:T(8,128)S(1)} %compare_select_fusion), slice={[3:11], [3:1027]} | slice | bytes 65536 | tf_op jit(solution)/shard_map/slice | solution.py:109
  19.6 0.0 copy-done
  19.6 0.0 copy-done.44
  19.7 0.2 fusion.114
  19.8 0.0 copy-done.45
  19.8 0.1 pad_maximum_fusion.5
  19.9 0.1 dynamic_slice.3
  20.0 0.7 %fusion.121 = (f32[6]{0:T(128)}, f32[6]{0:T(128)}) fusion(f32[7]{0:T(128)S(1)} %dynamic_slice.3), kind=kLoop, calls=%fused_computation.450 | loop fusion | bytes 96 | tf_op jit(solution)/shard_map/slice | solution.py:149
  20.7 0.0 collective-permute-done
  20.7 0.0 collective-permute-done.1
  20.7 0.0 copy-done.1
  20.7 0.8 %select_maximum_fusion = f32[3,6,14,1030]{3,2,1,0:T(8,128)S(1)} fusion(f32[3,6,3,1024]{3,2,1,0:T(4,128)S(1)} %collective-permute-done.1, f32[3,6,8,1024]{3,2,1,0:T(8,128)S(1)} %copy-done.1, f32[3,6,3,1024]{3,2,1,0:T(4,128)S(1)} %collective-permute-done), kind=kLoop, calls=%fused_computation.6 | loop fusion | flops 2076480 | bytes 2070432 | tf_op jit(solution)/shard_map/concatenate | solution.py:20
  21.4 2.8 %slice_subtract_fusion.1 = (f32[3,6,8,1024]{3,2,1,0:T(8,128)S(1)}, f32[3,6,8,1024]{3,2,1,0:T(8,128)S(1)}, f32[3,6,8,1024]{3,2,1,0:T(8,128)S(1)}, f32[3,6,8,1024]...) fusion(f32[3,6,8,1024]{3,2,1,0:T(8,128)S(1)} %copy-done.1, ...), kind=kLoop, calls=%fused_computation.24 | loop fusion | flops 2654207 | bytes 22413312 | tf_op jit(solution)/shard_map/sub | solution.py:60
  24.2 0.1 constant_dynamic-update-slice_fusion
  24.4 0.0 copy-start.34
  24.4 0.8 %slice_subtract_fusion = (f32[3,6,8,1024]{3,2,1,0:T(8,128)S(1)}, f32[3,6,8,1024]{3,2,1,0:T(8,128)S(1)}, f32[3,6,8,1024]{3,2,1,0:T(8,128)S(1)}, f32[3,6,8,1024]{3...) fusion(f32[3,6,8,1024]{3,2,1,0:T(8,128)S(1)} %copy-done.1, ...), kind=kLoop, calls=%fused_computation.23 | loop fusion | flops 1916928 | bytes 10838016 | tf_op jit(solution)/shard_map/sub | solution.py:60
  25.2 0.0 copy-done.34
  25.2 4.2 %fusion.63 = f32[6,8,1024]{2,1,0:T(8,128)S(1)} fusion(f32[8,1024]{1,0:T(8,128)S(1)} %compare_select_fusion.1, pred[8,1024]{1,0:T(8,128)(4,1)} %get-tuple-element.222, pred[8,1024]{1,0:T(8,128)(4,1)} %get-tuple-element.200, pred[8,1024]{1,0:T(8,128)(4,1)} %get-tuple-element.215, pred[8,1024]{1,0:T(8,128)(4,1)} %get-tuple-element.221, ...), kind=kLoop, calls=%fused_computation.203 | loop fusion | flops 13221888 | bytes 16973824 | tf_op jit(solution)/shard_map/div | solution.py:103
  29.4 0.0 copy-start.2
  29.5 0.0 copy-start.3
  29.5 0.0 copy-start.4
  29.5 0.0 copy-start.5
  29.5 0.0 copy-start.6
  29.5 0.0 copy-start.7
  29.5 0.0 copy-start.8
  29.5 0.0 copy-start.9
  29.5 0.0 copy-start.10
  29.5 0.0 copy-start.11
  29.5 0.0 copy-start.12
  29.6 0.0 copy-start.13
  29.6 0.0 copy-start.14
  29.6 0.0 copy-start.15
  29.6 0.0 copy-start.16
  29.9 4.7 %collective-permute-start.2 = (f32[6,3,1024]{2,1,0:T(4,128)S(1)}, f32[6,3,1024]{2,1,0:T(4,128)S(1)}, u32[]{:S(2)}, u32[]{:S(2)}) collective-permute-start(f32[6,3,1024]{2,1,0:T(4,128)S(1)} %get-tuple-element.89), channel_id=1, source_target_pairs={{0,1},{1,2},{2,3},{3,4},{4,5},{5,6},{6,7},{8,9},{9,10},{10,11},{11... | collective-permute-start | bytes 221192 | tf_op jit(solution)/shard_map/ppermute | solution.py:18
  34.6 1.3 %collective-permute-start.3 = (f32[6,3,1024]{2,1,0:T(4,128)S(1)}, f32[6,3,1024]{2,1,0:T(4,128)S(1)}, u32[]{:S(2)}, u32[]{:S(2)}) collective-permute-start(f32[6,3,1024]{2,1,0:T(4,128)S(1)} %get-tuple-element.88), channel_id=1, source_target_pairs={{1,0},{2,1},{3,2},{4,3},{5,4},{6,5},{7,6},{9,8},{10,9},{11,10},{12... | collective-permute-start | bytes 221192 | tf_op jit(solution)/shard_map/ppermute | solution.py:19
  35.9 0.4 multiply_reduce_fusion
  36.3 1.0 %collective-permute-done.2 = f32[6,3,1024]{2,1,0:T(4,128)S(1)} collective-permute-done((f32[6,3,1024]{2,1,0:T(4,128)S(1)}, f32[6,3,1024]{2,1,0:T(4,128)S(1)}, u32[]{:S(2)}, u32[]{:S(2)}) %collective-permute-start.2) | collective-permute-done | bytes 73760 | tf_op jit(solution)/shard_map/ppermute | solution.py:18
  37.3 4.8 %collective-permute-done.3 = f32[6,3,1024]{2,1,0:T(4,128)S(1)} collective-permute-done((f32[6,3,1024]{2,1,0:T(4,128)S(1)}, f32[6,3,1024]{2,1,0:T(4,128)S(1)}, u32[]{:S(2)}, u32[]{:S(2)}) %collective-permute-start.3) | collective-permute-done | bytes 73760 | tf_op jit(solution)/shard_map/ppermute | solution.py:19
  42.0 0.3 select_maximum_fusion.2
  42.7 13.6 %add_bitcast_fusion.2 = (f32[1,6,8,1024]{3,2,1,0:T(8,128)S(1)}, f32[6,8,1024]{2,1,0:T(8,128)S(1)}, f32[6,8,1024]{2,1,0:T(8,128)S(1)}, f32[6,8,1024]{2,1,0:T(8,12...) fusion(f32[3,6,8,1024]{3,2,1,0:T(8,128)S(1)} %get-tuple-element, ...), kind=kLoop, calls=%fused_computation.198 | loop fusion | flops 32833536 | bytes 29016400 | tf_op jit(solution)/shard_map/stack | solution.py:155
  56.4 1.3 %add_bitcast_fusion.1 = f32[1,6,8,1024]{3,2,1,0:T(8,128)S(1)} fusion(f32[6,8,1024]{2,1,0:T(8,128)S(1)} %get-tuple-element.47, f32[6,8,1024]{2,1,0:T(8,128)S(1)} %get-tuple-element.46, f32[6,8,1024]{2,1,0:T(8,128)S(1)} %get-tuple-element.45, f32[6,8,1024]{2,1,0:T(8,128)S(1)} %get-tuple-element.44, f32[6,8,1024]{2,1,0:T(8,128)S(1)} %get-tuple-element.43, ...), kind=kLoop, calls=%fused_computation.197 | loop fusion | flops 3784704 | bytes 11206656 | tf_op jit(solution)/shard_map/stack | solution.py:155
  57.7 0.0 copy-start.42
  57.7 0.0 copy-start.43
  57.7 1.3 %add_bitcast_fusion = f32[1,6,8,1024]{3,2,1,0:T(8,128)S(1)} fusion(f32[6,8,1024]{2,1,0:T(8,128)S(1)} %get-tuple-element.47, f32[6,8,1024]{2,1,0:T(8,128)S(1)} %get-tuple-element.46, f32[6,8,1024]{2,1,0:T(8,128)S(1)} %get-tuple-element.45, f32[6,8,1024]{2,1,0:T(8,128)S(1)} %get-tuple-element.44, f32[6,8,1024]{2,1,0:T(8,128)S(1)} %get-tuple-element.43, ...), kind=kLoop, calls=%fused_computation.196 | loop fusion | flops 2703360 | bytes 11206656 | tf_op jit(solution)/shard_map/stack | solution.py:155
  59.0 0.0 collective-permute-done.4
  59.0 0.0 collective-permute-done.5
  59.0 1.9 %fusion.8 = f32[3,6,8,1024]{3,2,1,0:T(8,128)} fusion(f32[3,6,8,1024]{3,2,1,0:T(8,128)S(1)} %copy-done.1, f32[3,1,8,1024]{3,2,1,0:T(8,128)} %collective-permute-done.5, f32[3,1,8,1024]{3,2,1,0:T(8,128)} %collective-permute-done.4, f32[1,6,8,1024]{3,2,1,0:T(8,128)S(1)} %add_bitcast_fusion, f32[1,6,8,1024]{3,2,1,0:T(8,128)S(1)} %add_bitcast_fusion.1, ...), kind=kLoop, calls=%fused_computation.19 | loop fusion | flops 1474560 | bytes 1966128 | tf_op jit(solution)/shard_map/add | solution.py:155
  (88 shorter events, 0.3 us)
Async XLA Ops:
  0.0 19.6 %copy-start = (f32[4,14]{1,0:T(4,128)S(1)}, f32[4,14]{1,0:T(4,128)}, u32[]{:S(2)}) copy-start(f32[4,14]{1,0:T(4,128)} %param.6) | copy-start | bytes 676
  1.4 19.3 %collective-permute-start = (f32[3,6,3,1024]{3,2,1,0:T(4,128)S(1)}, f32[3,6,3,1024]{3,2,1,0:T(4,128)S(1)}, u32[]{:S(2)}, u32[]{:S(2)}) collective-permute-start(f32[3,6,3,1024]{3,2,1,0:T(4,128)S(1)} %get-tuple-element.84), channel_id=1, source_target_pairs={{0,1},{1,2},{2,3},{3,4},{4,5},{5,6},{6,7},{8,9},{9,10},{10,11},{11... | collective-permute-start | bytes 663560 | tf_op jit(solution)/shard_map/ppermute | solution.py:18
  6.3 14.4 %collective-permute-start.1 = (f32[3,6,3,1024]{3,2,1,0:T(4,128)S(1)}, f32[3,6,3,1024]{3,2,1,0:T(4,128)S(1)}, u32[]{:S(2)}, u32[]{:S(2)}) collective-permute-start(f32[3,6,3,1024]{3,2,1,0:T(4,128)S(1)} %get-tuple-element.85), channel_id=1, source_target_pairs={{1,0},{2,1},{3,2},{4,3},{5,4},{6,5},{7,6},{9,8},{10,9},{11,10},{12... | collective-permute-start | bytes 663560 | tf_op jit(solution)/shard_map/ppermute | solution.py:19
  9.2 49.8 %collective-permute-start.4 = (f32[3,1,8,1024]{3,2,1,0:T(8,128)}, f32[3,1,8,1024]{3,2,1,0:T(8,128)}, u32[]{:S(2)}, u32[]{:S(2)}) collective-permute-start(f32[3,1,8,1024]{3,2,1,0:T(8,128)} %get-tuple-element.86), channel_id=1, source_target_pairs={{8,0},{16,8},{24,16},{9,1},{17,9},{25,17},{10,2},{18,10},{26,18},{... | collective-permute-start | bytes 294920 | tf_op jit(solution)/shard_map/ppermute | solution.py:19
  10.5 48.5 %collective-permute-start.5 = (f32[3,1,8,1024]{3,2,1,0:T(8,128)}, f32[3,1,8,1024]{3,2,1,0:T(8,128)}, u32[]{:S(2)}, u32[]{:S(2)}) collective-permute-start(f32[3,1,8,1024]{3,2,1,0:T(8,128)} %get-tuple-element.87), channel_id=1, source_target_pairs={{0,8},{8,16},{16,24},{1,9},{9,17},{17,25},{2,10},{10,18},{18,26},{... | collective-permute-start | bytes 294920 | tf_op jit(solution)/shard_map/ppermute | solution.py:18
  16.9 2.7 %copy-start.44 = (s32[6]{0:T(128)S(1)}, s32[6]{0:T(128)}, u32[]{:S(2)}) copy-start(s32[6]{0:T(128)} %param.5) | copy-start | bytes 76
  16.9 2.9 %copy-start.45 = (f32[23]{0:T(128)S(1)}, f32[23]{0:T(128)}, u32[]{:S(2)}) copy-start(f32[23]{0:T(128)} %param.7) | copy-start | bytes 280
  16.9 3.7 %copy-start.1 = (f32[3,6,8,1024]{3,2,1,0:T(8,128)S(1)}, f32[3,6,8,1024]{3,2,1,0:T(8,128)}, u32[]{:S(2)}) copy-start(f32[3,6,8,1024]{3,2,1,0:T(8,128)} %param.4) | copy-start | bytes 1769476
  24.4 0.9 %copy-start.34 = (pred[8,1024]{1,0:T(8,128)(4,1)S(1)}, pred[8,1024]{1,0:T(8,128)(4,1)}, u32[]{:S(2)}) copy-start(pred[8,1024]{1,0:T(8,128)(4,1)} %get-tuple-element.198) | copy-start | bytes 24580
  29.4 12.9 %copy-start.2 = (f32[8,1024]{1,0:T(8,128)S(1)}, f32[8,1024]{1,0:T(8,128)}, u32[]{:S(2)}) copy-start(f32[8,1024]{1,0:T(8,128)} %get-tuple-element.116) | copy-start | bytes 98308
  29.5 12.9 %copy-start.3 = (f32[8,1024]{1,0:T(8,128)S(1)}, f32[8,1024]{1,0:T(8,128)}, u32[]{:S(2)}) copy-start(f32[8,1024]{1,0:T(8,128)} %get-tuple-element.117) | copy-start | bytes 98308
  29.5 12.9 %copy-start.4 = (f32[8,1024]{1,0:T(8,128)S(1)}, f32[8,1024]{1,0:T(8,128)}, u32[]{:S(2)}) copy-start(f32[8,1024]{1,0:T(8,128)} %get-tuple-element.118) | copy-start | bytes 98308
  29.5 12.9 %copy-start.5 = (f32[8,1024]{1,0:T(8,128)S(1)}, f32[8,1024]{1,0:T(8,128)}, u32[]{:S(2)}) copy-start(f32[8,1024]{1,0:T(8,128)} %get-tuple-element.119) | copy-start | bytes 98308
  29.5 12.9 %copy-start.6 = (f32[8,1024]{1,0:T(8,128)S(1)}, f32[8,1024]{1,0:T(8,128)}, u32[]{:S(2)}) copy-start(f32[8,1024]{1,0:T(8,128)} %get-tuple-element.120) | copy-start | bytes 98308
  29.5 12.9 %copy-start.7 = (f32[8,1024]{1,0:T(8,128)S(1)}, f32[8,1024]{1,0:T(8,128)}, u32[]{:S(2)}) copy-start(f32[8,1024]{1,0:T(8,128)} %get-tuple-element.121) | copy-start | bytes 98308
  29.5 12.9 %copy-start.8 = (f32[8,1024]{1,0:T(8,128)S(1)}, f32[8,1024]{1,0:T(8,128)}, u32[]{:S(2)}) copy-start(f32[8,1024]{1,0:T(8,128)} %get-tuple-element.122) | copy-start | bytes 98308
  29.5 12.9 %copy-start.9 = (f32[8,1024]{1,0:T(8,128)S(1)}, f32[8,1024]{1,0:T(8,128)}, u32[]{:S(2)}) copy-start(f32[8,1024]{1,0:T(8,128)} %get-tuple-element.123) | copy-start | bytes 98308
  29.5 12.9 %copy-start.10 = (f32[8,1024]{1,0:T(8,128)S(1)}, f32[8,1024]{1,0:T(8,128)}, u32[]{:S(2)}) copy-start(f32[8,1024]{1,0:T(8,128)} %get-tuple-element.124) | copy-start | bytes 98308
  29.5 12.9 %copy-start.11 = (f32[8,1024]{1,0:T(8,128)S(1)}, f32[8,1024]{1,0:T(8,128)}, u32[]{:S(2)}) copy-start(f32[8,1024]{1,0:T(8,128)} %get-tuple-element.125) | copy-start | bytes 98308
  29.5 12.9 %copy-start.12 = (f32[8,1024]{1,0:T(8,128)S(1)}, f32[8,1024]{1,0:T(8,128)}, u32[]{:S(2)}) copy-start(f32[8,1024]{1,0:T(8,128)} %get-tuple-element.126) | copy-start | bytes 98308
  29.6 12.9 %copy-start.13 = (f32[8,1024]{1,0:T(8,128)S(1)}, f32[8,1024]{1,0:T(8,128)}, u32[]{:S(2)}) copy-start(f32[8,1024]{1,0:T(8,128)} %get-tuple-element.127) | copy-start | bytes 98308
  29.6 12.9 %copy-start.14 = (f32[8,1024]{1,0:T(8,128)S(1)}, f32[8,1024]{1,0:T(8,128)}, u32[]{:S(2)}) copy-start(f32[8,1024]{1,0:T(8,128)} %get-tuple-element.128) | copy-start | bytes 98308
  29.6 12.9 %copy-start.15 = (f32[8,1024]{1,0:T(8,128)S(1)}, f32[8,1024]{1,0:T(8,128)}, u32[]{:S(2)}) copy-start(f32[8,1024]{1,0:T(8,128)} %get-tuple-element.129) | copy-start | bytes 98308
  29.6 12.9 %copy-start.16 = (f32[8,1024]{1,0:T(8,128)S(1)}, f32[8,1024]{1,0:T(8,128)}, u32[]{:S(2)}) copy-start(f32[8,1024]{1,0:T(8,128)} %get-tuple-element.130) | copy-start | bytes 98308
  29.6 12.9 %copy-start.17 = (f32[8,1024]{1,0:T(8,128)S(1)}, f32[8,1024]{1,0:T(8,128)}, u32[]{:S(2)}) copy-start(f32[8,1024]{1,0:T(8,128)} %get-tuple-element.131) | copy-start | bytes 98308
  29.6 12.9 %copy-start.18 = (f32[8,1024]{1,0:T(8,128)S(1)}, f32[8,1024]{1,0:T(8,128)}, u32[]{:S(2)}) copy-start(f32[8,1024]{1,0:T(8,128)} %get-tuple-element.132) | copy-start | bytes 98308
  29.6 12.9 %copy-start.19 = (f32[8,1024]{1,0:T(8,128)S(1)}, f32[8,1024]{1,0:T(8,128)}, u32[]{:S(2)}) copy-start(f32[8,1024]{1,0:T(8,128)} %get-tuple-element.133) | copy-start | bytes 98308
  29.6 12.9 %copy-start.20 = (f32[8,1024]{1,0:T(8,128)S(1)}, f32[8,1024]{1,0:T(8,128)}, u32[]{:S(2)}) copy-start(f32[8,1024]{1,0:T(8,128)} %get-tuple-element.134) | copy-start | bytes 98308
  29.6 12.9 %copy-start.21 = (f32[8,1024]{1,0:T(8,128)S(1)}, f32[8,1024]{1,0:T(8,128)}, u32[]{:S(2)}) copy-start(f32[8,1024]{1,0:T(8,128)} %get-tuple-element.135) | copy-start | bytes 98308
  29.6 12.9 %copy-start.22 = (f32[8,1024]{1,0:T(8,128)S(1)}, f32[8,1024]{1,0:T(8,128)}, u32[]{:S(2)}) copy-start(f32[8,1024]{1,0:T(8,128)} %get-tuple-element.136) | copy-start | bytes 98308
  29.7 12.9 %copy-start.23 = (f32[8,1024]{1,0:T(8,128)S(1)}, f32[8,1024]{1,0:T(8,128)}, u32[]{:S(2)}) copy-start(f32[8,1024]{1,0:T(8,128)} %get-tuple-element.137) | copy-start | bytes 98308
  29.7 12.9 %copy-start.24 = (f32[8,1024]{1,0:T(8,128)S(1)}, f32[8,1024]{1,0:T(8,128)}, u32[]{:S(2)}) copy-start(f32[8,1024]{1,0:T(8,128)} %get-tuple-element.138) | copy-start | bytes 98308
  29.7 12.9 %copy-start.25 = (f32[8,1024]{1,0:T(8,128)S(1)}, f32[8,1024]{1,0:T(8,128)}, u32[]{:S(2)}) copy-start(f32[8,1024]{1,0:T(8,128)} %get-tuple-element.139) | copy-start | bytes 98308
  29.7 12.9 %copy-start.26 = (f32[8,1024]{1,0:T(8,128)S(1)}, f32[8,1024]{1,0:T(8,128)}, u32[]{:S(2)}) copy-start(f32[8,1024]{1,0:T(8,128)} %get-tuple-element.140) | copy-start | bytes 98308
  29.7 12.9 %copy-start.27 = (f32[8,1024]{1,0:T(8,128)S(1)}, f32[8,1024]{1,0:T(8,128)}, u32[]{:S(2)}) copy-start(f32[8,1024]{1,0:T(8,128)} %get-tuple-element.141) | copy-start | bytes 98308
  29.7 12.9 %copy-start.28 = (f32[8,1024]{1,0:T(8,128)S(1)}, f32[8,1024]{1,0:T(8,128)}, u32[]{:S(2)}) copy-start(f32[8,1024]{1,0:T(8,128)} %get-tuple-element.142) | copy-start | bytes 98308
  29.7 12.9 %copy-start.29 = (f32[8,1024]{1,0:T(8,128)S(1)}, f32[8,1024]{1,0:T(8,128)}, u32[]{:S(2)}) copy-start(f32[8,1024]{1,0:T(8,128)} %get-tuple-element.143) | copy-start | bytes 98308
  29.7 12.9 %copy-start.30 = (f32[8,1024]{1,0:T(8,128)S(1)}, f32[8,1024]{1,0:T(8,128)}, u32[]{:S(2)}) copy-start(f32[8,1024]{1,0:T(8,128)} %get-tuple-element.144) | copy-start | bytes 98308
  29.7 12.9 %copy-start.31 = (f32[8,1024]{1,0:T(8,128)S(1)}, f32[8,1024]{1,0:T(8,128)}, u32[]{:S(2)}) copy-start(f32[8,1024]{1,0:T(8,128)} %get-tuple-element.145) | copy-start | bytes 98308
  29.7 12.9 %copy-start.32 = (f32[8,1024]{1,0:T(8,128)S(1)}, f32[8,1024]{1,0:T(8,128)}, u32[]{:S(2)}) copy-start(f32[8,1024]{1,0:T(8,128)} %get-tuple-element.146) | copy-start | bytes 98308
  29.8 12.9 %copy-start.33 = (f32[8,1024]{1,0:T(8,128)S(1)}, f32[8,1024]{1,0:T(8,128)}, u32[]{:S(2)}) copy-start(f32[8,1024]{1,0:T(8,128)} %slice.1042) | copy-start | bytes 98308
  29.8 12.9 %copy-start.35 = (pred[8,1024]{1,0:T(8,128)(4,1)S(1)}, pred[8,1024]{1,0:T(8,128)(4,1)}, u32[]{:S(2)}) copy-start(pred[8,1024]{1,0:T(8,128)(4,1)} %get-tuple-element.199) | copy-start | bytes 24580
  29.8 12.9 %copy-start.36 = (pred[8,1024]{1,0:T(8,128)(4,1)S(1)}, pred[8,1024]{1,0:T(8,128)(4,1)}, u32[]{:S(2)}) copy-start(pred[8,1024]{1,0:T(8,128)(4,1)} %get-tuple-element.200) | copy-start | bytes 24580
  29.8 12.9 %copy-start.37 = (pred[8,1024]{1,0:T(8,128)(4,1)S(1)}, pred[8,1024]{1,0:T(8,128)(4,1)}, u32[]{:S(2)}) copy-start(pred[8,1024]{1,0:T(8,128)(4,1)} %get-tuple-element.201) | copy-start | bytes 24580
  29.8 12.9 %copy-start.38 = (pred[8,1024]{1,0:T(8,128)(4,1)S(1)}, pred[8,1024]{1,0:T(8,128)(4,1)}, u32[]{:S(2)}) copy-start(pred[8,1024]{1,0:T(8,128)(4,1)} %get-tuple-element.202) | copy-start | bytes 24580
  29.8 12.9 %copy-start.39 = (pred[8,1024]{1,0:T(8,128)(4,1)S(1)}, pred[8,1024]{1,0:T(8,128)(4,1)}, u32[]{:S(2)}) copy-start(pred[8,1024]{1,0:T(8,128)(4,1)} %get-tuple-element.203) | copy-start | bytes 24580
  29.8 12.9 %copy-start.40 = (pred[8,1024]{1,0:T(8,128)(4,1)S(1)}, pred[8,1024]{1,0:T(8,128)(4,1)}, u32[]{:S(2)}) copy-start(pred[8,1024]{1,0:T(8,128)(4,1)} %get-tuple-element.204) | copy-start | bytes 24580
  29.8 12.9 %copy-start.41 = (pred[8,1024]{1,0:T(8,128)(4,1)S(1)}, pred[8,1024]{1,0:T(8,128)(4,1)}, u32[]{:S(2)}) copy-start(pred[8,1024]{1,0:T(8,128)(4,1)} %get-tuple-element.205) | copy-start | bytes 24580
  29.9 7.4 %collective-permute-start.2 = (f32[6,3,1024]{2,1,0:T(4,128)S(1)}, f32[6,3,1024]{2,1,0:T(4,128)S(1)}, u32[]{:S(2)}, u32[]{:S(2)}) collective-permute-start(f32[6,3,1024]{2,1,0:T(4,128)S(1)} %get-tuple-element.89), channel_id=1, source_target_pairs={{0,1},{1,2},{2,3},{3,4},{4,5},{5,6},{6,7},{8,9},{9,10},{10,11},{11... | collective-permute-start | bytes 221192 | tf_op jit(solution)/shard_map/ppermute | solution.py:18
  34.6 7.5 %collective-permute-start.3 = (f32[6,3,1024]{2,1,0:T(4,128)S(1)}, f32[6,3,1024]{2,1,0:T(4,128)S(1)}, u32[]{:S(2)}, u32[]{:S(2)}) collective-permute-start(f32[6,3,1024]{2,1,0:T(4,128)S(1)} %get-tuple-element.88), channel_id=1, source_target_pairs={{1,0},{2,1},{3,2},{4,3},{5,4},{6,5},{7,6},{9,8},{10,9},{11,10},{12... | collective-permute-start | bytes 221192 | tf_op jit(solution)/shard_map/ppermute | solution.py:19
  57.7 1.3 %copy-start.42 = (f32[6]{0:T(128)S(1)}, f32[6]{0:T(128)}, u32[]{:S(2)}) copy-start(f32[6]{0:T(128)} %get-tuple-element.224) | copy-start | bytes 76
  57.7 1.3 %copy-start.43 = (f32[6]{0:T(128)S(1)}, f32[6]{0:T(128)}, u32[]{:S(2)}) copy-start(f32[6]{0:T(128)} %get-tuple-element.225) | copy-start | bytes 76
where the time goes:
time: 61.4 us; the launch traced here: 61 us
  other arithmetic  31.1 us (51%)
  starting transfers between devices  17.1 us (28%)
  local copies, waits for them, and re-layouts  5.82 us (9%)
  waiting for transfers between devices  5.79 us (9%)
  between operations  0.97 us (2%)
    another operation x3, other arithmetic, local(): return jnp.stack([force_x, force_y, force_z]) + layered  16.2 us
    ppermute x3, starting transfers between devices, padded_2(): before = lax.ppermute(last, axis, up)  13.2 us
    ppermute x3, waiting for transfers between devices, padded_2(): after = lax.ppermute(first, axis, down)  4.79 us
    div x1, other arithmetic, local(): dilation = 3.0 * dilation / mass_region  4.22 us
    ppermute x3, starting transfers between devices, padded_2(): after = lax.ppermute(first, axis, down)  3.86 us
    sub x2, other arithmetic, stretch(): gap = neighbour - anchor  3.62 us
    add x1, other arithmetic, local(): return jnp.stack([force_x, force_y, force_z]) + layered  1.95 us
    and x10, other arithmetic, inside(): (x_next >= 0) & (x_next < x_total) & (y_next >= 0) & (y_next < y_total)  1.65 us
  transfers between devices with their start and end apart: 6, of which 2 were waited for; matrix products, arithmetic and copies ran while one was open for 55% of the time, Pallas kernels for 0%

commit v1 on v0

v1 whole, which is shorter than its diff:
```python
import math

import jax
import jax.numpy as jnp
from jax import lax
from jax.experimental import pallas as pl
from jax.experimental.pallas import tpu as pltpu
from jax.sharding import PartitionSpec as P

bulk_modulus = 40.0
REACH = 3
LANES = 128
VMEM_LIMIT = 48 * 1024 * 1024


def bond_columns():
    halves = []
    for a in range(-REACH, REACH + 1):
        for b in range(-REACH, REACH + 1):
            if 0 < a * a + b * b <= 9 and (a > 0 or (a == 0 and b > 0)):
                halves.append((a, b))
    columns = {}
    for index, (a, b) in enumerate(halves):
        columns[(a, b)] = index
        columns[(-a, -b)] = index
    return columns


COLUMNS = bond_columns()
BONDS = {0: (1, 2, 3), 1: (-2, -1, 0, 1, 2), 2: (-2, -1, 0, 1, 2), 3: (0,)}


def length_of(a, b):
    return math.sqrt(a * a + b * b)


class Grid:
    def __init__(self, subs):
        self.subs = subs
        self.lane = lax.broadcasted_iota(jnp.int32, (subs, LANES), 1)
        self.sub = lax.broadcasted_iota(jnp.int32, (subs, LANES), 0)
        self.y = self.sub * LANES + self.lane
        self.total = subs * LANES

    def ahead(self, row, shifts):
        after = pltpu.roll(row, self.subs - 1, axis=0)
        return {
            b: pltpu.roll(jnp.where(self.lane < b, after, row), LANES - b, axis=1) for b in shifts
        }

    def back(self, rows):
        total = None
        for b, row in rows.items():
            before = pltpu.roll(row, 1, axis=0)
            moved = pltpu.roll(jnp.where(self.lane >= LANES - b, before, row), b, axis=1)
            total = moved if total is None else total + moved
        return total

    def has_ahead(self, b):
        return self.y < self.total - b

    def ring(self, a):
        total = None
        for b in range(-REACH, REACH + 1):
            if 0 < a * a + b * b <= 9:
                exists = (self.y + b >= 0) & (self.y + b < self.total)
                term = jnp.where(exists, length_of(a, b), 0.0)
                total = term if total is None else total + term
        return total


def row_of(ref, lead, x, cols, subs):
    return ref[(*lead, pl.ds(x, subs, stride=cols), slice(None))]


def separation(here, here_x, there):
    return (there[0] - here_x, there[1] - here[1], there[2] - here[2])


def square(sep):
    return sep[0] * sep[0] + sep[1] * sep[1] + sep[2] * sep[2]


def pack_kernel(tiles, u_ref, a_ref, b_ref):
    comps, plies, depth, _ = u_ref.shape
    subs = a_ref.shape[2]
    cols = depth // subs
    odd = lax.axis_index("tile") % 2 == 1
    for c in range(comps):
        for p in range(plies):
            for j in range(REACH):
                first = row_of(u_ref, (c, p), j, cols, subs)
                last = row_of(u_ref, (c, p), cols - REACH + j, cols, subs)
                at = (c * plies + p) * REACH + j
                a_ref[0, at] = jnp.where(odd, first, last)
                b_ref[0, at] = jnp.where(odd, last, first)


def fill_rows(grid, rows_ref, x, row):
    for c in range(3):
        rows_ref[0, c, x] = row[c]
        for b, moved in grid.ahead(row[c], (1, 2, 3)).items():
            rows_ref[b, c, x] = moved + float(b) if c == 1 else moved


def add_to(ref, at, value):
    ref[at] = ref[at] + value


def inner_kernel(u_ref, t_ref, a_ref, b_ref, rows_ref, sum_ref):
    comps, plies, depth, _ = u_ref.shape
    subs = t_ref.shape[2]
    cols = depth // subs
    grid = Grid(subs)
    odd = lax.axis_index("tile") % 2 == 1

    def ply(p, carry):
        for x in range(cols):
            fill_rows(grid, rows_ref, x, [row_of(u_ref, (c, p), x, cols, subs) for c in range(3)])
        extension_sums(grid, rows_ref, sum_ref, 0, cols, lambda i, j: True, lambda b, i, j: None)
        for x in range(cols):
            t_ref[p, x] = sum_ref[x]
        for j in range(REACH):
            first = sum_ref[j]
            last = sum_ref[cols - REACH + j]
            a_ref[0, p * REACH + j] = jnp.where(odd, first, last)
            b_ref[0, p * REACH + j] = jnp.where(odd, last, first)
        return carry

    lax.fori_loop(0, plies, ply, 0)


def extension_sums(grid, rows_ref, sum_ref, first, last, wanted, side):
    sums = {}
    shifted = {}
    for b, offsets in BONDS.items():
        for i in range(first, last):
            pairs = [(a, i + a) for a in offsets if first <= i + a < last and wanted(i, i + a)]
            if not pairs:
                continue
            here = [rows_ref[0, c, i] for c in range(3)]
            for a, j in pairs:
                there = [rows_ref[b, c, j] for c in range(3)]
                sep = separation(here, here[0] - float(a) if a else here[0], there)
                q = square(sep)
                e = q * lax.rsqrt(q) - length_of(a, b)
                mask = side(b, i, j)
                if mask is not None:
                    e = jnp.where(mask, e, 0.0)
                elif b:
                    e = jnp.where(grid.has_ahead(b), e, 0.0)
                sums[i] = sums[i] + e if i in sums else e
                if b == 0:
                    sums[j] = sums[j] + e if j in sums else e
                else:
                    key = (j, b)
                    shifted[key] = shifted[key] + e if key in shifted else e
    for x in range(first, last):
        rows = {b: shifted[(x, b)] for b in (1, 2, 3) if (x, b) in shifted}
        total = grid.back(rows) if rows else None
        if x in sums:
            total = sums[x] if total is None else total + sums[x]
        if total is not None:
            sum_ref[x] = total


def force_kernel(
    ply_peers, tile_peers, angle_ref, table_ref, stiff_ref, u_ref, ua_ref, ub_ref, t_ref, ta_ref, tb_ref,
    above_ref, below_ref, out_ref, rows_ref, sum_ref, strain_ref, weight_ref, pair_ref, force_ref,
):
    comps, plies, depth, _ = u_ref.shape
    subs = t_ref.shape[2]
    cols = depth // subs
    wide = cols + 2 * REACH
    grid = Grid(subs)
    tile = lax.axis_index("tile")
    slab = lax.axis_index("ply")
    odd = tile % 2 == 1
    has_left = tile > 0
    has_right = tile < tile_peers - 1

    def is_own(x):
        return REACH <= x < REACH + cols

    def crossing(i, j):
        return is_own(i) != is_own(j)

    def needed(i, j):
        return is_own(i) or is_own(j)

    ones = jnp.ones((subs, LANES), jnp.int32)
    left_mask = ones * has_left.astype(jnp.int32) > 0
    right_mask = ones * has_right.astype(jnp.int32) > 0
    masks = {}
    for b in range(REACH + 1):
        ahead = grid.has_ahead(b)
        masks[(b, 0)] = ahead
        masks[(b, -1)] = ahead & left_mask
        masks[(b, 1)] = ahead & right_mask

    def mask_of(b, i, j):
        side = 0
        if min(i, j) < REACH:
            side = -1
        if max(i, j) >= REACH + cols:
            side = 1
        if b == 0 and side == 0:
            return None
        return masks[(b, side)]

    ring = {a: grid.ring(a) for a in range(REACH + 1)}
    for x in range(wide):
        mass = ring[0]
        for a in range(-REACH, REACH + 1):
            if a == 0:
                continue
            term = ring[abs(a)]
            if is_own(x) and x + a < REACH:
                term = jnp.where(left_mask, term, 0.0)
            if is_own(x) and x + a >= REACH + cols:
                term = jnp.where(right_mask, term, 0.0)
            mass = mass + term
        weight_ref[x] = 1.0 / mass
    slot = {}
    for x in range(wide):
        moved = grid.ahead(weight_ref[x], (1, 2, 3))
        moved[0] = weight_ref[x]
        for b, offsets in BONDS.items():
            for a in offsets:
                i = x - a
                if 0 <= i < wide and needed(i, x):
                    slot[(b, a, i)] = len(slot)
                    pair_ref[slot[(b, a, i)]] = weight_ref[i] + moved[b]

    def ply(p, carry):
        for x in range(cols):
            fill_rows(grid, rows_ref, REACH + x, [row_of(u_ref, (c, p), x, cols, subs) for c in range(3)])
        for j in range(REACH):
            at = [(c * plies + p) * REACH + j for c in range(3)]
            from_a = [ua_ref[0, at[c]] for c in range(3)]
            from_b = [ub_ref[0, at[c]] for c in range(3)]
            fill_rows(grid, rows_ref, j, [jnp.where(odd, from_a[c], from_b[c]) for c in range(3)])
            fill_rows(grid, rows_ref, REACH + cols + j, [jnp.where(odd, from_b[c], from_a[c]) for c in range(3)])
        for x in range(wide):
            sum_ref[x] = jnp.zeros((subs, LANES), jnp.float32)
        extension_sums(grid, rows_ref, sum_ref, 0, wide, crossing, mask_of)
        for x in range(wide):
            if is_own(x):
                inner = t_ref[p, x - REACH]
            else:
                j = x if x < REACH else x - REACH - cols
                from_a = ta_ref[0, p * REACH + j]
                from_b = tb_ref[0, p * REACH + j]
                inner = jnp.where(odd, from_a, from_b) if x < REACH else jnp.where(odd, from_b, from_a)
            weight = weight_ref[x]
            strain = 3.0 * (sum_ref[x] + inner) * weight * weight
            strain_ref[0, x] = strain
            for b, moved in grid.ahead(strain, (1, 2, 3)).items():
                strain_ref[b, x] = moved

        ply_total = ply_peers * plies
        layer = slab * plies + p
        up = jnp.where(layer < ply_total - 1, stiff_ref[jnp.minimum(layer, ply_total - 2)], 0.0)
        down = jnp.where(layer > 0, stiff_ref[jnp.maximum(layer - 1, 0)], 0.0)
        top = p == plies - 1
        bottom = p == 0
        for c in range(3):
            for x in range(cols):
                here = rows_ref[0, c, REACH + x]
                over = jnp.where(
                    top,
                    row_of(above_ref, (c, 0), x, cols, subs),
                    row_of(u_ref, (c, jnp.minimum(p + 1, plies - 1)), x, cols, subs),
                )
                under = jnp.where(
                    bottom,
                    row_of(below_ref, (c, 0), x, cols, subs),
                    row_of(u_ref, (c, jnp.maximum(p - 1, 0)), x, cols, subs),
                )
                force_ref[c, x] = up * (over - here) + down * (under - here)

        angle = angle_ref[p]
        shifted = {}
        for b, offsets in BONDS.items():
            for i in range(wide):
                pairs = [(a, i + a) for a in offsets if 0 <= i + a < wide and needed(i, i + a)]
                if not pairs:
                    continue
                here = [rows_ref[0, c, i] for c in range(3)]
                strain = strain_ref[0, i]
                mine = None
                for a, j in pairs:
                    length = length_of(a, b)
                    shear = table_ref[angle, COLUMNS[(a, b)]]
                    alpha = 3.0 * bulk_modulus - 5.0 * shear
                    beta = 15.0 / length * shear
                    there = [rows_ref[b, c, j] for c in range(3)]
                    sep = separation(here, here[0] - float(a) if a else here[0], there)
                    r = lax.rsqrt(square(sep))
                    f = (alpha * r) * (strain + strain_ref[b, j]) + (beta * pair_ref[slot[(b, a, i)]]) * (
                        1.0 - length * r
                    )
                    mask = mask_of(b, i, j)
                    if mask is not None:
                        f = jnp.where(mask, f, 0.0)
                    push = [f * sep[c] for c in range(3)]
                    if is_own(i):
                        mine = push if mine is None else [mine[c] + push[c] for c in range(3)]
                    if is_own(j):
                        if b == 0:
                            for c in range(3):
                                force_ref[c, j - REACH] = force_ref[c, j - REACH] - push[c]
                        else:
                            key = (j, b)
                            if key in shifted:
                                shifted[key] = [shifted[key][c] + push[c] for c in range(3)]
                            else:
                                shifted[key] = push
                if mine is not None:
                    for c in range(3):
                        add_to(force_ref, (c, i - REACH), mine[c])
        for x in range(cols):
            for c in range(3):
                rows = {b: shifted[(x + REACH, b)][c] for b in (1, 2, 3)}
                total = force_ref[c, x] - grid.back(rows)
                out_ref[c, p, pl.ds(x, subs, stride=cols), :] = total
        return carry

    lax.fori_loop(0, plies, ply, 0)


def local(displacement, angle_index, bond_table, interface_stiffness):
    comps, plies, cols, rows = displacement.shape
    subs = rows // LANES
    tiles = lax.axis_size("tile")
    slabs = lax.axis_size("ply")
    assert rows % LANES == 0 and cols >= 2 * REACH
    view = (
        displacement.reshape(comps, plies, cols, subs, LANES)
        .transpose(0, 1, 3, 2, 4)
        .reshape(comps, plies, subs * cols, LANES)
    )
    f32 = jnp.float32
    whole = pl.BlockSpec(memory_space=pltpu.VMEM)
    scalars = pl.BlockSpec(memory_space=pltpu.SMEM)
    params = pltpu.CompilerParams(vmem_limit_bytes=VMEM_LIMIT)

    swap_a = [(i, i ^ 1) for i in range(tiles) if (i ^ 1) < tiles]
    swap_b = [(i, j) for k in range(1, tiles - 1, 2) for i, j in ((k, k + 1), (k + 1, k))]
    edge = jax.ShapeDtypeStruct((1, comps * plies * REACH, subs, LANES), f32)
    edge_a, edge_b = pl.pallas_call(
        lambda *refs: pack_kernel(tiles, *refs),
        out_shape=[edge, edge],
        in_specs=[whole],
        out_specs=[whole, whole],
        compiler_params=params,
        name="pack",
    )(view)
    got_a = lax.ppermute(edge_a, "tile", swap_a)
    got_b = lax.ppermute(edge_b, "tile", swap_b)

    thin = jax.ShapeDtypeStruct((1, plies * REACH, subs, LANES), f32)
    inner, thin_a, thin_b = pl.pallas_call(
        inner_kernel,
        out_shape=[jax.ShapeDtypeStruct((plies, cols, subs, LANES), f32), thin, thin],
        in_specs=[whole],
        out_specs=[whole, whole, whole],
        scratch_shapes=[
            pltpu.VMEM((REACH + 1, 3, cols, subs, LANES), f32),
            pltpu.VMEM((cols, subs, LANES), f32),
        ],
        compiler_params=params,
        name="inner",
    )(view)
    got_thin_a = lax.ppermute(thin_a, "tile", swap_a)
    got_thin_b = lax.ppermute(thin_b, "tile", swap_b)
    above = lax.ppermute(view[:, :1], "ply", [(i + 1, i) for i in range(slabs - 1)])
    below = lax.ppermute(view[:, plies - 1 :], "ply", [(i, i + 1) for i in range(slabs - 1)])

    wide = cols + 2 * REACH
    out = pl.pallas_call(
        lambda *refs: force_kernel(slabs, tiles, *refs),
        out_shape=jax.ShapeDtypeStruct(view.shape, f32),
        in_specs=[scalars] * 3 + [whole] * 8,
        out_specs=whole,
        scratch_shapes=[
            pltpu.VMEM((REACH + 1, 3, wide, subs, LANES), f32),
            pltpu.VMEM((wide, subs, LANES), f32),
            pltpu.VMEM((REACH + 1, wide, subs, LANES), f32),
            pltpu.VMEM((wide, subs, LANES), f32),
            pltpu.VMEM((14 * wide, subs, LANES), f32),
            pltpu.VMEM((3, cols, subs, LANES), f32),
        ],
        compiler_params=params,
        name="force",
    )(
        angle_index, bond_table, interface_stiffness, view, got_a, got_b, inner, got_thin_a, got_thin_b,
        above, below,
    )
    return (
        out.reshape(comps, plies, subs, cols, LANES)
        .transpose(0, 1, 3, 2, 4)
        .reshape(comps, plies, cols, rows)
    )


def solution(mesh):
    placed = (P(None, "ply", "tile", None), P("ply"), P(), P())
    return jax.shard_map(
        local, mesh=mesh, in_specs=placed, out_specs=P(None, "ply", "tile", None), check_vma=False
    )
```

time: 61.4 us -> 27.7 us (0.45)
  the two profiles are of different devices: /device:TPU:0 before, /device:TPU:6 now
where the time goes in v1:
time: 27.7 us; the launch traced here: 27.4 us
  starting transfers between devices  14.4 us (52%)
  Pallas kernels  7.92 us (29%)
  waiting for transfers between devices  3.84 us (14%)
  local copies, waits for them, and re-layouts  1.1 us (4%)
    pallas_call x1, Pallas kernels, local(): pl.pallas_call(lambda *refs: force_kernel(slabs, tiles, *refs), out_shape...  5.95 us
    ppermute x1, waiting for transfers between devices, local(): got_thin_b = lax.ppermute(thin_b, 'tile', swap_b)  3.82 us
    ppermute x1, starting transfers between devices, local(): lax.ppermute(view[:, :1], 'ply', [(i + 1, i) for i in range(slabs - 1)])  3.64 us
    ppermute x1, starting transfers between devices, local(): got_b = lax.ppermute(edge_b, 'tile', swap_b)  3.42 us
    ppermute x1, starting transfers between devices, local(): got_thin_b = lax.ppermute(thin_b, 'tile', swap_b)  3.31 us
    ppermute x1, starting transfers between devices, local(): lax.ppermute(view[:, plies - 1:], 'ply', [(i, i + 1) for i in range(slabs...  1.92 us
    pallas_call x1, Pallas kernels, local(): pl.pallas_call(inner_kernel, out_shape=[jax.ShapeDtypeStruct((plies, cols...  1.9 us
    ppermute x1, starting transfers between devices, local(): got_a = lax.ppermute(edge_a, 'tile', swap_a)  1.58 us
  transfers between devices with their start and end apart: 6, of which 1 were waited for; matrix products, arithmetic and copies ran while one was open for 0% of the time, Pallas kernels for 0%

profile of v1, /device:TPU:6, one launch (start us, length us, event | category | flops | bytes accessed | tf_op | source)
XLA Modules:
  0.0 27.4 jit_solution(5286764028910854952)
XLA Ops:
  0.0 0.0 copy-start
  0.0 1.1 %copy-done = f32[3,6,8,1024]{3,2,1,0:T(8,128)S(1)} copy-done((f32[3,6,8,1024]{3,2,1,0:T(8,128)S(1)}, f32[3,6,8,1024]{3,2,1,0:T(8,128)}, u32[]{:S(2)}) %copy-start) | copy-done | bytes 589848
  1.1 1.9 %inner.1 = (f32[6,8,8,128]{3,2,1,0:T(8,128)S(1)}, f32[1,18,8,128]{3,2,1,0:T(8,128)S(1)}, f32[1,18,8,128]{3,2,1,0:T(8,128)S(1)}) custom-call(f32[3,6,64,128]{3,2,1,0:T(8,128)S(1)} %bitcast.10), custom_call_target="tpu_custom_call" | custom-call | tf_op jit(solution)/shard_map/inner/pallas_call | solution.py:363
  3.0 0.6 %collective-permute-start.2 = (f32[1,18,8,128]{3,2,1,0:T(8,128)S(1)}, f32[1,18,8,128]{3,2,1,0:T(8,128)S(1)}, u32[]{:S(2)}, u32[]{:S(2)}) collective-permute-start(f32[1,18,8,128]{3,2,1,0:T(8,128)S(1)} %get-tuple-element.13), channel_id=1, source_target_pairs={{0,1},{1,0},{2,3},{3,2},{4,5},{5,4},{6,7},{7,6},{8,9},{9,8},{10,11... | collective-permute-start | bytes 221192 | tf_op jit(solution)/shard_map/ppermute | solution.py:375
  3.5 0.1 pack.1
  3.6 1.6 %collective-permute-start = (f32[1,54,8,128]{3,2,1,0:T(8,128)S(1)}, f32[1,54,8,128]{3,2,1,0:T(8,128)S(1)}, u32[]{:S(2)}, u32[]{:S(2)}) collective-permute-start(f32[1,54,8,128]{3,2,1,0:T(8,128)S(1)} %get-tuple-element.10), channel_id=1, source_target_pairs={{0,1},{1,0},{2,3},{3,2},{4,5},{5,4},{6,7},{7,6},{8,9},{9,8},{10,11... | collective-permute-start | bytes 663560 | tf_op jit(solution)/shard_map/ppermute | solution.py:359
  5.2 3.4 %collective-permute-start.1 = (f32[1,54,8,128]{3,2,1,0:T(8,128)S(1)}, f32[1,54,8,128]{3,2,1,0:T(8,128)S(1)}, u32[]{:S(2)}, u32[]{:S(2)}) collective-permute-start(f32[1,54,8,128]{3,2,1,0:T(8,128)S(1)} %get-tuple-element.11), channel_id=1, source_target_pairs={{1,2},{2,1},{3,4},{4,3},{5,6},{6,5},{9,10},{10,9},{11,12},{12,11},... | collective-permute-start | bytes 663560 | tf_op jit(solution)/shard_map/ppermute | solution.py:360
  8.7 1.9 %collective-permute-start.5 = (f32[3,1,64,128]{3,2,1,0:T(8,128)S(1)}, f32[3,1,64,128]{3,2,1,0:T(8,128)S(1)}, u32[]{:S(2)}, u32[]{:S(2)}) collective-permute-start(f32[3,1,64,128]{3,2,1,0:T(8,128)S(1)} %get-tuple-element.15), channel_id=1, source_target_pairs={{0,8},{8,16},{16,24},{1,9},{9,17},{17,25},{2,10},{10,18},{18,26},{... | collective-permute-start | bytes 294920 | tf_op jit(solution)/shard_map/ppermute | solution.py:378
  10.6 0.0 copy-start.1
  10.6 3.6 %collective-permute-start.4 = (f32[3,1,64,128]{3,2,1,0:T(8,128)S(1)}, f32[3,1,64,128]{3,2,1,0:T(8,128)S(1)}, u32[]{:S(2)}, u32[]{:S(2)}) collective-permute-start(f32[3,1,64,128]{3,2,1,0:T(8,128)S(1)} %get-tuple-element.16), channel_id=1, source_target_pairs={{8,0},{16,8},{24,16},{9,1},{17,9},{25,17},{10,2},{18,10},{26,18},{... | collective-permute-start | bytes 294920 | tf_op jit(solution)/shard_map/ppermute | solution.py:377
  14.2 0.0 collective-permute-done.2.refs_7_
  14.3 0.0 copy-start.2
  14.3 0.0 copy-start.3
  14.3 3.3 %collective-permute-start.3 = (f32[1,18,8,128]{3,2,1,0:T(8,128)S(1)}, f32[1,18,8,128]{3,2,1,0:T(8,128)S(1)}, u32[]{:S(2)}, u32[]{:S(2)}) collective-permute-start(f32[1,18,8,128]{3,2,1,0:T(8,128)S(1)} %get-tuple-element.14), channel_id=1, source_target_pairs={{1,2},{2,1},{3,4},{4,3},{5,6},{6,5},{9,10},{10,9},{11,12},{12,11},... | collective-permute-start | bytes 221192 | tf_op jit(solution)/shard_map/ppermute | solution.py:376
  17.6 3.8 %collective-permute-done.3.refs_8_ = f32[1,18,8,128]{3,2,1,0:T(8,128)S(1)} collective-permute-done((f32[1,18,8,128]{3,2,1,0:T(8,128)S(1)}, f32[1,18,8,128]{3,2,1,0:T(8,128)S(1)}, u32[]{:S(2)}, u32[]{:S(2)}) %collective-permute-start.3) | collective-permute-done | bytes 73760 | tf_op jit(solution)/shard_map/ppermute | solution.py:376
  21.4 0.0 collective-permute-done.5.refs_10_
  21.4 0.0 collective-permute-done.4.refs_9_
  21.4 0.0 collective-permute-done.refs_4_
  21.4 0.0 collective-permute-done.1.refs_5_
  21.4 0.0 copy-done.1
  21.5 0.0 copy-done.2
  21.5 0.0 copy-done.3
  21.5 5.9 %force.1 = f32[3,6,64,128]{3,2,1,0:T(8,128)} custom-call(s32[6]{0:T(128)S(1)} %copy-done.2, f32[4,14]{1,0:T(4,128)S(1)} %copy-done.1, f32[23]{0:T(128)S(1)} %copy-done.3, f32[3,6,64,128]{3,2,1,0:T(8,128)S(1)} %bitcast.13, f32[1,54,8,128]{3,2,1,0:T(8,128)S(1)} %collective-permute-done.refs_4_, f32[1,54,8,128]{3,2,1,0:T(8,128)S(1)} %collective-permute-done.1.refs_5_, ...), custom_call_target="tpu_custom_call" | custom-call | tf_op jit(solution)/shard_map/force/pallas_call | solution.py:381
  (1 shorter events, 0.0 us)
Async XLA Ops:
  0.0 1.1 %copy-start = (f32[3,6,8,1024]{3,2,1,0:T(8,128)S(1)}, f32[3,6,8,1024]{3,2,1,0:T(8,128)}, u32[]{:S(2)}) copy-start(f32[3,6,8,1024]{3,2,1,0:T(8,128)} %param.4) | copy-start | bytes 1769476
  3.0 11.3 %collective-permute-start.2 = (f32[1,18,8,128]{3,2,1,0:T(8,128)S(1)}, f32[1,18,8,128]{3,2,1,0:T(8,128)S(1)}, u32[]{:S(2)}, u32[]{:S(2)}) collective-permute-start(f32[1,18,8,128]{3,2,1,0:T(8,128)S(1)} %get-tuple-element.13), channel_id=1, source_target_pairs={{0,1},{1,0},{2,3},{3,2},{4,5},{5,4},{6,7},{7,6},{8,9},{9,8},{10,11... | collective-permute-start | bytes 221192 | tf_op jit(solution)/shard_map/ppermute | solution.py:375
  3.6 17.8 %collective-permute-start = (f32[1,54,8,128]{3,2,1,0:T(8,128)S(1)}, f32[1,54,8,128]{3,2,1,0:T(8,128)S(1)}, u32[]{:S(2)}, u32[]{:S(2)}) collective-permute-start(f32[1,54,8,128]{3,2,1,0:T(8,128)S(1)} %get-tuple-element.10), channel_id=1, source_target_pairs={{0,1},{1,0},{2,3},{3,2},{4,5},{5,4},{6,7},{7,6},{8,9},{9,8},{10,11... | collective-permute-start | bytes 663560 | tf_op jit(solution)/shard_map/ppermute | solution.py:359
  5.2 16.2 %collective-permute-start.1 = (f32[1,54,8,128]{3,2,1,0:T(8,128)S(1)}, f32[1,54,8,128]{3,2,1,0:T(8,128)S(1)}, u32[]{:S(2)}, u32[]{:S(2)}) collective-permute-start(f32[1,54,8,128]{3,2,1,0:T(8,128)S(1)} %get-tuple-element.11), channel_id=1, source_target_pairs={{1,2},{2,1},{3,4},{4,3},{5,6},{6,5},{9,10},{10,9},{11,12},{12,11},... | collective-permute-start | bytes 663560 | tf_op jit(solution)/shard_map/ppermute | solution.py:360
  8.7 12.8 %collective-permute-start.5 = (f32[3,1,64,128]{3,2,1,0:T(8,128)S(1)}, f32[3,1,64,128]{3,2,1,0:T(8,128)S(1)}, u32[]{:S(2)}, u32[]{:S(2)}) collective-permute-start(f32[3,1,64,128]{3,2,1,0:T(8,128)S(1)} %get-tuple-element.15), channel_id=1, source_target_pairs={{0,8},{8,16},{16,24},{1,9},{9,17},{17,25},{2,10},{10,18},{18,26},{... | collective-permute-start | bytes 294920 | tf_op jit(solution)/shard_map/ppermute | solution.py:378
  10.6 10.9 %copy-start.1 = (f32[4,14]{1,0:T(4,128)S(1)}, f32[4,14]{1,0:T(4,128)}, u32[]{:S(2)}) copy-start(f32[4,14]{1,0:T(4,128)} %refs_1_.1) | copy-start | bytes 676
  10.6 10.8 %collective-permute-start.4 = (f32[3,1,64,128]{3,2,1,0:T(8,128)S(1)}, f32[3,1,64,128]{3,2,1,0:T(8,128)S(1)}, u32[]{:S(2)}, u32[]{:S(2)}) collective-permute-start(f32[3,1,64,128]{3,2,1,0:T(8,128)S(1)} %get-tuple-element.16), channel_id=1, source_target_pairs={{8,0},{16,8},{24,16},{9,1},{17,9},{25,17},{10,2},{18,10},{26,18},{... | collective-permute-start | bytes 294920 | tf_op jit(solution)/shard_map/ppermute | solution.py:377
  14.3 7.2 %copy-start.2 = (s32[6]{0:T(128)S(1)}, s32[6]{0:T(128)}, u32[]{:S(2)}) copy-start(s32[6]{0:T(128)} %refs_0_.1) | copy-start | bytes 76
  14.3 7.2 %copy-start.3 = (f32[23]{0:T(128)S(1)}, f32[23]{0:T(128)}, u32[]{:S(2)}) copy-start(f32[23]{0:T(128)} %refs_2_.1) | copy-start | bytes 280
  14.3 7.1 %collective-permute-start.3 = (f32[1,18,8,128]{3,2,1,0:T(8,128)S(1)}, f32[1,18,8,128]{3,2,1,0:T(8,128)S(1)}, u32[]{:S(2)}, u32[]{:S(2)}) collective-permute-start(f32[1,18,8,128]{3,2,1,0:T(8,128)S(1)} %get-tuple-element.14), channel_id=1, source_target_pairs={{1,2},{2,1},{3,4},{4,3},{5,6},{6,5},{9,10},{10,9},{11,12},{12,11},... | collective-permute-start | bytes 221192 | tf_op jit(solution)/shard_map/ppermute | solution.py:376

commit v2 on v0

v2 whole, which is shorter than its diff:
```python
import math

import jax
import jax.numpy as jnp
from jax import lax
from jax.experimental import pallas as pl
from jax.experimental.pallas import tpu as pltpu
from jax.sharding import PartitionSpec as P

bulk_modulus = 40.0
REACH = 3
LANES = 128
VMEM_LIMIT = 24 * 1024 * 1024


def bond_columns():
    halves = []
    for a in range(-REACH, REACH + 1):
        for b in range(-REACH, REACH + 1):
            if 0 < a * a + b * b <= 9 and (a > 0 or (a == 0 and b > 0)):
                halves.append((a, b))
    columns = {}
    for index, (a, b) in enumerate(halves):
        columns[(a, b)] = index
        columns[(-a, -b)] = index
    return columns


COLUMNS = bond_columns()
BONDS = {0: (1, 2, 3), 1: (-2, -1, 0, 1, 2), 2: (-2, -1, 0, 1, 2), 3: (0,)}


def length_of(a, b):
    return math.sqrt(a * a + b * b)


class Plan:
    def __init__(self, cols):
        self.cols = cols
        self.wide = cols + 2 * REACH
        self.own = range(REACH, REACH + cols)
        self.low = range(0, REACH)
        self.high = range(REACH + cols, self.wide)
        self.near_b = range(REACH, 2 * REACH)
        self.near_a = range(cols, cols + REACH)
        every = [
            (b, a, i)
            for b, offsets in BONDS.items()
            for i in range(self.wide)
            for a in offsets
            if 0 <= i + a < self.wide and (i in self.own or i + a in self.own)
        ]
        inner = [k for k in every if k[2] in self.own and k[2] + k[1] in self.own]
        self.inner_a = [k for k in inner if k[2] in self.near_a or k[2] + k[1] in self.near_a]
        self.inner_b = [k for k in inner if k not in self.inner_a]
        self.cross_a = [k for k in every if max(k[2], k[2] + k[1]) in self.high]
        self.cross_b = [k for k in every if min(k[2], k[2] + k[1]) in self.low]
        self.late = [k for k in every if min(k[2], k[2] + k[1]) < 2 * REACH]
        self.early = [k for k in every if k not in self.late]
        self.start_a = min(min(k[2], k[2] + k[1]) for k in self.inner_a)


class Grid:
    def __init__(self, subs):
        self.subs = subs
        self.lane = lax.broadcasted_iota(jnp.int32, (subs, LANES), 1)
        self.y = lax.broadcasted_iota(jnp.int32, (subs, LANES), 0) * LANES + self.lane
        self.total = subs * LANES
        self.exists = {b: self.y < self.total - b for b in range(1, REACH + 1)}

    def ahead(self, row):
        after = pltpu.roll(row, self.subs - 1, axis=0)
        return {
            b: pltpu.roll(jnp.where(self.lane < b, after, row), LANES - b, axis=1) for b in range(1, REACH + 1)
        }

    def back(self, rows):
        total = None
        for b, row in rows.items():
            before = pltpu.roll(row, 1, axis=0)
            moved = pltpu.roll(jnp.where(self.lane >= LANES - b, before, row), b, axis=1)
            total = moved if total is None else total + moved
        return total

    def ring(self, a):
        total = None
        for b in range(-REACH, REACH + 1):
            if 0 < a * a + b * b <= 9:
                exists = (self.y + b >= 0) & (self.y + b < self.total)
                term = jnp.where(exists, length_of(a, b), 0.0)
                total = term if total is None else total + term
        return total


class Store:
    def __init__(self, *parts):
        self.parts = parts

    def at(self, column, *lead):
        for ref, first, columns, head in self.parts:
            if column in columns:
                return ref, (*head, *lead, column - first)
        raise KeyError(column)

    def get(self, column, *lead):
        ref, index = self.at(column, *lead)
        return ref[index]

    def put(self, column, value, *lead):
        ref, index = self.at(column, *lead)
        ref[index] = value


def frame():
    odd = lax.axis_index("tile") % 2 == 1
    return odd, jnp.where(odd, -1.0, 1.0).astype(jnp.float32)


def sides(tiles):
    tile = lax.axis_index("tile")
    has_a = (tile % 2 == 1) | (tile + 1 < tiles)
    has_b = jnp.where(tile % 2 == 1, tile + 1 < tiles, tile > 0)
    return has_a, has_b


def keep_row(grid, rows, column, row):
    for c in range(3):
        rows.put(column, row[c], 0, c)
        for b, moved in grid.ahead(row[c]).items():
            rows.put(column, moved + float(b) if c == 1 else moved, b, c)


def separation(rows, b, a, i, here):
    there = [rows.get(i + a, b, c) for c in range(3)]
    here_x = here[0] - float(a) if a else here[0]
    return there[0] - here_x, there[1] - here[1], there[2] - here[2]


def by_row(keys):
    groups = {}
    for b, a, i in keys:
        groups.setdefault((b, i), []).append(a)
    return groups.items()


def extension_sums(grid, rows, keys, mask_of, keep):
    sums = {}
    shifted = {}
    for (b, i), offsets in by_row(keys):
        here = [rows.get(i, 0, c) for c in range(3)]
        for a in offsets:
            sep = separation(rows, b, a, i, here)
            q = sep[0] * sep[0] + sep[1] * sep[1] + sep[2] * sep[2]
            r = lax.rsqrt(q)
            keep((b, a, i), r)
            e = q * r - length_of(a, b)
            mask = mask_of(b)
            if mask is not None:
                e = jnp.where(mask, e, 0.0)
            sums[i] = sums[i] + e if i in sums else e
            if b == 0:
                sums[i + a] = sums[i + a] + e if i + a in sums else e
            else:
                key = (i + a, b)
                shifted[key] = shifted[key] + e if key in shifted else e
    for x in sorted({x for x, _ in shifted}):
        total = grid.back({b: shifted[(x, b)] for b in range(1, REACH + 1) if (x, b) in shifted})
        sums[x] = sums[x] + total if x in sums else total
    return sums


def near_a_kernel(plan, u_hbm, message, rows_ref, rest_ref, sums_ref, inverse_ref, u_ref, sems):
    comps, plies, depth, _ = u_ref.shape
    subs = depth // plan.cols
    copies = [
        pltpu.make_async_copy(u_hbm.at[:, pl.ds(p, 1)], u_ref.at[:, pl.ds(p, 1)], sems.at[p]) for p in range(plies)
    ]
    for copy in copies:
        copy.start()
    grid = Grid(subs)
    odd, sign = frame()
    slots = {key: n for n, key in enumerate(plan.inner_a)}

    def source(p, c, column):
        x = column - REACH
        at = jnp.where(odd, plan.cols - 1 - x, x)
        row = u_ref[c, p, pl.ds(at, subs, stride=plan.cols), :]
        return row * sign if c == 0 else row

    def ply(p, carry):
        pltpu.make_async_copy(u_hbm.at[:, pl.ds(p, 1)], u_ref.at[:, pl.ds(p, 1)], sems.at[p]).wait()
        rows = Store((rows_ref, plan.start_a, range(plan.start_a, plan.own.stop), (p,)))
        for x in rows.parts[0][2]:
            row = [source(p, c, x) for c in range(3)]
            keep_row(grid, rows, x, row)
            if x in plan.near_a:
                for c in range(3):
                    message[0, p, c * REACH + x - plan.near_a.start] = row[c]
        for x in range(REACH, plan.start_a):
            for c in range(3):
                rest_ref[p, c, x - REACH] = source(p, c, x)

        def keep(key, r):
            inverse_ref[p, slots[key]] = r

        sums = extension_sums(grid, rows, plan.inner_a, grid.exists.get, keep)
        for x in rows.parts[0][2]:
            sums_ref[p, x - plan.start_a] = sums[x]
            if x in plan.near_a:
                message[0, p, 3 * REACH + x - plan.near_a.start] = sums[x]
        return carry

    lax.fori_loop(0, plies, ply, 0)


def near_b_kernel(plan, rows_a_ref, rest_ref, sums_a_ref, message, rows_ref, sums_ref, inverse_ref, bottom_ref, top_ref):
    plies = rows_a_ref.shape[0]
    grid = Grid(rows_a_ref.shape[-2])
    slots = {key: n for n, key in enumerate(plan.inner_b)}
    fresh = range(REACH, plan.start_a)

    def ply(p, carry):
        rows = Store(
            (rows_ref, REACH, fresh, (p,)), (rows_a_ref, plan.start_a, range(plan.start_a, plan.own.stop), (p,))
        )
        for x in fresh:
            keep_row(grid, rows, x, [rest_ref[p, c, x - REACH] for c in range(3)])

        def keep(key, r):
            inverse_ref[p, slots[key]] = r

        sums = extension_sums(grid, rows, plan.inner_b, grid.exists.get, keep)
        for x in range(REACH, plan.near_a.start):
            total = sums[x] + sums_a_ref[p, x - plan.start_a] if x >= plan.start_a else sums[x]
            sums_ref[p, x - REACH] = total
            if x in plan.near_b:
                message[0, p, 3 * REACH + x - REACH] = total
                for c in range(3):
                    message[0, p, c * REACH + x - REACH] = rows.get(x, 0, c)
        return carry

    lax.fori_loop(0, plies, ply, 0)
    for p, ref in ((0, bottom_ref), (plies - 1, top_ref)):
        rows = Store(
            (rows_ref, REACH, fresh, (p,)), (rows_a_ref, plan.start_a, range(plan.start_a, plan.own.stop), (p,))
        )
        for c in range(3):
            for x in plan.own:
                ref[0, c, x - REACH] = rows.get(x, 0, c)


def weight_kernel(plan, tiles, weight_ref, pair_ref):
    grid = Grid(weight_ref.shape[-2])
    ones = jnp.ones((grid.subs, LANES), jnp.int32)
    has_a, has_b = (ones * side.astype(jnp.int32) > 0 for side in sides(tiles))
    ring = {a: grid.ring(a) for a in range(REACH + 1)}
    weight = {}
    for x in range(plan.wide):
        mass = ring[0]
        for a in range(-REACH, REACH + 1):
            term = ring[abs(a)]
            if x in plan.own and x + a in plan.low:
                term = jnp.where(has_b, term, 0.0)
            if x in plan.own and x + a in plan.high:
                term = jnp.where(has_a, term, 0.0)
            if a:
                mass = mass + term
        weight[x] = 1.0 / mass
        weight_ref[x] = weight[x]
    moved = {x: {0: weight[x], **grid.ahead(weight[x])} for x in range(plan.wide)}
    for n, (b, a, i) in enumerate(plan.early + plan.late):
        pair_ref[n] = weight[i] + moved[i + a][b]


def bond_forces(plan, grid, odd, table_ref, angle, rows, strains, inverse, pair, keys, mask_of, force):
    shears = {}

    def shear_of(a, b):
        if (a, b) not in shears:
            column = COLUMNS[(a, b)]
            mirrored = COLUMNS[(-a, b)]
            at = column if column == mirrored else jnp.where(odd, mirrored, column)
            shears[(a, b)] = table_ref[angle, at]
        return shears[(a, b)]

    shifted = {}
    for (b, i), offsets in by_row(keys):
        here = [rows.get(i, 0, c) for c in range(3)]
        strain = strains.get(i, 0)
        mine = None
        for a in offsets:
            j = i + a
            length = length_of(a, b)
            shear = shear_of(a, b)
            alpha = 3.0 * bulk_modulus - 5.0 * shear
            beta = 15.0 / length * shear
            sep = separation(rows, b, a, i, here)
            r = inverse((b, a, i))
            f = (alpha * r) * (strain + strains.get(j, b)) + (beta * pair((b, a, i))) * (1.0 - length * r)
            mask = mask_of(b, i, j)
            if mask is not None:
                f = jnp.where(mask, f, 0.0)
            push = [f * sep[c] for c in range(3)]
            if i in plan.own:
                mine = push if mine is None else [mine[c] + push[c] for c in range(3)]
            if j in plan.own:
                if b == 0:
                    force(j, [-push[c] for c in range(3)])
                elif (j, b) in shifted:
                    shifted[(j, b)] = [shifted[(j, b)][c] + push[c] for c in range(3)]
                else:
                    shifted[(j, b)] = push
        if mine is not None:
            force(i, mine)
    for x in sorted({x for x, _ in shifted}):
        held = {b: shifted[(x, b)] for b in range(1, REACH + 1) if (x, b) in shifted}
        force(x, [-grid.back({b: row[c] for b, row in held.items()}) for c in range(3)])


def early_kernel(
    plan, tiles, slabs, angle_ref, table_ref, stiff_ref, got_ref, rows_a_ref, rows_b_ref, sums_a_ref, sums_b_ref,
    inverse_a_ref, inverse_b_ref, weight_ref, pair_ref, above_ref, below_ref,
    force_ref, strain_ref, halo_ref, cross_ref,
):
    plies = rows_a_ref.shape[0]
    grid = Grid(rows_a_ref.shape[-2])
    odd, _ = frame()
    slab = lax.axis_index("ply")
    in_a = {key: n for n, key in enumerate(plan.inner_a)}
    in_b = {key: n for n, key in enumerate(plan.inner_b)}
    in_cross = {key: n for n, key in enumerate(plan.cross_a)}
    in_pair = {key: n for n, key in enumerate(plan.early + plan.late)}
    first = 2 * REACH
    has_a = None
    if tiles % 2:
        has_a = jnp.ones((grid.subs, LANES), jnp.int32) * sides(tiles)[0].astype(jnp.int32) > 0

    def cross_mask(b):
        mask = grid.exists.get(b)
        if has_a is None:
            return mask
        return has_a if mask is None else mask & has_a

    def mask_of(b, i, j):
        return cross_mask(b) if max(i, j) in plan.high else grid.exists.get(b)

    def ply(p, carry):
        rows = Store(
            (rows_b_ref, REACH, range(REACH, plan.start_a), (p,)),
            (rows_a_ref, plan.start_a, range(plan.start_a, plan.own.stop), (p,)),
            (halo_ref, plan.high.start, plan.high, ()),
        )
        strains = Store((strain_ref, first, range(first, plan.wide), (p,)))
        for j in range(REACH):
            row = [got_ref[0, p, c * REACH + j] for c in range(3)]
            keep_row(grid, rows, plan.wide - 1 - j, [-row[0], row[1], row[2]])

        def keep(key, r):
            cross_ref[in_cross[key]] = r

        sums = extension_sums(grid, rows, plan.cross_a, cross_mask, keep)
        for x in range(first, plan.wide):
            if x in plan.high:
                total = got_ref[0, p, 3 * REACH + plan.wide - 1 - x]
            elif x >= plan.near_a.start:
                total = sums_a_ref[p, x - plan.start_a]
            else:
                total = sums_b_ref[p, x - REACH]
            if x in sums:
                total = total + sums[x]
            strain = 3.0 * total * (weight_ref[x] * weight_ref[x])
            strains.put(x, strain, 0)
            for b, moved in grid.ahead(strain).items():
                strains.put(x, moved, b)

        layers = slabs * plies
        layer = slab * plies + p
        up = jnp.where(layer < layers - 1, stiff_ref[jnp.minimum(layer, layers - 2)], 0.0)
        down = jnp.where(layer > 0, stiff_ref[jnp.maximum(layer - 1, 0)], 0.0)
        over = Store(*((r, s, cs, (jnp.minimum(p + 1, plies - 1),)) for r, s, cs, _ in rows.parts[:2]))
        under = Store(*((r, s, cs, (jnp.maximum(p - 1, 0),)) for r, s, cs, _ in rows.parts[:2]))
        for x in plan.own:
            for c in range(3):
                here = rows.get(x, 0, c)
                above = jnp.where(p == plies - 1, above_ref[0, c, x - REACH], over.get(x, 0, c))
                below = jnp.where(p == 0, below_ref[0, c, x - REACH], under.get(x, 0, c))
                force_ref[p, c, x - REACH] = up * (above - here) + down * (below - here)

        def inverse(key):
            if key in in_cross:
                return cross_ref[in_cross[key]]
            return inverse_a_ref[p, in_a[key]] if key in in_a else inverse_b_ref[p, in_b[key]]

        def force(x, values):
            for c in range(3):
                force_ref[p, c, x - REACH] = force_ref[p, c, x - REACH] + values[c]

        bond_forces(
            plan, grid, odd, table_ref, angle_ref[p], rows, strains, inverse, lambda key: pair_ref[in_pair[key]],
            plan.early, mask_of, force,
        )
        return carry

    lax.fori_loop(0, plies, ply, 0)


def late_kernel(
    plan, tiles, angle_ref, table_ref, got_ref, rows_a_ref, rows_b_ref, sums_b_ref, inverse_a_ref, inverse_b_ref,
    weight_ref, pair_ref, force_in_ref, strain_a_ref, out_hbm, halo_ref, cross_ref, strain_ref, force_ref, out_ref, sems,
):
    plies = rows_a_ref.shape[0]
    grid = Grid(rows_a_ref.shape[-2])
    odd, sign = frame()
    in_a = {key: n for n, key in enumerate(plan.inner_a)}
    in_b = {key: n for n, key in enumerate(plan.inner_b)}
    in_cross = {key: n for n, key in enumerate(plan.cross_b)}
    in_pair = {key: n for n, key in enumerate(plan.early + plan.late)}
    first = 2 * REACH
    has_b = jnp.ones((grid.subs, LANES), jnp.int32) * sides(tiles)[1].astype(jnp.int32) > 0
    cross_masks = {b: grid.exists[b] & has_b if b else has_b for b in range(REACH + 1)}

    def mask_of(b, i, j):
        return cross_masks[b] if min(i, j) in plan.low else grid.exists.get(b)

    def ply(p, carry):
        rows = Store(
            (halo_ref, 0, plan.low, ()),
            (rows_b_ref, REACH, range(REACH, plan.start_a), (p,)),
            (rows_a_ref, plan.start_a, range(plan.start_a, plan.own.stop), (p,)),
        )
        strains = Store((strain_ref, 0, range(first), ()), (strain_a_ref, first, range(first, plan.wide), (p,)))
        for j in range(REACH):
            row = [got_ref[0, p, c * REACH + j] for c in range(3)]
            keep_row(grid, rows, REACH - 1 - j, [-row[0], row[1], row[2]])

        def keep(key, r):
            cross_ref[in_cross[key]] = r

        sums = extension_sums(grid, rows, plan.cross_b, cross_masks.get, keep)
        for x in range(first):
            total = got_ref[0, p, 3 * REACH + REACH - 1 - x] if x in plan.low else sums_b_ref[p, x - REACH]
            strain = 3.0 * (total + sums[x]) * (weight_ref[x] * weight_ref[x])
            strains.put(x, strain, 0)
            for b, moved in grid.ahead(strain).items():
                strains.put(x, moved, b)
        for c in range(3):
            for x in plan.own:
                force_ref[c, x - REACH] = force_in_ref[p, c, x - REACH]

        def inverse(key):
            if key in in_cross:
                return cross_ref[in_cross[key]]
            return inverse_a_ref[p, in_a[key]] if key in in_a else inverse_b_ref[p, in_b[key]]

        def force(x, values):
            for c in range(3):
                force_ref[c, x - REACH] = force_ref[c, x - REACH] + values[c]

        bond_forces(
            plan, grid, odd, table_ref, angle_ref[p], rows, strains, inverse, lambda key: pair_ref[in_pair[key]],
            plan.late, mask_of, force,
        )
        for x in plan.own:
            at = jnp.where(odd, plan.cols - 1 - (x - REACH), x - REACH)
            for c in range(3):
                value = force_ref[c, x - REACH]
                out_ref[c, p, pl.ds(at, grid.subs, stride=plan.cols), :] = value * sign if c == 0 else value
        pltpu.make_async_copy(out_ref.at[:, pl.ds(p, 1)], out_hbm.at[:, pl.ds(p, 1)], sems.at[p]).start()
        return carry

    lax.fori_loop(0, plies, ply, 0)
    for p in range(plies):
        pltpu.make_async_copy(out_ref.at[:, pl.ds(p, 1)], out_hbm.at[:, pl.ds(p, 1)], sems.at[p]).wait()


def local(displacement, angle_index, bond_table, interface_stiffness):
    comps, plies, cols, length = displacement.shape
    subs = length // LANES
    tiles = lax.axis_size("tile")
    slabs = lax.axis_size("ply")
    assert length % LANES == 0 and cols >= 2 * REACH
    plan = Plan(cols)
    view = (
        displacement.reshape(comps, plies, cols, subs, LANES)
        .transpose(0, 1, 3, 2, 4)
        .reshape(comps, plies, subs * cols, LANES)
    )
    whole = pl.BlockSpec(memory_space=pltpu.VMEM)
    scalars = pl.BlockSpec(memory_space=pltpu.SMEM)
    anywhere = pl.BlockSpec(memory_space=pl.ANY)

    def array(*shape):
        return jax.ShapeDtypeStruct((*shape, subs, LANES), jnp.float32)

    def scratch(*shape):
        return pltpu.VMEM((*shape, subs, LANES), jnp.float32)

    def call(body, name, ins, outs, out_specs=None, scratches=(), vectors=0):
        return pl.pallas_call(
            body,
            out_shape=outs,
            in_specs=ins,
            out_specs=out_specs or [whole] * len(outs),
            scratch_shapes=list(scratches),
            compiler_params=pltpu.CompilerParams(vmem_limit_bytes=VMEM_LIMIT),
            cost_estimate=pl.CostEstimate(flops=vectors * subs * LANES, bytes_accessed=1 << 20, transcendentals=0),
            name=name,
        )

    swap_a = [(i, i ^ 1) for i in range(tiles) if (i ^ 1) < tiles]
    swap_b = [(i, j) for k in range(1, tiles - 1, 2) for i, j in ((k, k + 1), (k + 1, k))]
    tall = plan.own.stop - plan.start_a
    short = plan.start_a - REACH

    message_a, rows_a, rest, sums_a, inverse_a = call(
        lambda *refs: near_a_kernel(plan, *refs),
        "near_a",
        [anywhere],
        [
            array(1, plies, 4 * REACH), array(plies, REACH + 1, 3, tall), array(plies, 3, short), array(plies, tall),
            array(plies, len(plan.inner_a)),
        ],
        scratches=[pltpu.VMEM(view.shape, jnp.float32), pltpu.SemaphoreType.DMA((plies,))],
        vectors=plies * 1000,
    )(view)
    got_a = lax.ppermute(message_a, "tile", swap_a)

    message_b, rows_b, sums_b, inverse_b, bottom, top = call(
        lambda *refs: near_b_kernel(plan, *refs),
        "near_b",
        [whole] * 3,
        [
            array(1, plies, 4 * REACH), array(plies, REACH + 1, 3, short), array(plies, plan.near_a.start - REACH),
            array(plies, len(plan.inner_b)), array(1, 3, cols), array(1, 3, cols),
        ],
        vectors=plies * 800,
    )(rows_a, rest, sums_a)
    got_b = lax.ppermute(message_b, "tile", swap_b)
    above = lax.ppermute(bottom, "ply", [(i + 1, i) for i in range(slabs - 1)])
    below = lax.ppermute(top, "ply", [(i, i + 1) for i in range(slabs - 1)])

    weight, pair = call(
        lambda *refs: weight_kernel(plan, tiles, *refs),
        "weights",
        [],
        [array(plan.wide), array(len(plan.early) + len(plan.late))],
        vectors=600,
    )()

    force, strain = call(
        lambda *refs: early_kernel(plan, tiles, slabs, *refs),
        "early",
        [scalars] * 3 + [whole] * 11,
        [array(plies, 3, cols), array(plies, REACH + 1, plan.wide - 2 * REACH)],
        scratches=[scratch(REACH + 1, 3, REACH), scratch(len(plan.cross_a))],
        vectors=plies * 2000,
    )(
        angle_index, bond_table, interface_stiffness, got_a, rows_a, rows_b, sums_a, sums_b, inverse_a, inverse_b,
        weight, pair, above, below,
    )

    (out,) = call(
        lambda *refs: late_kernel(plan, tiles, *refs),
        "late",
        [scalars] * 2 + [whole] * 10,
        [jax.ShapeDtypeStruct(view.shape, jnp.float32)],
        out_specs=[anywhere],
        scratches=[
            scratch(REACH + 1, 3, REACH), scratch(len(plan.cross_b)), scratch(REACH + 1, 2 * REACH), scratch(3, cols),
            pltpu.VMEM(view.shape, jnp.float32), pltpu.SemaphoreType.DMA((plies,)),
        ],
        vectors=plies * 1700,
    )(
        angle_index, bond_table, got_b, rows_a, rows_b, sums_b, inverse_a, inverse_b, weight, pair, force, strain,
    )
    return (
        out.reshape(comps, plies, subs, cols, LANES)
        .transpose(0, 1, 3, 2, 4)
        .reshape(comps, plies, cols, length)
    )


def solution(mesh):
    placed = (P(None, "ply", "tile", None), P("ply"), P(), P())
    return jax.shard_map(
        local, mesh=mesh, in_specs=placed, out_specs=P(None, "ply", "tile", None), check_vma=False
    )
```

time: 61.4 us -> 25.1 us (0.41)
  other arithmetic: 31.1 us -> 0 us
  Pallas kernels: 0 us -> 9.4 us
  starting transfers between devices: 17.1 us -> 8.04 us
  local copies, waits for them, and re-layouts: 5.82 us -> 1.1 us
  between operations: 0.97 us -> 0.07 us
    another operation x3 -> x0, other arithmetic: 16.2 us -> none  [local(): return jnp.stack([force_x, force_y, force_z]) + layered]
    pallas_call x0 -> x5, Pallas kernels: none -> 9.4 us  [the longest x1 3.32 us: local(): call(lambda *refs: late_kernel(plan, tiles, *refs), 'late', [scalars] * 2...]
    ppermute x6 -> x4, starting transfers between devices: 17.1 us -> 8.04 us  [the longest x1 3.04 us: local(): below = lax.ppermute(top, 'ply', [(i, i + 1) for i in range(slabs - 1)])]
    slice x6 -> x0, local copies, waits for them, and re-layouts: 5.43 us -> none  [the longest x2 1.65 us: padded_2(): first = lax.slice_in_dim(shard, 0, width, axis=dim)]
    div x1 -> x0, other arithmetic: 4.22 us -> none  [local(): dilation = 3.0 * dilation / mass_region]
    sub x2 -> x0, other arithmetic: 3.62 us -> none  [stretch(): gap = neighbour - anchor]
    add x1 -> x0, other arithmetic: 1.95 us -> none  [local(): return jnp.stack([force_x, force_y, force_z]) + layered]
    and x10 -> x0, other arithmetic: 1.65 us -> none  [inside(): (x_next >= 0) & (x_next < x_total) & (y_next >= 0) & (y_next < y_total)]
  transfers between devices with their start and end apart: 6 -> 4, of which waited for: 2 -> 2; matrix products, arithmetic and copies ran while one was open for 55% -> 0% of each run, Pallas kernels for 0% -> 17%
where the time goes in v2:
time: 25.1 us; the launch traced here: 24.9 us
  Pallas kernels  9.4 us (37%)
  starting transfers between devices  8.04 us (32%)
  waiting for transfers between devices  6.31 us (25%)
  local copies, waits for them, and re-layouts  1.1 us (4%)
    ppermute x1, waiting for transfers between devices, local(): got_a = lax.ppermute(message_a, 'tile', swap_a)  5.52 us
    pallas_call x1, Pallas kernels, local(): call(lambda *refs: late_kernel(plan, tiles, *refs), 'late', [scalars] * 2...  3.32 us
    pallas_call x1, Pallas kernels, local(): call(lambda *refs: early_kernel(plan, tiles, slabs, *refs), 'early', [sca...  3.08 us
    ppermute x1, starting transfers between devices, local(): below = lax.ppermute(top, 'ply', [(i, i + 1) for i in range(slabs - 1)])  3.04 us
    ppermute x1, starting transfers between devices, local(): got_a = lax.ppermute(message_a, 'tile', swap_a)  3.03 us
    pallas_call x1, Pallas kernels, local(): call(lambda *refs: near_a_kernel(plan, *refs), 'near_a', [anywhere], [arr...  1.76 us
    ppermute x1, starting transfers between devices, local(): above = lax.ppermute(bottom, 'ply', [(i + 1, i) for i in range(slabs - 1)])  1.29 us
    pallas_call x1, Pallas kernels, local(): call(lambda *refs: near_b_kernel(plan, *refs), 'near_b', [whole] * 3, [ar...  1.11 us
  transfers between devices with their start and end apart: 4, of which 2 were waited for; matrix products, arithmetic and copies ran while one was open for 0% of the time, Pallas kernels for 17%

profile of v2, /device:TPU:0, one launch (start us, length us, event | category | flops | bytes accessed | tf_op | source)
XLA Modules:
  0.0 24.9 jit_solution(6473775731662304977)
XLA Ops:
  0.0 0.0 copy-start.2
  0.0 0.0 copy-start.3
  0.0 0.0 copy-start
  0.0 1.1 %copy-done = f32[3,6,8,1024]{3,2,1,0:T(8,128)S(1)} copy-done((f32[3,6,8,1024]{3,2,1,0:T(8,128)S(1)}, f32[3,6,8,1024]{3,2,1,0:T(8,128)}, u32[]{:S(2)}) %copy-start) | copy-done | bytes 589848
  1.1 0.0 copy-start.1
  1.1 1.8 %near_a.1 = (f32[1,6,12,8,128]{4,3,2,1,0:T(8,128)S(1)}, f32[6,4,3,6,8,128]{5,4,3,2,1,0:T(8,128)S(1)}, f32[6,3,2,8,128]{4,3,2,1,0:T(8,128)S(1)}, f32[6,6,8,128]{3,2,1,0:T(8,128)S(1)}, f32[6,42,8,128]{3,2,1,0:T(8,128)S(1)}) custom-call(f32[3,6,64,128]{3,2,1,0:T(8,128)S(1)} %bitcast.10), custom_call_target="tpu_custom_call" | custom-call | flops 6144000 | bytes 1048576 | tf_op jit(solution)/shard_map/near_a/pallas_call | solution.py:515
  2.9 3.0 %collective-permute-start.1 = (f32[1,6,12,8,128]{4,3,2,1,0:T(8,128)S(1)}, f32[1,6,12,8,128]{4,3,2,1,0:T(8,128)S(1)}, u32[]{:S(2)}, u32[]{:S(2)}) collective-permute-start(f32[1,6,12,8,128]{4,3,2,1,0:T(8,128)S(1)} %get-tuple-element.30), channel_id=1, source_target_pairs={{0,1},{1,0},{2,3},{3,2},{4,5},{5,4},{6,7},{7,6},{8,9},{9,8},{10,11... | collective-permute-start | bytes 884744 | tf_op jit(solution)/shard_map/ppermute | solution.py:526
  5.9 1.1 %near_b.1 = (f32[1,6,12,8,128]{4,3,2,1,0:T(8,128)S(1)}, f32[6,4,3,2,8,128]{5,4,3,2,1,0:T(8,128)S(1)}, f32[6,5,8,128]{3,2,1,0:T(8,128)S(1)}, f32[6,52,8,128]{3,2,...) custom-call(f32[6,4,3,6,8,128]{5,4,3,2,1,0:T(8,128)S(1)} %get-tuple-element.20.refs_0_.refs_4_.refs_3_,, ...), custom_call_target="tpu_custom_call" | custom-call | flops 4915200 | bytes 1048576 | tf_op jit(solution)/shard_map/near_b/pallas_call | solution.py:528
  7.0 0.7 %collective-permute-start = (f32[1,6,12,8,128]{4,3,2,1,0:T(8,128)S(1)}, f32[1,6,12,8,128]{4,3,2,1,0:T(8,128)S(1)}, u32[]{:S(2)}, u32[]{:S(2)}) collective-permute-start(f32[1,6,12,8,128]{4,3,2,1,0:T(8,128)S(1)} %get-tuple-element.23), channel_id=1, source_target_pairs={{1,2},{2,1},{3,4},{4,3},{5,6},{6,5},{9,10},{10,9},{11,12},{12,11},... | collective-permute-start | bytes 884744 | tf_op jit(solution)/shard_map/ppermute | solution.py:538
  7.7 1.3 %collective-permute-start.2 = (f32[1,3,8,8,128]{4,3,2,1,0:T(8,128)S(1)}, f32[1,3,8,8,128]{4,3,2,1,0:T(8,128)S(1)}, u32[]{:S(2)}, u32[]{:S(2)}) collective-permute-start(f32[1,3,8,8,128]{4,3,2,1,0:T(8,128)S(1)} %get-tuple-element.31), channel_id=1, source_target_pairs={{8,0},{16,8},{24,16},{9,1},{17,9},{25,17},{10,2},{18,10},{26,18},{... | collective-permute-start | bytes 294920 | tf_op jit(solution)/shard_map/ppermute | solution.py:539
  9.0 3.0 %collective-permute-start.3 = (f32[1,3,8,8,128]{4,3,2,1,0:T(8,128)S(1)}, f32[1,3,8,8,128]{4,3,2,1,0:T(8,128)S(1)}, u32[]{:S(2)}, u32[]{:S(2)}) collective-permute-start(f32[1,3,8,8,128]{4,3,2,1,0:T(8,128)S(1)} %get-tuple-element.32), channel_id=1, source_target_pairs={{0,8},{8,16},{16,24},{1,9},{9,17},{17,25},{2,10},{10,18},{18,26},{... | collective-permute-start | bytes 294920 | tf_op jit(solution)/shard_map/ppermute | solution.py:540
  12.0 0.1 weights.1
  12.2 0.0 collective-permute-done.2.refs_12_
  12.2 0.8 %collective-permute-done.3.refs_13_ = f32[1,3,8,8,128]{4,3,2,1,0:T(8,128)S(1)} collective-permute-done((f32[1,3,8,8,128]{4,3,2,1,0:T(8,128)S(1)}, f32[1,3,8,8,128]{4,3,2,1,0:T(8,128)S(1)}, u32[]{:S(2)}, u32[]{:S(2)}) %collective-permute-start.3) | collective-permute-done | bytes 98336 | tf_op jit(solution)/shard_map/ppermute | solution.py:540
  13.0 5.5 %collective-permute-done.1.refs_3_ = f32[1,6,12,8,128]{4,3,2,1,0:T(8,128)S(1)} collective-permute-done((f32[1,6,12,8,128]{4,3,2,1,0:T(8,128)S(1)}, f32[1,6,12,8,128]{4,3,2,1,0:T(8,128)S(1)}, u32[]{:S(2)}, u32[]{:S(2)}) %collective-permute-start.1) | collective-permute-done | bytes 294944 | tf_op jit(solution)/shard_map/ppermute | solution.py:526
  18.5 0.0 copy-done.2
  18.5 0.0 copy-done.3
  18.5 0.0 copy-done.1
  18.5 3.1 %early.1 = (f32[6,3,8,8,128]{4,3,2,1,0:T(8,128)S(1)}, f32[6,4,8,8,128]{4,3,2,1,0:T(8,128)S(1)}) custom-call(s32[6]{0:T(128)S(1)} %copy-done.2, f32[4,14]{1,0:T(4,128)S(1)} %copy-done.1, f32[23]{0:T(128)S(1)} %copy-done.3, f32[1,6,12,8,128]{4,3,2,1,0:T(8,128)S(1)} %collective-permute-done.1.refs_3_, ...), custom_call_target="tpu_custom_call" | custom-call | flops 12288000 | bytes 1048576 | tf_op jit(solution)/shard_map/early/pallas_call | solution.py:550
  21.6 0.0 collective-permute-done.refs_2_
  21.6 3.3 %late.1 = f32[3,6,64,128]{3,2,1,0:T(8,128)} custom-call(s32[6]{0:T(128)S(1)} %copy-done.2, f32[4,14]{1,0:T(4,128)S(1)} %copy-done.1, f32[1,6,12,8,128]{4,3,2,1,0:T(8,128)S(1)} %collective-permute-done.refs_2_, f32[6,4,3,6,8,128]{5,4,3,2,1,0:T(8,128)S(1)} %get-tuple-element.20.refs_0_.refs_4_.refs_3_, ...), custom_call_target="tpu_custom_call" | custom-call | flops 10444800 | bytes 1048576 | tf_op jit(solution)/shard_map/late/pallas_call | solution.py:562
Async XLA Ops:
  0.0 18.5 %copy-start.2 = (s32[6]{0:T(128)S(1)}, s32[6]{0:T(128)}, u32[]{:S(2)}) copy-start(s32[6]{0:T(128)} %refs_0_.3) | copy-start | bytes 76
  0.0 18.5 %copy-start.3 = (f32[23]{0:T(128)S(1)}, f32[23]{0:T(128)}, u32[]{:S(2)}) copy-start(f32[23]{0:T(128)} %refs_2_.1) | copy-start | bytes 280
  0.0 1.1 %copy-start = (f32[3,6,8,1024]{3,2,1,0:T(8,128)S(1)}, f32[3,6,8,1024]{3,2,1,0:T(8,128)}, u32[]{:S(2)}) copy-start(f32[3,6,8,1024]{3,2,1,0:T(8,128)} %param.4) | copy-start | bytes 1769476
  1.1 17.4 %copy-start.1 = (f32[4,14]{1,0:T(4,128)S(1)}, f32[4,14]{1,0:T(4,128)}, u32[]{:S(2)}) copy-start(f32[4,14]{1,0:T(4,128)} %refs_1_.3) | copy-start | bytes 676
  2.9 15.6 %collective-permute-start.1 = (f32[1,6,12,8,128]{4,3,2,1,0:T(8,128)S(1)}, f32[1,6,12,8,128]{4,3,2,1,0:T(8,128)S(1)}, u32[]{:S(2)}, u32[]{:S(2)}) collective-permute-start(f32[1,6,12,8,128]{4,3,2,1,0:T(8,128)S(1)} %get-tuple-element.30), channel_id=1, source_target_pairs={{0,1},{1,0},{2,3},{3,2},{4,5},{5,4},{6,7},{7,6},{8,9},{9,8},{10,11... | collective-permute-start | bytes 884744 | tf_op jit(solution)/shard_map/ppermute | solution.py:526
  7.0 14.6 %collective-permute-start = (f32[1,6,12,8,128]{4,3,2,1,0:T(8,128)S(1)}, f32[1,6,12,8,128]{4,3,2,1,0:T(8,128)S(1)}, u32[]{:S(2)}, u32[]{:S(2)}) collective-permute-start(f32[1,6,12,8,128]{4,3,2,1,0:T(8,128)S(1)} %get-tuple-element.23), channel_id=1, source_target_pairs={{1,2},{2,1},{3,4},{4,3},{5,6},{6,5},{9,10},{10,9},{11,12},{12,11},... | collective-permute-start | bytes 884744 | tf_op jit(solution)/shard_map/ppermute | solution.py:538
  7.7 4.5 %collective-permute-start.2 = (f32[1,3,8,8,128]{4,3,2,1,0:T(8,128)S(1)}, f32[1,3,8,8,128]{4,3,2,1,0:T(8,128)S(1)}, u32[]{:S(2)}, u32[]{:S(2)}) collective-permute-start(f32[1,3,8,8,128]{4,3,2,1,0:T(8,128)S(1)} %get-tuple-element.31), channel_id=1, source_target_pairs={{8,0},{16,8},{24,16},{9,1},{17,9},{25,17},{10,2},{18,10},{26,18},{... | collective-permute-start | bytes 294920 | tf_op jit(solution)/shard_map/ppermute | solution.py:539
  9.0 4.0 %collective-permute-start.3 = (f32[1,3,8,8,128]{4,3,2,1,0:T(8,128)S(1)}, f32[1,3,8,8,128]{4,3,2,1,0:T(8,128)S(1)}, u32[]{:S(2)}, u32[]{:S(2)}) collective-permute-start(f32[1,3,8,8,128]{4,3,2,1,0:T(8,128)S(1)} %get-tuple-element.32), channel_id=1, source_target_pairs={{0,8},{8,16},{16,24},{1,9},{9,17},{17,25},{2,10},{10,18},{18,26},{... | collective-permute-start | bytes 294920 | tf_op jit(solution)/shard_map/ppermute | solution.py:540

commit v3 on v2

v3 whole, which is shorter than its diff:
```python
import math

import jax
import jax.numpy as jnp
from jax import lax
from jax.experimental import pallas as pl
from jax.experimental.pallas import tpu as pltpu
from jax.sharding import PartitionSpec as P

bulk_modulus = 40.0
REACH = 3
LANES = 128
VMEM_LIMIT = 24 * 1024 * 1024
EARLY_COST = 2 * 10**9
MIDDLE_COST = 2 * 10**9


def bond_columns():
    halves = []
    for a in range(-REACH, REACH + 1):
        for b in range(-REACH, REACH + 1):
            if 0 < a * a + b * b <= 9 and (a > 0 or (a == 0 and b > 0)):
                halves.append((a, b))
    columns = {}
    for index, (a, b) in enumerate(halves):
        columns[(a, b)] = index
        columns[(-a, -b)] = index
    return columns


COLUMNS = bond_columns()
BONDS = {0: (1, 2, 3), 1: (-2, -1, 0, 1, 2), 2: (-2, -1, 0, 1, 2), 3: (0,)}


def length_of(a, b):
    return math.sqrt(a * a + b * b)


class Plan:
    def __init__(self, cols):
        self.cols = cols
        self.wide = cols + 2 * REACH
        self.own = range(REACH, REACH + cols)
        self.low = range(0, REACH)
        self.high = range(REACH + cols, self.wide)
        self.near_b = range(REACH, 2 * REACH)
        self.near_a = range(cols, cols + REACH)
        every = [
            (b, a, i)
            for b, offsets in BONDS.items()
            for i in range(self.wide)
            for a in offsets
            if 0 <= i + a < self.wide and (i in self.own or i + a in self.own)
        ]
        inner = [k for k in every if k[2] in self.own and k[2] + k[1] in self.own]
        self.inner = inner
        self.inner_a = [k for k in inner if k[2] in self.near_a or k[2] + k[1] in self.near_a]
        self.inner_b = [k for k in inner if k not in self.inner_a]
        self.cross_a = [k for k in every if max(k[2], k[2] + k[1]) in self.high]
        self.cross_b = [k for k in every if min(k[2], k[2] + k[1]) in self.low]
        self.late = [k for k in every if min(k[2], k[2] + k[1]) < 2 * REACH]
        self.early = [k for k in every if k not in self.late]
        self.inner_early = [k for k in self.early if k in inner]
        self.inner_late = [k for k in self.late if k in inner]
        self.inner_start = self.span(self.inner_early).start
        self.start_a = min(min(k[2], k[2] + k[1]) for k in self.inner_a)


    def span(self, keys):
        ends = [x for _, a, i in keys for x in (i, i + a)]
        return range(min(ends), max(ends) + 1)


class Grid:
    def __init__(self, subs):
        self.subs = subs
        self.lane = lax.broadcasted_iota(jnp.int32, (subs, LANES), 1)
        self.y = lax.broadcasted_iota(jnp.int32, (subs, LANES), 0) * LANES + self.lane
        self.total = subs * LANES
        self.exists = {b: self.y < self.total - b for b in range(1, REACH + 1)}

    def ahead(self, row):
        after = pltpu.roll(row, self.subs - 1, axis=0)
        return {
            b: pltpu.roll(jnp.where(self.lane < b, after, row), LANES - b, axis=1) for b in range(1, REACH + 1)
        }

    def back(self, rows):
        total = None
        for b, row in rows.items():
            before = pltpu.roll(row, 1, axis=0)
            moved = pltpu.roll(jnp.where(self.lane >= LANES - b, before, row), b, axis=1)
            total = moved if total is None else total + moved
        return total

    def ring(self, a):
        total = None
        for b in range(-REACH, REACH + 1):
            if 0 < a * a + b * b <= 9:
                exists = (self.y + b >= 0) & (self.y + b < self.total)
                term = jnp.where(exists, length_of(a, b), 0.0)
                total = term if total is None else total + term
        return total


class Store:
    def __init__(self, *parts):
        self.parts = parts

    def at(self, column, *lead):
        for ref, first, columns, head in self.parts:
            if column in columns:
                return ref, (*head, *lead, column - first)
        raise KeyError(column)

    def get(self, column, *lead):
        ref, index = self.at(column, *lead)
        return ref[index]

    def put(self, column, value, *lead):
        ref, index = self.at(column, *lead)
        ref[index] = value


def frame():
    odd = lax.axis_index("tile") % 2 == 1
    return odd, jnp.where(odd, -1.0, 1.0).astype(jnp.float32)


def sides(tiles):
    tile = lax.axis_index("tile")
    has_a = (tile % 2 == 1) | (tile + 1 < tiles)
    has_b = jnp.where(tile % 2 == 1, tile + 1 < tiles, tile > 0)
    return has_a, has_b


def keep_row(grid, rows, column, row):
    for c in range(3):
        rows.put(column, row[c], 0, c)
        for b, moved in grid.ahead(row[c]).items():
            rows.put(column, moved + float(b) if c == 1 else moved, b, c)


def separation(rows, b, a, i, here):
    there = [rows.get(i + a, b, c) for c in range(3)]
    here_x = here[0] - float(a) if a else here[0]
    return there[0] - here_x, there[1] - here[1], there[2] - here[2]


def by_row(keys):
    groups = {}
    for b, a, i in keys:
        groups.setdefault((b, i), []).append(a)
    return groups.items()


def extension_sums(grid, rows, keys, mask_of, keep):
    sums = {}
    shifted = {}
    for (b, i), offsets in by_row(keys):
        here = [rows.get(i, 0, c) for c in range(3)]
        for a in offsets:
            sep = separation(rows, b, a, i, here)
            q = sep[0] * sep[0] + sep[1] * sep[1] + sep[2] * sep[2]
            r = lax.rsqrt(q)
            keep((b, a, i), r)
            e = q * r - length_of(a, b)
            mask = mask_of(b)
            if mask is not None:
                e = jnp.where(mask, e, 0.0)
            sums[i] = sums[i] + e if i in sums else e
            if b == 0:
                sums[i + a] = sums[i + a] + e if i + a in sums else e
            else:
                key = (i + a, b)
                shifted[key] = shifted[key] + e if key in shifted else e
    for x in sorted({x for x, _ in shifted}):
        total = grid.back({b: shifted[(x, b)] for b in range(1, REACH + 1) if (x, b) in shifted})
        sums[x] = sums[x] + total if x in sums else total
    return sums


def chunk_of(plies, most):
    return max(n for n in range(1, most + 1) if plies % n == 0)


def for_plies(plies, most, body):
    count = chunk_of(plies, most)

    def step(n, carry):
        for k in range(count):
            body(n * count + k)
        return carry

    lax.fori_loop(0, plies // count, step, 0)


def pack_kernel(plan, u_ref, rows_ref, message):
    comps, plies, depth, _ = u_ref.shape
    odd, sign = frame()
    for p in range(plies):
        for x in range(plan.cols):
            at = jnp.where(odd, plan.cols - 1 - x, x)
            for c in range(comps):
                row = u_ref[c, p, pl.ds(at, depth // plan.cols, stride=plan.cols), :]
                row = row * sign if c == 0 else row
                rows_ref[p, c, x] = row
                if x + REACH in plan.near_a:
                    message[0, p, c * REACH + x + REACH - plan.near_a.start] = row


def near_a_kernel(plan, base_ref, thin, rows_ref, sums_ref, inverse_ref, first_ref, second_ref):
    plies = base_ref.shape[0]
    grid = Grid(base_ref.shape[-2])
    slots = {key: n for n, key in enumerate(plan.inner_a)}

    def ply(p):
        rows = Store((rows_ref, plan.start_a, range(plan.start_a, plan.own.stop), (p,)))
        for x in rows.parts[0][2]:
            keep_row(grid, rows, x, [base_ref[p, c, x - REACH] for c in range(3)])

        def keep(key, r):
            inverse_ref[p, slots[key]] = r

        sums = extension_sums(grid, rows, plan.inner_a, grid.exists.get, keep)
        for x in rows.parts[0][2]:
            sums_ref[p, x - plan.start_a] = sums[x]
            if x in plan.near_a:
                thin[0, p, x - plan.near_a.start] = sums[x]

    for_plies(plies, 2, ply)
    upper = lax.axis_index("ply") % 2 == 1
    for c in range(3):
        for x in range(plan.cols):
            low, high = base_ref[0, c, x], base_ref[plies - 1, c, x]
            first_ref[0, c, x] = jnp.where(upper, low, high)
            second_ref[0, c, x] = jnp.where(upper, high, low)


def near_b_kernel(
    plan, base_ref, rows_a_ref, sums_a_ref, rows_ref, sums_ref, inverse_ref
):
    plies = rows_a_ref.shape[0]
    grid = Grid(rows_a_ref.shape[-2])
    slots = {key: n for n, key in enumerate(plan.inner_b)}
    fresh = range(REACH, plan.start_a)
    tall = range(plan.start_a, plan.own.stop)

    def ply(p):
        rows = Store((rows_ref, REACH, fresh, (p,)), (rows_a_ref, plan.start_a, tall, (p,)))
        for x in fresh:
            keep_row(grid, rows, x, [base_ref[p, c, x - REACH] for c in range(3)])

        def keep(key, r):
            inverse_ref[p, slots[key]] = r

        sums = extension_sums(grid, rows, plan.inner_b, grid.exists.get, keep)
        for x in range(REACH, plan.near_a.start):
            total = sums[x] + sums_a_ref[p, x - plan.start_a] if x >= plan.start_a else sums[x]
            sums_ref[p, x - REACH] = total

    for_plies(plies, 2, ply)


def weight_kernel(plan, tiles, weight_ref, pair_ref):
    grid = Grid(weight_ref.shape[-2])
    ones = jnp.ones((grid.subs, LANES), jnp.int32)
    has_a, has_b = (ones * side.astype(jnp.int32) > 0 for side in sides(tiles))
    ring = {a: grid.ring(a) for a in range(REACH + 1)}
    weight = {}
    for x in range(plan.wide):
        mass = ring[0]
        for a in range(-REACH, REACH + 1):
            term = ring[abs(a)]
            if x in plan.own and x + a in plan.low:
                term = jnp.where(has_b, term, 0.0)
            if x in plan.own and x + a in plan.high:
                term = jnp.where(has_a, term, 0.0)
            if a:
                mass = mass + term
        weight[x] = 1.0 / mass
        weight_ref[x] = weight[x]
    moved = {x: {0: weight[x], **grid.ahead(weight[x])} for x in range(plan.wide)}
    for n, (b, a, i) in enumerate(plan.early + plan.late):
        pair_ref[n] = weight[i] + moved[i + a][b]


def constants(odd, table_ref, angle):
    found = {}

    def of(a, b):
        if (a, b) not in found:
            column = COLUMNS[(a, b)]
            mirrored = COLUMNS[(-a, b)]
            at = column if column == mirrored else jnp.where(odd, mirrored, column)
            shear = table_ref[angle, at]
            found[(a, b)] = 3.0 * bulk_modulus - 5.0 * shear, 15.0 / length_of(a, b) * shear
        return found[(a, b)]

    return of


def collect(plan, grid, keys, push_of, force):
    held = {}
    last = {}
    for b, a, i in keys:
        last[(i + a, b)] = i
    for (b, i), offsets in by_row(keys):
        mine = None
        for a in offsets:
            j = i + a
            push = push_of((b, a, i))
            if i in plan.own:
                mine = push if mine is None else [mine[c] + push[c] for c in range(3)]
            if j in plan.own:
                held[(j, b)] = [held[(j, b)][c] + push[c] for c in range(3)] if (j, b) in held else push
        if mine is not None:
            force(i, mine)
        for j, _ in [k for k in held if k[1] == b and last[k] == i]:
            total = held.pop((j, b))
            force(j, [-(grid.back({b: total[c]}) if b else total[c]) for c in range(3)])
    assert not held


def whole_push(rows, strains, factors, inverse, pair, mask_of, key):
    b, a, i = key
    alpha, beta = factors(a, b)
    sep = separation(rows, b, a, i, [rows.get(i, 0, c) for c in range(3)])
    r = inverse(key)
    f = (alpha * r) * (strains.get(i, 0) + strains.get(i + a, b)) + (beta * pair(key)) * (1.0 - length_of(a, b) * r)
    mask = mask_of(b)
    if mask is not None:
        f = jnp.where(mask, f, 0.0)
    return [f * sep[c] for c in range(3)]


def inner_kernel(
    plan, keys, angle_ref, table_ref, after_ref, rows_a_ref, rows_b_ref, inverse_a_ref, inverse_b_ref, pair_ref,
    vector_ref, force_ref,
):
    plies = rows_a_ref.shape[0]
    grid = Grid(rows_a_ref.shape[-2])
    odd, _ = frame()
    in_a = {key: n for n, key in enumerate(plan.inner_a)}
    in_b = {key: n for n, key in enumerate(plan.inner_b)}
    in_pair = {key: n for n, key in enumerate(plan.early + plan.late)}
    in_vector = {key: n for n, key in enumerate(keys)}

    def ply(p):
        rows = Store(
            (rows_b_ref, REACH, range(REACH, plan.start_a), (p,)),
            (rows_a_ref, plan.start_a, range(plan.start_a, plan.own.stop), (p,)),
        )
        factors = constants(odd, table_ref, angle_ref[p])
        span = plan.span(keys)
        started = set()
        def push_of(key):
            b, a, i = key
            alpha, beta = factors(a, b)
            sep = separation(rows, b, a, i, [rows.get(i, 0, c) for c in range(3)])
            r = inverse_a_ref[p, in_a[key]] if key in in_a else inverse_b_ref[p, in_b[key]]
            scale = alpha * r
            f = (beta * pair_ref[in_pair[key]]) * (1.0 - length_of(a, b) * r)
            if b:
                scale = jnp.where(grid.exists[b], scale, 0.0)
                f = jnp.where(grid.exists[b], f, 0.0)
            for c in range(3):
                vector_ref[p, in_vector[key], c] = scale * sep[c]
            return [f * sep[c] for c in range(3)]

        def force(x, values):
            for c in range(3):
                at = (p, c, x - span.start)
                force_ref[at] = force_ref[at] + values[c] if x in started else values[c]
            started.add(x)

        collect(plan, grid, keys, push_of, force)
        assert started == set(span)

    for_plies(plies, 2, ply)


def send_kernel(plan, after_ref, inner_ref, base_ref, message):
    for p in range(base_ref.shape[0]):
        for x in range(REACH):
            for c in range(3):
                message[0, p, c * REACH + x] = base_ref[p, c, x]


def early_kernel(
    plan, tiles, slabs, angle_ref, table_ref, stiff_ref, got_ref, thin_ref, rows_a_ref, rows_b_ref, sums_a_ref,
    sums_b_ref, weight_ref, pair_ref, vector_ref, inner_ref, first_ref, second_ref,
    force_ref, strain_ref, thin, halo_ref, cross_ref,
):
    slab = lax.axis_index("ply")
    upper = slab % 2 == 1
    plies = rows_a_ref.shape[0]
    grid = Grid(rows_a_ref.shape[-2])
    odd, _ = frame()
    in_cross = {key: n for n, key in enumerate(plan.cross_a)}
    in_pair = {key: n for n, key in enumerate(plan.early + plan.late)}
    in_vector = {key: n for n, key in enumerate(plan.inner_early)}
    start = 2 * REACH
    has_a = None
    if tiles % 2:
        has_a = jnp.ones((grid.subs, LANES), jnp.int32) * sides(tiles)[0].astype(jnp.int32) > 0

    def cross_mask(b):
        mask = grid.exists.get(b)
        if has_a is None:
            return mask
        return has_a if mask is None else mask & has_a

    def ply(p):
        rows = Store(
            (rows_b_ref, REACH, range(REACH, plan.start_a), (p,)),
            (rows_a_ref, plan.start_a, range(plan.start_a, plan.own.stop), (p,)),
            (halo_ref, plan.high.start, plan.high, ()),
        )
        strains = Store((strain_ref, start, range(start, plan.wide), (p,)))
        factors = constants(odd, table_ref, angle_ref[p])
        for j in range(REACH):
            row = [got_ref[0, p, c * REACH + j] for c in range(3)]
            keep_row(grid, rows, plan.wide - 1 - j, [-row[0], row[1], row[2]])

        def keep(key, r):
            cross_ref[in_cross[key]] = r

        sums = extension_sums(grid, rows, plan.cross_a, cross_mask, keep)
        for x in range(start, plan.wide):
            if x in plan.high:
                total = thin_ref[0, p, plan.wide - 1 - x]
            elif x >= plan.near_a.start:
                total = sums_a_ref[p, x - plan.start_a]
            else:
                total = sums_b_ref[p, x - REACH]
            if x in sums:
                total = total + sums[x]
            strain = 3.0 * total * (weight_ref[x] * weight_ref[x])
            strains.put(x, strain, 0)
            for b, moved in grid.ahead(strain).items():
                strains.put(x, moved, b)

        layers = slabs * plies
        layer = slab * plies + p
        up = jnp.where(layer < layers - 1, stiff_ref[jnp.minimum(layer, layers - 2)], 0.0)
        down = jnp.where(layer > 0, stiff_ref[jnp.maximum(layer - 1, 0)], 0.0)
        over = Store(*((r, s, cs, (jnp.minimum(p + 1, plies - 1),)) for r, s, cs, _ in rows.parts[:2]))
        under = Store(*((r, s, cs, (jnp.maximum(p - 1, 0),)) for r, s, cs, _ in rows.parts[:2]))
        for x in plan.own:
            for c in range(3):
                here = rows.get(x, 0, c)
                first, second = first_ref[0, c, x - REACH], second_ref[0, c, x - REACH]
                above = jnp.where(p == plies - 1, jnp.where(upper, second, first), over.get(x, 0, c))
                below = jnp.where(p == 0, jnp.where(upper, first, second), under.get(x, 0, c))
                spring = up * (above - here) + down * (below - here)
                start_at = plan.inner_start
                force_ref[p, c, x - REACH] = inner_ref[p, c, x - start_at] + spring if x >= start_at else spring

        def push_of(key):
            if key in in_cross:
                return whole_push(
                    rows, strains, factors, lambda k: cross_ref[in_cross[k]], lambda k: pair_ref[in_pair[k]],
                    cross_mask, key,
                )
            b, a, i = key
            total = strains.get(i, 0) + strains.get(i + a, b)
            return [vector_ref[p, in_vector[key], c] * total for c in range(3)]

        def force(x, values):
            for c in range(3):
                force_ref[p, c, x - REACH] = force_ref[p, c, x - REACH] + values[c]

        collect(plan, grid, plan.early, push_of, force)
        for x in range(REACH):
            thin[0, p, x] = sums_b_ref[p, x]

    for_plies(plies, 2, ply)


def middle_kernel(
    plan, tiles, angle_ref, table_ref, got_ref, rows_a_ref, rows_b_ref, sums_b_ref,
    weight_ref, pair_ref, vector_ref, inner_ref, force_in_ref, strain_a_ref,
    force_ref, cross_ref, sums_ref, halo_ref, inverse_ref, strain_ref,
):
    plies = rows_a_ref.shape[0]
    grid = Grid(rows_a_ref.shape[-2])
    odd, _ = frame()
    in_cross = {key: n for n, key in enumerate(plan.cross_b)}
    in_pair = {key: n for n, key in enumerate(plan.early + plan.late)}
    in_vector = {key: n for n, key in enumerate(plan.inner_late)}
    start = 2 * REACH
    has_b = jnp.ones((grid.subs, LANES), jnp.int32) * sides(tiles)[1].astype(jnp.int32) > 0
    cross_masks = {b: grid.exists[b] & has_b if b else has_b for b in range(REACH + 1)}
    late = plan.span(plan.inner_late)

    def ply(p):
        rows = Store(
            (halo_ref, 0, plan.low, ()),
            (rows_b_ref, REACH, range(REACH, plan.start_a), (p,)),
            (rows_a_ref, plan.start_a, range(plan.start_a, plan.own.stop), (p,)),
        )
        strains = Store(
            (strain_ref, REACH, plan.near_b, ()), (strain_a_ref, start, range(start, plan.wide), (p,))
        )
        factors = constants(odd, table_ref, angle_ref[p])
        for j in range(REACH):
            row = [got_ref[0, p, c * REACH + j] for c in range(3)]
            keep_row(grid, rows, REACH - 1 - j, [-row[0], row[1], row[2]])

        def keep(key, r):
            inverse_ref[in_cross[key]] = r

        sums = extension_sums(grid, rows, plan.cross_b, cross_masks.get, keep)
        for x in plan.low:
            sums_ref[p, x] = sums[x]
        for x in plan.near_b:
            strain = 3.0 * (sums_b_ref[p, x - REACH] + sums[x]) * (weight_ref[x] * weight_ref[x])
            strains.put(x, strain, 0)
            for b, moved in grid.ahead(strain).items():
                strains.put(x, moved, b)
        for c in range(3):
            for x in plan.own:
                value = force_in_ref[p, c, x - REACH]
                force_ref[p, c, x - REACH] = value + inner_ref[p, c, x - REACH] if x in late else value

        def push_of(key):
            b, a, i = key
            if key not in in_cross:
                total = strains.get(i, 0) + strains.get(i + a, b)
                return [vector_ref[p, in_vector[key], c] * total for c in range(3)]
            alpha, beta = factors(a, b)
            sep = separation(rows, b, a, i, [rows.get(i, 0, c) for c in range(3)])
            r = inverse_ref[in_cross[key]]
            scale = jnp.where(cross_masks[b], alpha * r, 0.0)
            rest = (beta * pair_ref[in_pair[key]]) * (1.0 - length_of(a, b) * r)
            known = strains.get(i, 0) if i in plan.own else strains.get(i + a, b)
            f = scale * known + jnp.where(cross_masks[b], rest, 0.0)
            for c in range(3):
                cross_ref[p, in_cross[key], c] = scale * sep[c]
            return [f * sep[c] for c in range(3)]

        def force(x, values):
            for c in range(3):
                force_ref[p, c, x - REACH] = force_ref[p, c, x - REACH] + values[c]

        collect(plan, grid, plan.late, push_of, force)

    for_plies(plies, 2, ply)


def last_kernel(plan, thin_ref, sums_ref, weight_ref, cross_ref, force_in_ref, out_hbm, out_ref, sems):
    plies = force_in_ref.shape[0]
    grid = Grid(force_in_ref.shape[-2])
    odd, sign = frame()
    in_cross = {key: n for n, key in enumerate(plan.cross_b)}

    def copy_out(p):
        return pltpu.make_async_copy(out_ref.at[:, pl.ds(p, 1)], out_hbm.at[:, pl.ds(p, 1)], sems.at[p])

    def ply(p):
        strains = {}
        for x in plan.low:
            strain = 3.0 * (thin_ref[0, p, REACH - 1 - x] + sums_ref[p, x]) * (weight_ref[x] * weight_ref[x])
            strains[x] = {0: strain, **grid.ahead(strain)}
        found = {x: [force_in_ref[p, c, x - REACH] for c in range(3)] for x in plan.own}

        def push_of(key):
            b, a, i = key
            strain = strains[i][0] if i in plan.low else strains[i + a][b]
            return [cross_ref[p, in_cross[key], c] * strain for c in range(3)]

        def force(x, values):
            found[x] = [found[x][c] + values[c] for c in range(3)]

        collect(plan, grid, plan.cross_b, push_of, force)
        for x in plan.own:
            at = jnp.where(odd, plan.cols - 1 - (x - REACH), x - REACH)
            for c in range(3):
                value = found[x][c] * sign if c == 0 else found[x][c]
                out_ref[c, p, pl.ds(at, grid.subs, stride=plan.cols), :] = value

    count = chunk_of(plies, 2)

    def step(n, carry):
        for k in range(count):
            ply(n * count + k)
        for k in range(count):
            copy_out(n * count + k).start()
        return carry

    lax.fori_loop(0, plies // count, step, 0)
    for p in range(plies):
        copy_out(p).wait()


def local(displacement, angle_index, bond_table, interface_stiffness):
    comps, plies, cols, length = displacement.shape
    subs = length // LANES
    tiles = lax.axis_size("tile")
    slabs = lax.axis_size("ply")
    assert length % LANES == 0 and cols >= 2 * REACH
    plan = Plan(cols)
    view = (
        displacement.reshape(comps, plies, cols, subs, LANES)
        .transpose(0, 1, 3, 2, 4)
        .reshape(comps, plies, subs * cols, LANES)
    )
    whole = pl.BlockSpec(memory_space=pltpu.VMEM)
    scalars = pl.BlockSpec(memory_space=pltpu.SMEM)

    def array(*shape):
        return jax.ShapeDtypeStruct((*shape, subs, LANES), jnp.float32)

    def scratch(*shape):
        return pltpu.VMEM((*shape, subs, LANES), jnp.float32)

    def call(body, name, ins, outs, out_specs=None, scratches=(), cost=1):
        return pl.pallas_call(
            body,
            out_shape=outs,
            in_specs=ins,
            out_specs=out_specs or [whole] * len(outs),
            scratch_shapes=list(scratches),
            compiler_params=pltpu.CompilerParams(vmem_limit_bytes=VMEM_LIMIT),
            cost_estimate=pl.CostEstimate(flops=cost, bytes_accessed=1, transcendentals=0),
            name=name,
        )

    swap_a = [(i, i ^ 1) for i in range(tiles) if (i ^ 1) < tiles]
    swap_b = []
    for slab in range(slabs):
        for tile in range(tiles):
            other = tile + 1 if tile % 2 else tile - 1
            if 0 <= other < tiles:
                swap_b.append((slab * tiles + tile, slab * tiles + other))
            elif (slab ^ 1) < slabs:
                swap_b.append((slab * tiles + tile, (slab ^ 1) * tiles + tile))
    swap_first = [(i, i ^ 1) for i in range(slabs) if (i ^ 1) < slabs]
    swap_second = [(i, j) for k in range(1, slabs - 1, 2) for i, j in ((k, k + 1), (k + 1, k))]
    if slabs % 2 == 0:
        swap_second += [(0, slabs - 1), (slabs - 1, 0)]
    tall = plan.own.stop - plan.start_a
    short = plan.start_a - REACH

    base, message_a = call(
        lambda *refs: pack_kernel(plan, *refs),
        "pack",
        [whole],
        [array(plies, 3, cols), array(1, plies, 3 * REACH)],
    )(view)
    got_a = lax.ppermute(message_a, "tile", swap_a)

    thin_a, rows_a, sums_a, inverse_a, first, second = call(
        lambda *refs: near_a_kernel(plan, *refs),
        "near_a",
        [whole],
        [
            array(1, plies, REACH), array(plies, REACH + 1, 3, tall), array(plies, tall),
            array(plies, len(plan.inner_a)), array(1, 3, cols), array(1, 3, cols),
        ],
    )(base)
    got_thin_a = lax.ppermute(thin_a, "tile", swap_a)
    got_first = lax.ppermute(first, "ply", swap_first)
    got_second = lax.ppermute(second, "ply", swap_second)

    rows_b, sums_b, inverse_b = call(
        lambda *refs: near_b_kernel(plan, *refs),
        "near_b",
        [whole] * 3,
        [
            array(plies, REACH + 1, 3, short), array(plies, plan.near_a.start - REACH),
            array(plies, len(plan.inner_b)),
        ],
    )(base, rows_a, sums_a)

    weight, pair = call(
        lambda *refs: weight_kernel(plan, tiles, *refs),
        "weights",
        [],
        [array(plan.wide), array(len(plan.early) + len(plan.late))],
    )()

    def inner_part(keys, name, after):
        return call(
            lambda *refs: inner_kernel(plan, keys, *refs),
            name,
            [scalars] * 2 + [whole] * 6,
            [array(plies, len(keys), 3), array(plies, 3, len(plan.span(keys)))],
        )(angle_index, bond_table, after, rows_a, rows_b, inverse_a, inverse_b, pair)

    vector_late, inner_late = inner_part(plan.inner_late, "inner_late", got_first)
    (message_b,) = call(
        lambda *refs: send_kernel(plan, *refs),
        "send",
        [whole] * 3,
        [array(1, plies, 3 * REACH)],
    )(got_a, inner_late, base)
    got_b = lax.ppermute(message_b, ("ply", "tile"), swap_b)
    vector_early, inner_early = inner_part(plan.inner_early, "inner_early", message_b)

    force, strain, thin_b = call(
        lambda *refs: early_kernel(plan, tiles, slabs, *refs),
        "early",
        [scalars] * 3 + [whole] * 12,
        [array(plies, 3, cols), array(plies, REACH + 1, plan.wide - 2 * REACH), array(1, plies, REACH)],
        cost=EARLY_COST,
        scratches=[scratch(REACH + 1, 3, REACH), scratch(len(plan.cross_a))],
    )(
        angle_index, bond_table, interface_stiffness, got_a, got_thin_a, rows_a, rows_b, sums_a, sums_b,
        weight, pair, vector_early, inner_early, got_first, got_second,
    )
    got_thin_b = lax.ppermute(thin_b, ("ply", "tile"), swap_b)

    force, cross, sums_low = call(
        lambda *refs: middle_kernel(plan, tiles, *refs),
        "middle",
        [scalars] * 2 + [whole] * 10,
        [array(plies, 3, cols), array(plies, len(plan.cross_b), 3), array(plies, REACH)],
        cost=MIDDLE_COST,
        scratches=[scratch(REACH + 1, 3, REACH), scratch(len(plan.cross_b)), scratch(REACH + 1, REACH)],
    )(angle_index, bond_table, got_b, rows_a, rows_b, sums_b, weight, pair, vector_late, inner_late, force, strain)

    (out,) = call(
        lambda *refs: last_kernel(plan, *refs),
        "last",
        [whole] * 5,
        [jax.ShapeDtypeStruct(view.shape, jnp.float32)],
        out_specs=[pl.BlockSpec(memory_space=pltpu.HBM)],
        scratches=[pltpu.VMEM(view.shape, jnp.float32), pltpu.SemaphoreType.DMA((plies,))],
    )(got_thin_b, sums_low, weight, cross, force)
    return (
        out.reshape(comps, plies, subs, cols, LANES)
        .transpose(0, 1, 3, 2, 4)
        .reshape(comps, plies, cols, length)
    )


def solution(mesh):
    placed = (P(None, "ply", "tile", None), P("ply"), P(), P())
    return jax.shard_map(
        local, mesh=mesh, in_specs=placed, out_specs=P(None, "ply", "tile", None), check_vma=False
    )
```

time: 25.1 us -> 21.4 us (0.85)
  the two profiles are of different devices: /device:TPU:0 before, /device:TPU:8 now
where the time goes in v3:
time: 21.4 us; the launch traced here: 21.1 us
  Pallas kernels  10.6 us (50%)
  starting transfers between devices  6.82 us (32%)
  waiting for transfers between devices  2.44 us (11%)
  local copies, waits for them, and re-layouts  1.08 us (5%)
    pallas_call x2, Pallas kernels, inner_part(): call(lambda *refs: inner_kernel(plan, keys, *refs), name, [scalars] * 2 +...  3.47 us
    pallas_call x1, Pallas kernels, local(): call(lambda *refs: early_kernel(plan, tiles, slabs, *refs), 'early', [sca...  2.09 us
    ppermute x1, starting transfers between devices, local(): got_b = lax.ppermute(message_b, ('ply', 'tile'), swap_b)  2 us
    pallas_call x1, Pallas kernels, local(): call(lambda *refs: middle_kernel(plan, tiles, *refs), 'middle', [scalars]...  1.84 us
    ppermute x1, starting transfers between devices, local(): got_second = lax.ppermute(second, 'ply', swap_second)  1.61 us
    ppermute x1, starting transfers between devices, local(): got_a = lax.ppermute(message_a, 'tile', swap_a)  1.58 us
    ppermute x1, waiting for transfers between devices, local(): got_thin_b = lax.ppermute(thin_b, ('ply', 'tile'), swap_b)  1.35 us
    pallas_call x1, Pallas kernels, local(): call(lambda *refs: last_kernel(plan, *refs), 'last', [whole] * 5, [jax.Sh...  1.1 us
  transfers between devices with their start and end apart: 6, of which 2 were waited for; matrix products, arithmetic and copies ran while one was open for 0% of the time, Pallas kernels for 44%

profile of v3, /device:TPU:8, one launch (start us, length us, event | category | flops | bytes accessed | tf_op | source)
XLA Modules:
  0.0 21.1 jit_solution(7893382979387537464)
XLA Ops:
  0.0 0.0 copy-start
  0.0 1.1 %copy-done = f32[3,6,8,1024]{3,2,1,0:T(8,128)S(1)} copy-done((f32[3,6,8,1024]{3,2,1,0:T(8,128)S(1)}, f32[3,6,8,1024]{3,2,1,0:T(8,128)}, u32[]{:S(2)}) %copy-start) | copy-done | bytes 589848
  1.1 0.0 copy-start.1
  1.1 0.0 copy-start.2
  1.1 0.2 pack.1
  1.2 1.6 %collective-permute-start = (f32[1,6,9,8,128]{4,3,2,1,0:T(8,128)S(1)}, f32[1,6,9,8,128]{4,3,2,1,0:T(8,128)S(1)}, u32[]{:S(2)}, u32[]{:S(2)}) collective-permute-start(f32[1,6,9,8,128]{4,3,2,1,0:T(8,128)S(1)} %get-tuple-element.28), channel_id=1, source_target_pairs={{0,1},{1,0},{2,3},{3,2},{4,5},{5,4},{6,7},{7,6},{8,9},{9,8},{10,11... | collective-permute-start | bytes 663560 | tf_op jit(solution)/shard_map/ppermute | solution.py:652
  2.8 1.0 %near_a.1 = (f32[1,6,3,8,128]{4,3,2,1,0:T(8,128)S(1)}, f32[6,4,3,6,8,128]{5,4,3,2,1,0:T(8,128)S(1)}, f32[6,6,8,128]{3,2,1,0:T(8,128)S(1)}, f32[6,42,8,128]{3,2,1...) custom-call(f32[6,3,8,8,128]{4,3,2,1,0:T(8,128)S(1)} %get-tuple-element.29.refs_0_.refs_2_), custom_call_target="tpu_custom_call" | custom-call | flops 1 | bytes 1 | tf_op jit(solution)/shard_map/near_a/pallas_call | solution.py:654
  3.8 0.1 collective-permute-start.2
  3.9 1.6 %collective-permute-start.3 = (f32[1,3,8,8,128]{4,3,2,1,0:T(8,128)S(1)}, f32[1,3,8,8,128]{4,3,2,1,0:T(8,128)S(1)}, u32[]{:S(2)}, u32[]{:S(2)}) collective-permute-start(f32[1,3,8,8,128]{4,3,2,1,0:T(8,128)S(1)} %get-tuple-element.43), channel_id=1, source_target_pairs={{8,16},{16,8},{0,24},{24,0},{9,17},{17,9},{1,25},{25,1},{10,18},{1... | collective-permute-start | bytes 294920 | tf_op jit(solution)/shard_map/ppermute | solution.py:665
  5.5 0.5 %collective-permute-start.1 = (f32[1,6,3,8,128]{4,3,2,1,0:T(8,128)S(1)}, f32[1,6,3,8,128]{4,3,2,1,0:T(8,128)S(1)}, u32[]{:S(2)}, u32[]{:S(2)}) collective-permute-start(f32[1,6,3,8,128]{4,3,2,1,0:T(8,128)S(1)} %get-tuple-element.30), channel_id=1, source_target_pairs={{0,1},{1,0},{2,3},{3,2},{4,5},{5,4},{6,7},{7,6},{8,9},{9,8},{10,11... | collective-permute-start | bytes 221192 | tf_op jit(solution)/shard_map/ppermute | solution.py:663
  6.0 0.1 weights.1
  6.1 0.9 %near_b.1 = (f32[6,4,3,2,8,128]{5,4,3,2,1,0:T(8,128)S(1)}, f32[6,5,8,128]{3,2,1,0:T(8,128)S(1)}, f32[6,52,8,128]{3,2,1,0:T(8,128)S(1)}) custom-call(f32[6,3,8,8,128]{4,3,2,1,0:T(8,128)S(1)} %get-tuple-element.29.refs_0_.refs_2_, f32[6,4,3,6,8,128]{5,4,3,2,1,0:T(8,128)S(1)} %get-tuple-element.31.refs_1_.refs_3_.refs_5_, ...), custom_call_target="tpu_custom_call" | custom-call | flops 1 | bytes 1 | tf_op jit(solution)/shard_map/near_b/pallas_call | solution.py:667
  7.0 0.0 collective-permute-done.2.refs_2_.refs_13_
  7.0 0.0 copy-done.1
  7.0 0.0 copy-done.2
  7.1 1.6 %inner_late.1 = (f32[6,42,3,8,128]{4,3,2,1,0:T(8,128)S(1)}, f32[6,3,6,8,128]{4,3,2,1,0:T(8,128)S(1)}) custom-call(s32[6]{0:T(128)S(1)} %copy-done.2, f32[4,14]{1,0:T(4,128)S(1)} %copy-done.1, f32[1,3,8,8,128]{4,3,2,1,0:T(8,128)S(1)} %collective-permute-done.2.refs_2_.refs_13_, f32[6,4,3,6,8,128]{5,4,3,2,1,0:T(8,128)S(1)} %get-tuple-element.31.refs_1_.refs_3_.refs_5_, ...), custom_call_target="tpu_custom_call" | custom-call | flops 1 | bytes 1 | tf_op jit(solution)/shard_map/inner_late/pallas_call | solution.py:685
  8.7 0.0 collective-permute-done.refs_0_.refs_3_
  8.7 0.0 copy-start.3
  8.7 2.0 %collective-permute-start.5 = (f32[1,6,9,8,128]{4,3,2,1,0:T(8,128)S(1)}, f32[1,6,9,8,128]{4,3,2,1,0:T(8,128)S(1)}, u32[]{:S(2)}, u32[]{:S(2)}) collective-permute-start(f32[1,6,9,8,128]{4,3,2,1,0:T(8,128)S(1)} %send.1.refs_2_), channel_id=1, source_target_pairs={{0,8},{1,2},{2,1},{3,4},{4,3},{5,6},{6,5},{7,15},{8,0},{9,10},{10,... | collective-permute-start | bytes 663560 | tf_op jit(solution)/shard_map/ppermute | solution.py:699
  10.8 1.8 %inner_early.1 = (f32[6,52,3,8,128]{4,3,2,1,0:T(8,128)S(1)}, f32[6,3,5,8,128]{4,3,2,1,0:T(8,128)S(1)}) custom-call(s32[6]{0:T(128)S(1)} %copy-done.2, f32[4,14]{1,0:T(4,128)S(1)} %copy-done.1, f32[1,6,9,8,128]{4,3,2,1,0:T(8,128)S(1)} %send.1.refs_2_, f32[6,4,3,6,8,128]{5,4,3,2,1,0:T(8,128)S(1)} %get-tuple-element.31.refs_1_.refs_3_.refs_5_, ...), custom_call_target="tpu_custom_call" | custom-call | flops 1 | bytes 1 | tf_op jit(solution)/shard_map/inner_early/pallas_call | solution.py:685
  12.6 0.0 collective-permute-done.1.refs_4_
  12.6 0.0 collective-permute-done.3.refs_14_
  12.6 0.0 copy-done.3
  12.6 2.1 %early.1 = (f32[6,3,8,8,128]{4,3,2,1,0:T(8,128)S(1)}, f32[6,4,8,8,128]{4,3,2,1,0:T(8,128)S(1)}, f32[1,6,3,8,128]{4,3,2,1,0:T(8,128)S(1)}) custom-call(s32[6]{0:T(128)S(1)} %copy-done.2, f32[4,14]{1,0:T(4,128)S(1)} %copy-done.1, f32[23]{0:T(128)S(1)} %copy-done.3, f32[1,6,9,8,128]{4,3,2,1,0:T(8,128)S(1)} %collective-permute-done.refs_0_.refs_3_, ...), custom_call_target="tpu_custom_call" | custom-call | flops 2000000000 | bytes 1 | tf_op jit(solution)/shard_map/early/pallas_call | solution.py:702
  14.7 1.1 %collective-permute-start.4 = (f32[1,6,3,8,128]{4,3,2,1,0:T(8,128)S(1)}, f32[1,6,3,8,128]{4,3,2,1,0:T(8,128)S(1)}, u32[]{:S(2)}, u32[]{:S(2)}) collective-permute-start(f32[1,6,3,8,128]{4,3,2,1,0:T(8,128)S(1)} %get-tuple-element.44), channel_id=1, source_target_pairs={{0,8},{1,2},{2,1},{3,4},{4,3},{5,6},{6,5},{7,15},{8,0},{9,10},{10,... | collective-permute-start | bytes 221192 | tf_op jit(solution)/shard_map/ppermute | solution.py:713
  15.8 1.1 %collective-permute-done.5.refs_2_ = f32[1,6,9,8,128]{4,3,2,1,0:T(8,128)S(1)} collective-permute-done((f32[1,6,9,8,128]{4,3,2,1,0:T(8,128)S(1)}, f32[1,6,9,8,128]{4,3,2,1,0:T(8,128)S(1)}, u32[]{:S(2)}, u32[]{:S(2)}) %collective-permute-start.5) | collective-permute-done | bytes 221216 | tf_op jit(solution)/shard_map/ppermute | solution.py:699
  16.8 1.8 %middle.1 = (f32[6,3,8,8,128]{4,3,2,1,0:T(8,128)S(1)}, f32[6,18,3,8,128]{4,3,2,1,0:T(8,128)S(1)}, f32[6,3,8,128]{3,2,1,0:T(8,128)S(1)}) custom-call(s32[6]{0:T(128)S(1)} %copy-done.2, f32[4,14]{1,0:T(4,128)S(1)} %copy-done.1, f32[1,6,9,8,128]{4,3,2,1,0:T(8,128)S(1)} %collective-permute-done.5.refs_2_, ...), custom_call_target="tpu_custom_call" | custom-call | flops 2000000000 | bytes 1 | tf_op jit(solution)/shard_map/middle/pallas_call | solution.py:715
  18.7 1.3 %collective-permute-done.4.refs_0_ = f32[1,6,3,8,128]{4,3,2,1,0:T(8,128)S(1)} collective-permute-done((f32[1,6,3,8,128]{4,3,2,1,0:T(8,128)S(1)}, f32[1,6,3,8,128]{4,3,2,1,0:T(8,128)S(1)}, u32[]{:S(2)}, u32[]{:S(2)}) %collective-permute-start.4) | collective-permute-done | bytes 73760 | tf_op jit(solution)/shard_map/ppermute | solution.py:713
  20.0 1.1 %last.1 = f32[3,6,64,128]{3,2,1,0:T(8,128)} custom-call(f32[1,6,3,8,128]{4,3,2,1,0:T(8,128)S(1)} %collective-permute-done.4.refs_0_, f32[6,3,8,128]{3,2,1,0:T(8,128)S(1)} %get-tuple-element.48.refs_1_, f32[14,8,128]{2,1,0:T(8,128)S(1)} %get-tuple-element.35.refs_9_.refs_6_.refs_2_, f32[6,18,3,8,128]{4,3,2,1,0:T(8,128)S(1)} %get-tuple-element.49.refs_3_, ...), custom_call_target="tpu_custom_call" | custom-call | flops 1 | bytes 1 | tf_op jit(solution)/shard_map/last/pallas_call | solution.py:724
  (1 shorter events, 0.0 us)
Async XLA Ops:
  0.0 1.1 %copy-start = (f32[3,6,8,1024]{3,2,1,0:T(8,128)S(1)}, f32[3,6,8,1024]{3,2,1,0:T(8,128)}, u32[]{:S(2)}) copy-start(f32[3,6,8,1024]{3,2,1,0:T(8,128)} %param.4) | copy-start | bytes 1769476
  1.1 6.0 %copy-start.1 = (f32[4,14]{1,0:T(4,128)S(1)}, f32[4,14]{1,0:T(4,128)}, u32[]{:S(2)}) copy-start(f32[4,14]{1,0:T(4,128)} %refs_1_.7) | copy-start | bytes 676
  1.1 6.0 %copy-start.2 = (s32[6]{0:T(128)S(1)}, s32[6]{0:T(128)}, u32[]{:S(2)}) copy-start(s32[6]{0:T(128)} %refs_0_.7) | copy-start | bytes 76
  1.2 7.5 %collective-permute-start = (f32[1,6,9,8,128]{4,3,2,1,0:T(8,128)S(1)}, f32[1,6,9,8,128]{4,3,2,1,0:T(8,128)S(1)}, u32[]{:S(2)}, u32[]{:S(2)}) collective-permute-start(f32[1,6,9,8,128]{4,3,2,1,0:T(8,128)S(1)} %get-tuple-element.28), channel_id=1, source_target_pairs={{0,1},{1,0},{2,3},{3,2},{4,5},{5,4},{6,7},{7,6},{8,9},{9,8},{10,11... | collective-permute-start | bytes 663560 | tf_op jit(solution)/shard_map/ppermute | solution.py:652
  3.8 3.2 %collective-permute-start.2 = (f32[1,3,8,8,128]{4,3,2,1,0:T(8,128)S(1)}, f32[1,3,8,8,128]{4,3,2,1,0:T(8,128)S(1)}, u32[]{:S(2)}, u32[]{:S(2)}) collective-permute-start(f32[1,3,8,8,128]{4,3,2,1,0:T(8,128)S(1)} %get-tuple-element.37), channel_id=1, source_target_pairs={{0,8},{8,0},{16,24},{24,16},{1,9},{9,1},{17,25},{25,17},{2,10},{10... | collective-permute-start | bytes 294920 | tf_op jit(solution)/shard_map/ppermute | solution.py:664
  3.9 8.7 %collective-permute-start.3 = (f32[1,3,8,8,128]{4,3,2,1,0:T(8,128)S(1)}, f32[1,3,8,8,128]{4,3,2,1,0:T(8,128)S(1)}, u32[]{:S(2)}, u32[]{:S(2)}) collective-permute-start(f32[1,3,8,8,128]{4,3,2,1,0:T(8,128)S(1)} %get-tuple-element.43), channel_id=1, source_target_pairs={{8,16},{16,8},{0,24},{24,0},{9,17},{17,9},{1,25},{25,1},{10,18},{1... | collective-permute-start | bytes 294920 | tf_op jit(solution)/shard_map/ppermute | solution.py:665
  5.5 7.1 %collective-permute-start.1 = (f32[1,6,3,8,128]{4,3,2,1,0:T(8,128)S(1)}, f32[1,6,3,8,128]{4,3,2,1,0:T(8,128)S(1)}, u32[]{:S(2)}, u32[]{:S(2)}) collective-permute-start(f32[1,6,3,8,128]{4,3,2,1,0:T(8,128)S(1)} %get-tuple-element.30), channel_id=1, source_target_pairs={{0,1},{1,0},{2,3},{3,2},{4,5},{5,4},{6,7},{7,6},{8,9},{9,8},{10,11... | collective-permute-start | bytes 221192 | tf_op jit(solution)/shard_map/ppermute | solution.py:663
  8.7 3.9 %copy-start.3 = (f32[23]{0:T(128)S(1)}, f32[23]{0:T(128)}, u32[]{:S(2)}) copy-start(f32[23]{0:T(128)} %refs_2_.1) | copy-start | bytes 280
  8.7 8.1 %collective-permute-start.5 = (f32[1,6,9,8,128]{4,3,2,1,0:T(8,128)S(1)}, f32[1,6,9,8,128]{4,3,2,1,0:T(8,128)S(1)}, u32[]{:S(2)}, u32[]{:S(2)}) collective-permute-start(f32[1,6,9,8,128]{4,3,2,1,0:T(8,128)S(1)} %send.1.refs_2_), channel_id=1, source_target_pairs={{0,8},{1,2},{2,1},{3,4},{4,3},{5,6},{6,5},{7,15},{8,0},{9,10},{10,... | collective-permute-start | bytes 663560 | tf_op jit(solution)/shard_map/ppermute | solution.py:699
  14.7 5.3 %collective-permute-start.4 = (f32[1,6,3,8,128]{4,3,2,1,0:T(8,128)S(1)}, f32[1,6,3,8,128]{4,3,2,1,0:T(8,128)S(1)}, u32[]{:S(2)}, u32[]{:S(2)}) collective-permute-start(f32[1,6,3,8,128]{4,3,2,1,0:T(8,128)S(1)} %get-tuple-element.44), channel_id=1, source_target_pairs={{0,8},{1,2},{2,1},{3,4},{4,3},{5,6},{6,5},{7,15},{8,0},{9,10},{10,... | collective-permute-start | bytes 221192 | tf_op jit(solution)/shard_map/ppermute | solution.py:713

commit v4 on v3

--- a/solution.py
+++ b/solution.py
@@ -12,7 +12,7 @@
 LANES = 128
 VMEM_LIMIT = 24 * 1024 * 1024
 EARLY_COST = 2 * 10**9
-MIDDLE_COST = 2 * 10**9
+LATE_COST = 2 * 10**9
 
 
 def bond_columns():
@@ -30,6 +30,9 @@
 
 COLUMNS = bond_columns()
 BONDS = {0: (1, 2, 3), 1: (-2, -1, 0, 1, 2), 2: (-2, -1, 0, 1, 2), 3: (0,)}
+
+
+OFFSETS = [(a, b) for b, offsets in BONDS.items() for a in offsets]
 
 
 def length_of(a, b):
@@ -205,11 +208,11 @@
                 row = u_ref[c, p, pl.ds(at, depth // plan.cols, stride=plan.cols), :]
                 row = row * sign if c == 0 else row
                 rows_ref[p, c, x] = row
-                if x + REACH in plan.near_a:
+                if x + REACH in plan.near_a and c < 2:
                     message[0, p, c * REACH + x + REACH - plan.near_a.start] = row
 
 
-def near_a_kernel(plan, base_ref, thin, rows_ref, sums_ref, inverse_ref, first_ref, second_ref):
+def near_a_kernel(plan, base_ref, message, rows_ref, sums_ref, inverse_ref, first_ref, second_ref):
     plies = base_ref.shape[0]
     grid = Grid(base_ref.shape[-2])
     slots = {key: n for n, key in enumerate(plan.inner_a)}
@@ -226,7 +229,8 @@
         for x in rows.parts[0][2]:
             sums_ref[p, x - plan.start_a] = sums[x]
             if x in plan.near_a:
-                thin[0, p, x - plan.near_a.start] = sums[x]
+                message[0, p, x - plan.near_a.start] = base_ref[p, 2, x - REACH]
+                message[0, p, REACH + x - plan.near_a.start] = sums[x]
 
     for_plies(plies, 2, ply)
     upper = lax.axis_index("ply") % 2 == 1
@@ -262,7 +266,31 @@
     for_plies(plies, 2, ply)
 
 
-def weight_kernel(plan, tiles, weight_ref, pair_ref):
+def weight_kernel(
+    plan, tiles, slabs, angle_ref, table_ref, stiff_ref, after_ref, weight_ref, pair_ref, factor_ref, spring_ref
+):
+    plies = factor_ref.shape[0]
+    odd, _ = frame()
+    slab = lax.axis_index("ply")
+    layers = slabs * plies
+
+    def fill(ref, at, value):
+        ref[at] = jnp.full(ref.shape[-2:], value, jnp.float32)
+
+    for p in range(plies):
+        for n, (a, b) in enumerate(OFFSETS):
+            column = COLUMNS[(a, b)]
+            mirrored = COLUMNS[(-a, b)]
+            shear = table_ref[angle_ref[p], column if column == mirrored else jnp.where(odd, mirrored, column)]
+            fill(factor_ref, (p, 2 * n), 3.0 * bulk_modulus - 5.0 * shear)
+            fill(factor_ref, (p, 2 * n + 1), 15.0 / length_of(a, b) * shear)
+        layer = slab * plies + p
+        up = jnp.where(layer < layers - 1, stiff_ref[jnp.minimum(layer, layers - 2)], 0.0)
+        down = jnp.where(layer > 0, stiff_ref[jnp.maximum(layer - 1, 0)], 0.0)
+        fill(spring_ref, (p, 0), up)
+        fill(spring_ref, (p, 1), down)
+        fill(spring_ref, (p, 2), up if p < plies - 1 else 0.0)
+        fill(spring_ref, (p, 3), down if p > 0 else 0.0)
     grid = Grid(weight_ref.shape[-2])
     ones = jnp.ones((grid.subs, LANES), jnp.int32)
     has_a, has_b = (ones * side.astype(jnp.int32) > 0 for side in sides(tiles))
@@ -285,17 +313,10 @@
         pair_ref[n] = weight[i] + moved[i + a][b]
 
 
-def constants(odd, table_ref, angle):
-    found = {}
-
+def factors_of(factor_ref, p):
     def of(a, b):
-        if (a, b) not in found:
-            column = COLUMNS[(a, b)]
-            mirrored = COLUMNS[(-a, b)]
-            at = column if column == mirrored else jnp.where(odd, mirrored, column)
-            shear = table_ref[angle, at]
-            found[(a, b)] = 3.0 * bulk_modulus - 5.0 * shear, 15.0 / length_of(a, b) * shear
-        return found[(a, b)]
+        n = OFFSETS.index((a, b))
+        return factor_ref[p, 2 * n], factor_ref[p, 2 * n + 1]
 
     return of
 
@@ -335,12 +356,11 @@
 
 
 def inner_kernel(
-    plan, keys, angle_ref, table_ref, after_ref, rows_a_ref, rows_b_ref, inverse_a_ref, inverse_b_ref, pair_ref,
-    vector_ref, force_ref,
+    plan, after_ref, factor_ref, rows_a_ref, rows_b_ref, inverse_a_ref, inverse_b_ref, pair_ref, vector_ref, force_ref
 ):
+    keys = plan.inner_late
     plies = rows_a_ref.shape[0]
     grid = Grid(rows_a_ref.shape[-2])
-    odd, _ = frame()
     in_a = {key: n for n, key in enumerate(plan.inner_a)}
     in_b = {key: n for n, key in enumerate(plan.inner_b)}
     in_pair = {key: n for n, key in enumerate(plan.early + plan.late)}
@@ -351,7 +371,7 @@
             (rows_b_ref, REACH, range(REACH, plan.start_a), (p,)),
             (rows_a_ref, plan.start_a, range(plan.start_a, plan.own.stop), (p,)),
         )
-        factors = constants(odd, table_ref, angle_ref[p])
+        factors = factors_of(factor_ref, p)
         span = plan.span(keys)
         started = set()
         def push_of(key):
@@ -380,56 +400,42 @@
     for_plies(plies, 2, ply)
 
 
-def send_kernel(plan, after_ref, inner_ref, base_ref, message):
-    for p in range(base_ref.shape[0]):
+def send_kernel(plan, part, after_ref, base_ref, sums_b_ref, message):
+    for p in part:
         for x in range(REACH):
+            message[0, p - part.start, 3 * REACH + x] = sums_b_ref[p, x]
             for c in range(3):
-                message[0, p, c * REACH + x] = base_ref[p, c, x]
-
-
-def early_kernel(
-    plan, tiles, slabs, angle_ref, table_ref, stiff_ref, got_ref, thin_ref, rows_a_ref, rows_b_ref, sums_a_ref,
-    sums_b_ref, weight_ref, pair_ref, vector_ref, inner_ref, first_ref, second_ref,
-    force_ref, strain_ref, thin, halo_ref, cross_ref,
+                message[0, p - part.start, c * REACH + x] = base_ref[p, c, x]
+
+
+def strain_kernel(
+    plan, tiles, after_ref, got_ref, got_more_ref, rows_a_ref, rows_b_ref, sums_a_ref, sums_b_ref, weight_ref,
+    halo_ref, strain_ref, inverse_ref,
 ):
-    slab = lax.axis_index("ply")
-    upper = slab % 2 == 1
     plies = rows_a_ref.shape[0]
     grid = Grid(rows_a_ref.shape[-2])
-    odd, _ = frame()
     in_cross = {key: n for n, key in enumerate(plan.cross_a)}
-    in_pair = {key: n for n, key in enumerate(plan.early + plan.late)}
-    in_vector = {key: n for n, key in enumerate(plan.inner_early)}
     start = 2 * REACH
-    has_a = None
-    if tiles % 2:
-        has_a = jnp.ones((grid.subs, LANES), jnp.int32) * sides(tiles)[0].astype(jnp.int32) > 0
-
-    def cross_mask(b):
-        mask = grid.exists.get(b)
-        if has_a is None:
-            return mask
-        return has_a if mask is None else mask & has_a
+    mask_of = cross_mask_a(grid, tiles)
 
     def ply(p):
         rows = Store(
             (rows_b_ref, REACH, range(REACH, plan.start_a), (p,)),
             (rows_a_ref, plan.start_a, range(plan.start_a, plan.own.stop), (p,)),
-            (halo_ref, plan.high.start, plan.high, ()),
+            (halo_ref, plan.high.start, plan.high, (p,)),
         )
         strains = Store((strain_ref, start, range(start, plan.wide), (p,)))
-        factors = constants(odd, table_ref, angle_ref[p])
         for j in range(REACH):
-            row = [got_ref[0, p, c * REACH + j] for c in range(3)]
+            row = [got_ref[0, p, j], got_ref[0, p, REACH + j], got_more_ref[0, p, j]]
             keep_row(grid, rows, plan.wide - 1 - j, [-row[0], row[1], row[2]])
 
         def keep(key, r):
-            cross_ref[in_cross[key]] = r
-
-        sums = extension_sums(grid, rows, plan.cross_a, cross_mask, keep)
+            inverse_ref[p, in_cross[key]] = r
+
+        sums = extension_sums(grid, rows, plan.cross_a, mask_of, keep)
         for x in range(start, plan.wide):
             if x in plan.high:
-                total = thin_ref[0, p, plan.wide - 1 - x]
+                total = got_more_ref[0, p, REACH + plan.wide - 1 - x]
             elif x >= plan.near_a.start:
                 total = sums_a_ref[p, x - plan.start_a]
             else:
@@ -441,51 +447,80 @@
             for b, moved in grid.ahead(strain).items():
                 strains.put(x, moved, b)
 
-        layers = slabs * plies
-        layer = slab * plies + p
-        up = jnp.where(layer < layers - 1, stiff_ref[jnp.minimum(layer, layers - 2)], 0.0)
-        down = jnp.where(layer > 0, stiff_ref[jnp.maximum(layer - 1, 0)], 0.0)
-        over = Store(*((r, s, cs, (jnp.minimum(p + 1, plies - 1),)) for r, s, cs, _ in rows.parts[:2]))
-        under = Store(*((r, s, cs, (jnp.maximum(p - 1, 0),)) for r, s, cs, _ in rows.parts[:2]))
+    for_plies(plies, 2, ply)
+
+
+def cross_mask_a(grid, tiles):
+    if tiles % 2 == 0:
+        return grid.exists.get
+    has_a = jnp.ones((grid.subs, LANES), jnp.int32) * sides(tiles)[0].astype(jnp.int32) > 0
+    return {b: grid.exists[b] & has_a if b else has_a for b in range(REACH + 1)}.get
+
+
+def early_kernel(
+    plan, tiles, rows_a_ref, rows_b_ref, halo_ref, strain_ref, inverse_ref, inverse_a_ref, inverse_b_ref, pair_ref,
+    factor_ref, spring_ref, force_ref,
+):
+    plies = rows_a_ref.shape[0]
+    grid = Grid(rows_a_ref.shape[-2])
+    in_a = {key: n for n, key in enumerate(plan.inner_a)}
+    in_b = {key: n for n, key in enumerate(plan.inner_b)}
+    in_cross = {key: n for n, key in enumerate(plan.cross_a)}
+    in_pair = {key: n for n, key in enumerate(plan.early + plan.late)}
+    start = 2 * REACH
+    cross_mask = cross_mask_a(grid, tiles)
+
+    def ply(p):
+        def rows_of(q, *more):
+            return Store(
+                (rows_b_ref, REACH, range(REACH, plan.start_a), (q,)),
+                (rows_a_ref, plan.start_a, range(plan.start_a, plan.own.stop), (q,)),
+                *more,
+            )
+
+        rows = rows_of(p, (halo_ref, plan.high.start, plan.high, (p,)))
+        strains = Store((strain_ref, start, range(start, plan.wide), (p,)))
+        factors = factors_of(factor_ref, p)
+        up, down = spring_ref[p, 2], spring_ref[p, 3]
+        over, under = rows_of(jnp.minimum(p + 1, plies - 1)), rows_of(jnp.maximum(p - 1, 0))
         for x in plan.own:
             for c in range(3):
                 here = rows.get(x, 0, c)
-                first, second = first_ref[0, c, x - REACH], second_ref[0, c, x - REACH]
-                above = jnp.where(p == plies - 1, jnp.where(upper, second, first), over.get(x, 0, c))
-                below = jnp.where(p == 0, jnp.where(upper, first, second), under.get(x, 0, c))
-                spring = up * (above - here) + down * (below - here)
-                start_at = plan.inner_start
-                force_ref[p, c, x - REACH] = inner_ref[p, c, x - start_at] + spring if x >= start_at else spring
+                spring = up * (over.get(x, 0, c) - here) + down * (under.get(x, 0, c) - here)
+                force_ref[p, c, x - REACH] = spring
+
+        def inverse(key):
+            if key in in_cross:
+                return inverse_ref[p, in_cross[key]]
+            return inverse_a_ref[p, in_a[key]] if key in in_a else inverse_b_ref[p, in_b[key]]
 
         def push_of(key):
-            if key in in_cross:
-                return whole_push(
-                    rows, strains, factors, lambda k: cross_ref[in_cross[k]], lambda k: pair_ref[in_pair[k]],
-                    cross_mask, key,
-                )
-            b, a, i = key
-            total = strains.get(i, 0) + strains.get(i + a, b)
-            return [vector_ref[p, in_vector[key], c] * total for c in range(3)]
+            mask_of = cross_mask if key in in_cross else grid.exists.get
+            return whole_push(rows, strains, factors, inverse, lambda k: pair_ref[in_pair[k]], mask_of, key)
 
         def force(x, values):
             for c in range(3):
                 force_ref[p, c, x - REACH] = force_ref[p, c, x - REACH] + values[c]
 
         collect(plan, grid, plan.early, push_of, force)
-        for x in range(REACH):
-            thin[0, p, x] = sums_b_ref[p, x]
 
     for_plies(plies, 2, ply)
 
 
-def middle_kernel(
-    plan, tiles, angle_ref, table_ref, got_ref, rows_a_ref, rows_b_ref, sums_b_ref,
-    weight_ref, pair_ref, vector_ref, inner_ref, force_in_ref, strain_a_ref,
-    force_ref, cross_ref, sums_ref, halo_ref, inverse_ref, strain_ref,
+def late_kernel(
+    plan, tiles, part, final, first_ref, second_ref, got_ref, rows_a_ref, rows_b_ref, sums_b_ref, weight_ref, pair_ref,
+    factor_ref, spring_ref, vector_ref, inner_ref, force_in_ref, strain_a_ref, *rest,
 ):
+    if final:
+        before_ref, out_hbm, halo_ref, cross_ref, strain_ref, force_ref, out_ref, sems, before_sem = rest
+        copy_before = pltpu.make_async_copy(before_ref, out_hbm.at[:, pl.ds(0, part.start)], before_sem)
+        copy_before.start()
+    else:
+        out_ref, halo_ref, cross_ref, strain_ref, force_ref = rest
     plies = rows_a_ref.shape[0]
     grid = Grid(rows_a_ref.shape[-2])
-    odd, _ = frame()
+    odd, sign = frame()
+    upper = lax.axis_index("ply") % 2 == 1
     in_cross = {key: n for n, key in enumerate(plan.cross_b)}
     in_pair = {key: n for n, key in enumerate(plan.early + plan.late)}
     in_vector = {key: n for n, key in enumerate(plan.inner_late)}
@@ -494,104 +529,83 @@
     cross_masks = {b: grid.exists[b] & has_b if b else has_b for b in range(REACH + 1)}
     late = plan.span(plan.inner_late)
 
+    def copy_out(p):
+        return pltpu.make_async_copy(
+            out_ref.at[:, pl.ds(p - part.start, 1)], out_hbm.at[:, pl.ds(p, 1)], sems.at[p - part.start]
+        )
+
     def ply(p):
+        n = p - part.start
         rows = Store(
-            (halo_ref, 0, plan.low, ()),
+            (halo_ref, 0, plan.low, (n,)),
             (rows_b_ref, REACH, range(REACH, plan.start_a), (p,)),
             (rows_a_ref, plan.start_a, range(plan.start_a, plan.own.stop), (p,)),
         )
         strains = Store(
-            (strain_ref, REACH, plan.near_b, ()), (strain_a_ref, start, range(start, plan.wide), (p,))
+            (strain_ref, 0, range(start), (n,)), (strain_a_ref, start, range(start, plan.wide), (p,))
         )
-        factors = constants(odd, table_ref, angle_ref[p])
+        factors = factors_of(factor_ref, p)
         for j in range(REACH):
-            row = [got_ref[0, p, c * REACH + j] for c in range(3)]
+            row = [got_ref[0, n, c * REACH + j] for c in range(3)]
             keep_row(grid, rows, REACH - 1 - j, [-row[0], row[1], row[2]])
 
         def keep(key, r):
-            inverse_ref[in_cross[key]] = r
+            cross_ref[n, in_cross[key]] = r
 
         sums = extension_sums(grid, rows, plan.cross_b, cross_masks.get, keep)
-        for x in plan.low:
-            sums_ref[p, x] = sums[x]
-        for x in plan.near_b:
-            strain = 3.0 * (sums_b_ref[p, x - REACH] + sums[x]) * (weight_ref[x] * weight_ref[x])
+        for x in range(start):
+            total = got_ref[0, n, 3 * REACH + REACH - 1 - x] if x in plan.low else sums_b_ref[p, x - REACH]
+            strain = 3.0 * (total + sums[x]) * (weight_ref[x] * weight_ref[x])
             strains.put(x, strain, 0)
             for b, moved in grid.ahead(strain).items():
                 strains.put(x, moved, b)
+        faces = []
+        if p == plies - 1:
+            faces.append((spring_ref[p, 0], second_ref, first_ref))
+        if p == 0:
+            faces.append((spring_ref[p, 1], first_ref, second_ref))
         for c in range(3):
             for x in plan.own:
                 value = force_in_ref[p, c, x - REACH]
-                force_ref[p, c, x - REACH] = value + inner_ref[p, c, x - REACH] if x in late else value
+                if x in late:
+                    value = value + inner_ref[p, c, x - REACH]
+                for factor, one, two in faces:
+                    beyond = jnp.where(upper, one[0, c, x - REACH], two[0, c, x - REACH])
+                    value = value + factor * (beyond - rows.get(x, 0, c))
+                force_ref[n, c, x - REACH] = value
 
         def push_of(key):
+            if key in in_cross:
+                return whole_push(
+                    rows, strains, factors, lambda k: cross_ref[n, in_cross[k]], lambda k: pair_ref[in_pair[k]],
+                    cross_masks.get, key,
+                )
             b, a, i = key
-            if key not in in_cross:
-                total = strains.get(i, 0) + strains.get(i + a, b)
-                return [vector_ref[p, in_vector[key], c] * total for c in range(3)]
-            alpha, beta = factors(a, b)
-            sep = separation(rows, b, a, i, [rows.get(i, 0, c) for c in range(3)])
-            r = inverse_ref[in_cross[key]]
-            scale = jnp.where(cross_masks[b], alpha * r, 0.0)
-            rest = (beta * pair_ref[in_pair[key]]) * (1.0 - length_of(a, b) * r)
-            known = strains.get(i, 0) if i in plan.own else strains.get(i + a, b)
-            f = scale * known + jnp.where(cross_masks[b], rest, 0.0)
-            for c in range(3):
-                cross_ref[p, in_cross[key], c] = scale * sep[c]
-            return [f * sep[c] for c in range(3)]
+            total = strains.get(i, 0) + strains.get(i + a, b)
+            return [vector_ref[p, in_vector[key], c] * total for c in range(3)]
 
         def force(x, values):
             for c in range(3):
-                force_ref[p, c, x - REACH] = force_ref[p, c, x - REACH] + values[c]
+                force_ref[n, c, x - REACH] = force_ref[n, c, x - REACH] + values[c]
 
         collect(plan, grid, plan.late, push_of, force)
-
-    for_plies(plies, 2, ply)
-
-
-def last_kernel(plan, thin_ref, sums_ref, weight_ref, cross_ref, force_in_ref, out_hbm, out_ref, sems):
-    plies = force_in_ref.shape[0]
-    grid = Grid(force_in_ref.shape[-2])
-    odd, sign = frame()
-    in_cross = {key: n for n, key in enumerate(plan.cross_b)}
-
-    def copy_out(p):
-        return pltpu.make_async_copy(out_ref.at[:, pl.ds(p, 1)], out_hbm.at[:, pl.ds(p, 1)], sems.at[p])
-
-    def ply(p):
-        strains = {}
-        for x in plan.low:
-            strain = 3.0 * (thin_ref[0, p, REACH - 1 - x] + sums_ref[p, x]) * (weight_ref[x] * weight_ref[x])
-            strains[x] = {0: strain, **grid.ahead(strain)}
-        found = {x: [force_in_ref[p, c, x - REACH] for c in range(3)] for x in plan.own}
-
-        def push_of(key):
-            b, a, i = key
-            strain = strains[i][0] if i in plan.low else strains[i + a][b]
-            return [cross_ref[p, in_cross[key], c] * strain for c in range(3)]
-
-        def force(x, values):
-            found[x] = [found[x][c] + values[c] for c in range(3)]
-
-        collect(plan, grid, plan.cross_b, push_of, force)
         for x in plan.own:
             at = jnp.where(odd, plan.cols - 1 - (x - REACH), x - REACH)
             for c in range(3):
-                value = found[x][c] * sign if c == 0 else found[x][c]
-                out_ref[c, p, pl.ds(at, grid.subs, stride=plan.cols), :] = value
-
-    count = chunk_of(plies, 2)
-
-    def step(n, carry):
-        for k in range(count):
-            ply(n * count + k)
-        for k in range(count):
-            copy_out(n * count + k).start()
-        return carry
-
-    lax.fori_loop(0, plies // count, step, 0)
-    for p in range(plies):
-        copy_out(p).wait()
+                value = force_ref[n, c, x - REACH]
+                out_ref[c, n, pl.ds(at, grid.subs, stride=plan.cols), :] = value * sign if c == 0 else value
+
+    for first in range(part.start, part.stop, 2):
+        group = range(first, min(first + 2, part.stop))
+        for p in group:
+            ply(p)
+        if final:
+            for p in group:
+                copy_out(p).start()
+    if final:
+        copy_before.wait()
+        for p in part:
+            copy_out(p).wait()
 
 
 def local(displacement, angle_index, bond_table, interface_stiffness):
@@ -647,22 +661,22 @@
         lambda *refs: pack_kernel(plan, *refs),
         "pack",
         [whole],
-        [array(plies, 3, cols), array(1, plies, 3 * REACH)],
+        [array(plies, 3, cols), array(1, plies, 2 * REACH)],
     )(view)
     got_a = lax.ppermute(message_a, "tile", swap_a)
 
-    thin_a, rows_a, sums_a, inverse_a, first, second = call(
+    more_a, rows_a, sums_a, inverse_a, first, second = call(
         lambda *refs: near_a_kernel(plan, *refs),
         "near_a",
         [whole],
         [
-            array(1, plies, REACH), array(plies, REACH + 1, 3, tall), array(plies, tall),
+            array(1, plies, 2 * REACH), array(plies, REACH + 1, 3, tall), array(plies, tall),
             array(plies, len(plan.inner_a)), array(1, 3, cols), array(1, 3, cols),
         ],
     )(base)
-    got_thin_a = lax.ppermute(thin_a, "tile", swap_a)
+    got_more_a = lax.ppermute(more_a, "tile", swap_a)
+    got_second = lax.ppermute(second, "ply", swap_second)
     got_first = lax.ppermute(first, "ply", swap_first)
-    got_second = lax.ppermute(second, "ply", swap_second)
 
     rows_b, sums_b, inverse_b = call(
         lambda *refs: near_b_kernel(plan, *refs),
@@ -674,61 +688,79 @@
         ],
     )(base, rows_a, sums_a)
 
-    weight, pair = call(
-        lambda *refs: weight_kernel(plan, tiles, *refs),
+    weight, pair, factor, spring = call(
+        lambda *refs: weight_kernel(plan, tiles, slabs, *refs),
         "weights",
-        [],
-        [array(plan.wide), array(len(plan.early) + len(plan.late))],
-    )()
-
-    def inner_part(keys, name, after):
-        return call(
-            lambda *refs: inner_kernel(plan, keys, *refs),
-            name,
-            [scalars] * 2 + [whole] * 6,
-            [array(plies, len(keys), 3), array(plies, 3, len(plan.span(keys)))],
-        )(angle_index, bond_table, after, rows_a, rows_b, inverse_a, inverse_b, pair)
-
-    vector_late, inner_late = inner_part(plan.inner_late, "inner_late", got_first)
-    (message_b,) = call(
-        lambda *refs: send_kernel(plan, *refs),
-        "send",
-        [whole] * 3,
-        [array(1, plies, 3 * REACH)],
-    )(got_a, inner_late, base)
-    got_b = lax.ppermute(message_b, ("ply", "tile"), swap_b)
-    vector_early, inner_early = inner_part(plan.inner_early, "inner_early", message_b)
-
-    force, strain, thin_b = call(
-        lambda *refs: early_kernel(plan, tiles, slabs, *refs),
+        [scalars] * 3 + [whole],
+        [
+            array(plan.wide), array(len(plan.early) + len(plan.late)), array(plies, 2 * len(OFFSETS)),
+            array(plies, 4),
+        ],
+    )(angle_index, bond_table, interface_stiffness, got_first)
+
+    vector_late, inner_late = call(
+        lambda *refs: inner_kernel(plan, *refs),
+        "inner",
+        [whole] * 7,
+        [array(plies, len(plan.inner_late), 3), array(plies, 3, len(plan.span(plan.inner_late)))],
+    )(got_second, factor, rows_a, rows_b, inverse_a, inverse_b, pair)
+
+    count = plies - plies // 3
+    parts = [range(count), range(count, plies)]
+    def send_part(part, name, after):
+        (message,) = call(
+            lambda *refs: send_kernel(plan, part, *refs), name, [whole] * 3, [array(1, len(part), 4 * REACH)]
+        )(after, base, sums_b)
+        return message, lax.ppermute(message, ("ply", "tile"), swap_b)
+
+    message_b, got = send_part(parts[0], "send", got_a)
+    got_b = [got]
+    message_b, got = send_part(parts[1], "send_rest", inner_late)
+    got_b.append(got)
+
+    halo_a, strain, inverse_cross = call(
+        lambda *refs: strain_kernel(plan, tiles, *refs),
+        "strain",
+        [whole] * 8,
+        [
+            array(plies, REACH + 1, 3, REACH), array(plies, REACH + 1, plan.wide - 2 * REACH),
+            array(plies, len(plan.cross_a)),
+        ],
+    )(message_b, got_a, got_more_a, rows_a, rows_b, sums_a, sums_b, weight)
+
+    (force,) = call(
+        lambda *refs: early_kernel(plan, tiles, *refs),
         "early",
-        [scalars] * 3 + [whole] * 12,
-        [array(plies, 3, cols), array(plies, REACH + 1, plan.wide - 2 * REACH), array(1, plies, REACH)],
+        [whole] * 10,
+        [array(plies, 3, cols)],
         cost=EARLY_COST,
-        scratches=[scratch(REACH + 1, 3, REACH), scratch(len(plan.cross_a))],
-    )(
-        angle_index, bond_table, interface_stiffness, got_a, got_thin_a, rows_a, rows_b, sums_a, sums_b,
-        weight, pair, vector_early, inner_early, got_first, got_second,
-    )
-    got_thin_b = lax.ppermute(thin_b, ("ply", "tile"), swap_b)
-
-    force, cross, sums_low = call(
-        lambda *refs: middle_kernel(plan, tiles, *refs),
-        "middle",
-        [scalars] * 2 + [whole] * 10,
-        [array(plies, 3, cols), array(plies, len(plan.cross_b), 3), array(plies, REACH)],
-        cost=MIDDLE_COST,
-        scratches=[scratch(REACH + 1, 3, REACH), scratch(len(plan.cross_b)), scratch(REACH + 1, REACH)],
-    )(angle_index, bond_table, got_b, rows_a, rows_b, sums_b, weight, pair, vector_late, inner_late, force, strain)
-
-    (out,) = call(
-        lambda *refs: last_kernel(plan, *refs),
-        "last",
-        [whole] * 5,
-        [jax.ShapeDtypeStruct(view.shape, jnp.float32)],
-        out_specs=[pl.BlockSpec(memory_space=pltpu.HBM)],
-        scratches=[pltpu.VMEM(view.shape, jnp.float32), pltpu.SemaphoreType.DMA((plies,))],
-    )(got_thin_b, sums_low, weight, cross, force)
+    )(rows_a, rows_b, halo_a, strain, inverse_cross, inverse_a, inverse_b, pair, factor, spring)
+
+    out = []
+    for part, got in zip(parts, got_b):
+        final = part.stop == plies
+        result = jax.ShapeDtypeStruct((comps, len(part), *view.shape[2:]), jnp.float32)
+        scratches = [
+            scratch(len(part), REACH + 1, 3, REACH), scratch(len(part), len(plan.cross_b)),
+            scratch(len(part), REACH + 1, 2 * REACH), scratch(len(part), 3, cols),
+        ]
+        if final:
+            scratches += [
+                pltpu.VMEM(result.shape, jnp.float32), pltpu.SemaphoreType.DMA((len(part),)), pltpu.SemaphoreType.DMA,
+            ]
+        out = call(
+            lambda *refs: late_kernel(plan, tiles, part, final, *refs),
+            "late_rest" if final else "late",
+            [whole] * (14 + len(out)),
+            [jax.ShapeDtypeStruct(view.shape, jnp.float32) if final else result],
+            out_specs=[pl.BlockSpec(memory_space=pltpu.HBM)] if final else None,
+            scratches=scratches,
+            cost=LATE_COST,
+        )(
+            got_first, got_second, got, rows_a, rows_b, sums_b, weight, pair, factor, spring, vector_late, inner_late,
+            force, strain, *out,
+        )
+    (out,) = out
     return (
         out.reshape(comps, plies, subs, cols, LANES)
         .transpose(0, 1, 3, 2, 4)

time: 21.4 us -> 18.3 us (0.86)
  Pallas kernels: 10.6 us -> 8.26 us
  waiting for transfers between devices: 2.44 us -> 1.93 us
    pallas_call x7 -> x8, Pallas kernels: 8.63 us -> 6.23 us  [the longest x2 2.06 us: local(): call(lambda *refs: late_kernel(plan, tiles, part, final, *refs), 'late_re...]
    ppermute x3, waiting for transfers between devices: 2.43 us -> 1.11 us  [the longest x2 1.11 us: send_part(): return (message, lax.ppermute(message, ('ply', 'tile'), swap_b))]
    ppermute x1, waiting for transfers between devices: 0.01 us -> 0.81 us  [local(): got_a = lax.ppermute(message_a, 'tile', swap_a)]
  transfers between devices with their start and end apart: 6 -> 6, of which waited for: 2 -> 3; matrix products, arithmetic and copies ran while one was open for 0% -> 0% of each run, Pallas kernels for 44% -> 38%
where the time goes in v4:
time: 18.3 us; the launch traced here: 18.2 us
  Pallas kernels  8.26 us (45%)
  starting transfers between devices  6.82 us (37%)
  waiting for transfers between devices  1.93 us (11%)
  local copies, waits for them, and re-layouts  1.07 us (6%)
    ppermute x2, starting transfers between devices, send_part(): return (message, lax.ppermute(message, ('ply', 'tile'), swap_b))  3.06 us
    pallas_call x2, Pallas kernels, local(): call(lambda *refs: late_kernel(plan, tiles, part, final, *refs), 'late_re...  2.06 us
    ppermute x1, starting transfers between devices, local(): got_second = lax.ppermute(second, 'ply', swap_second)  1.6 us
    ppermute x1, starting transfers between devices, local(): got_a = lax.ppermute(message_a, 'tile', swap_a)  1.58 us
    pallas_call x1, Pallas kernels, local(): call(lambda *refs: early_kernel(plan, tiles, *refs), 'early', [whole] * 1...  1.5 us
    ppermute x2, waiting for transfers between devices, send_part(): return (message, lax.ppermute(message, ('ply', 'tile'), swap_b))  1.11 us
    unnamed x8, local copies, waits for them, and re-layouts  1.07 us
    pallas_call x1, Pallas kernels, local(): call(lambda *refs: inner_kernel(plan, *refs), 'inner', [whole] * 7, [arra...  1.04 us
  transfers between devices with their start and end apart: 6, of which 3 were waited for; matrix products, arithmetic and copies ran while one was open for 0% of the time, Pallas kernels for 38%

profile of v4, /device:TPU:8, one launch (start us, length us, event | category | flops | bytes accessed | tf_op | source)
XLA Modules:
  0.0 18.2 jit_solution(13087768706593337056)
XLA Ops:
  0.0 0.0 copy-start
  0.0 1.1 %copy-done = f32[3,6,8,1024]{3,2,1,0:T(8,128)S(1)} copy-done((f32[3,6,8,1024]{3,2,1,0:T(8,128)S(1)}, f32[3,6,8,1024]{3,2,1,0:T(8,128)}, u32[]{:S(2)}) %copy-start) | copy-done | bytes 589848
  1.1 0.2 pack.1
  1.2 1.6 %collective-permute-start.3 = (f32[1,6,6,8,128]{4,3,2,1,0:T(8,128)S(1)}, f32[1,6,6,8,128]{4,3,2,1,0:T(8,128)S(1)}, u32[]{:S(2)}, u32[]{:S(2)}) collective-permute-start(f32[1,6,6,8,128]{4,3,2,1,0:T(8,128)S(1)} %get-tuple-element.40), channel_id=1, source_target_pairs={{0,1},{1,0},{2,3},{3,2},{4,5},{5,4},{6,7},{7,6},{8,9},{9,8},{10,11... | collective-permute-start | bytes 442376 | tf_op jit(solution)/shard_map/ppermute | solution.py:666
  2.8 1.0 %near_a.1 = (f32[1,6,6,8,128]{4,3,2,1,0:T(8,128)S(1)}, f32[6,4,3,6,8,128]{5,4,3,2,1,0:T(8,128)S(1)}, f32[6,6,8,128]{3,2,1,0:T(8,128)S(1)}, f32[6,42,8,128]{3,2,1...) custom-call(f32[6,3,8,8,128]{4,3,2,1,0:T(8,128)S(1)} %get-tuple-element.25.refs_0_.refs_1_), custom_call_target="tpu_custom_call" | custom-call | flops 1 | bytes 1 | tf_op jit(solution)/shard_map/near_a/pallas_call | solution.py:668
  3.8 0.6 %collective-permute-start.4 = (f32[1,6,6,8,128]{4,3,2,1,0:T(8,128)S(1)}, f32[1,6,6,8,128]{4,3,2,1,0:T(8,128)S(1)}, u32[]{:S(2)}, u32[]{:S(2)}) collective-permute-start(f32[1,6,6,8,128]{4,3,2,1,0:T(8,128)S(1)} %get-tuple-element.41), channel_id=1, source_target_pairs={{0,1},{1,0},{2,3},{3,2},{4,5},{5,4},{6,7},{7,6},{8,9},{9,8},{10,11... | collective-permute-start | bytes 442376 | tf_op jit(solution)/shard_map/ppermute | solution.py:677
  4.4 0.0 collective-permute-start
  4.4 1.6 %collective-permute-start.1 = (f32[1,3,8,8,128]{4,3,2,1,0:T(8,128)S(1)}, f32[1,3,8,8,128]{4,3,2,1,0:T(8,128)S(1)}, u32[]{:S(2)}, u32[]{:S(2)}) collective-permute-start(f32[1,3,8,8,128]{4,3,2,1,0:T(8,128)S(1)} %get-tuple-element.27), channel_id=1, source_target_pairs={{8,16},{16,8},{0,24},{24,0},{9,17},{17,9},{1,25},{25,1},{10,18},{1... | collective-permute-start | bytes 294920 | tf_op jit(solution)/shard_map/ppermute | solution.py:678
  6.0 0.0 copy-start.1
  6.0 0.0 copy-start.2
  6.0 0.0 copy-start.3
  6.0 0.9 %near_b.1 = (f32[6,4,3,2,8,128]{5,4,3,2,1,0:T(8,128)S(1)}, f32[6,5,8,128]{3,2,1,0:T(8,128)S(1)}, f32[6,52,8,128]{3,2,1,0:T(8,128)S(1)}) custom-call(f32[6,3,8,8,128]{4,3,2,1,0:T(8,128)S(1)} %get-tuple-element.25.refs_0_.refs_1_, f32[6,4,3,6,8,128]{5,4,3,2,1,0:T(8,128)S(1)} %get-tuple-element.29.refs_1_.refs_2_.refs_3_.refs_0_, ...), custom_call_target="tpu_custom_call" | custom-call | flops 1 | bytes 1 | tf_op jit(solution)/shard_map/near_b/pallas_call | solution.py:681
  6.9 0.8 %collective-permute-done.3.refs_1_.refs_0_ = f32[1,6,6,8,128]{4,3,2,1,0:T(8,128)S(1)} collective-permute-done((f32[1,6,6,8,128]{4,3,2,1,0:T(8,128)S(1)}, f32[1,6,6,8,128]{4,3,2,1,0:T(8,128)S(1)}, u32[]{:S(2)}, u32[]{:S(2)}) %collective-permute-start.3) | collective-permute-done | bytes 147488 | tf_op jit(solution)/shard_map/ppermute | solution.py:666
  7.7 1.8 %collective-permute-start.5 = (f32[1,4,12,8,128]{4,3,2,1,0:T(8,128)S(1)}, f32[1,4,12,8,128]{4,3,2,1,0:T(8,128)S(1)}, u32[]{:S(2)}, u32[]{:S(2)}) collective-permute-start(f32[1,4,12,8,128]{4,3,2,1,0:T(8,128)S(1)} %send.1), channel_id=1, source_target_pairs={{0,8},{1,2},{2,1},{3,4},{4,3},{5,6},{6,5},{7,15},{8,0},{9,10},{10,... | collective-permute-start | bytes 589832 | tf_op jit(solution)/shard_map/ppermute | solution.py:714
  9.5 0.0 collective-permute-done.refs_3_.refs_0_
  9.5 0.0 copy-done.1
  9.5 0.0 copy-done.2
  9.5 0.0 copy-done.3
  9.5 0.8 %weights.1 = (f32[14,8,128]{2,1,0:T(8,128)S(1)}, f32[130,8,128]{2,1,0:T(8,128)S(1)}, f32[6,28,8,128]{3,2,1,0:T(8,128)S(1)}, f32[6,4,8,128]{3,2,1,0:T(8,128)S(1)}) custom-call(s32[6]{0:T(128)S(1)} %copy-done.2, f32[4,14]{1,0:T(4,128)S(1)} %copy-done.1, f32[23]{0:T(128)S(1)} %copy-done.3, f32[1,3,8,8,128]{4,3,2,1,0:T(8,128)S(1)} %collective-permute-done.refs_3_.refs_0_), custom_call_target="tpu_custom_call" | custom-call | flops 1 | bytes 1 | tf_op jit(solution)/shard_map/weights/pallas_call | solution.py:691
  10.4 0.0 collective-permute-done.1.refs_0_.refs_1_
  10.4 1.0 %inner.1 = (f32[6,42,3,8,128]{4,3,2,1,0:T(8,128)S(1)}, f32[6,3,6,8,128]{4,3,2,1,0:T(8,128)S(1)}) custom-call(f32[1,3,8,8,128]{4,3,2,1,0:T(8,128)S(1)} %collective-permute-done.1.refs_0_.refs_1_, f32[6,28,8,128]{3,2,1,0:T(8,128)S(1)} %get-tuple-element.28.refs_1_.refs_8_, f32[6,4,3,6,8,128]{5,4,3,2,1,0:T(8,128)S(1)} %get-tuple-element.29.refs_1_.refs_2_.refs_3_.refs_0_, ...), custom_call_target="tpu_custom_call" | custom-call | flops 1 | bytes 1 | tf_op jit(solution)/shard_map/inner/pallas_call | solution.py:701
  11.4 1.3 %collective-permute-start.2 = (f32[1,2,12,8,128]{4,3,2,1,0:T(8,128)S(1)}, f32[1,2,12,8,128]{4,3,2,1,0:T(8,128)S(1)}, u32[]{:S(2)}, u32[]{:S(2)}) collective-permute-start(f32[1,2,12,8,128]{4,3,2,1,0:T(8,128)S(1)} %send_rest.1.refs_0_), channel_id=1, source_target_pairs={{0,8},{1,2},{2,1},{3,4},{4,3},{5,6},{6,5},{7,15},{8,0},{9,10},{10,... | collective-permute-start | bytes 294920 | tf_op jit(solution)/shard_map/ppermute | solution.py:714
  12.7 0.0 collective-permute-done.4.refs_2_
  12.7 0.8 %strain.1 = (f32[6,4,3,3,8,128]{5,4,3,2,1,0:T(8,128)S(1)}, f32[6,4,8,8,128]{4,3,2,1,0:T(8,128)S(1)}, f32[6,18,8,128]{3,2,1,0:T(8,128)S(1)}) custom-call(f32[1,2,12,8,128]{4,3,2,1,0:T(8,128)S(1)} %send_rest.1.refs_0_, f32[1,6,6,8,128]{4,3,2,1,0:T(8,128)S(1)} %collective-permute-done.3.refs_1_.refs_0_, ...), custom_call_target="tpu_custom_call" | custom-call | flops 1 | bytes 1 | tf_op jit(solution)/shard_map/strain/pallas_call | solution.py:721
  13.5 1.5 %early.1.refs_12_ = f32[6,3,8,8,128]{4,3,2,1,0:T(8,128)S(1)} custom-call(f32[6,4,3,6,8,128]{5,4,3,2,1,0:T(8,128)S(1)} %get-tuple-element.29.refs_1_.refs_2_.refs_3_.refs_0_, f32[6,4,3,2,8,128]{5,4,3,2,1,0:T(8,128)S(1)} %get-tuple-element.31.refs_3_.refs_4_.refs_1_, f32[6,4,3,3,8,128]{5,4,3,2,1,0:T(8,128)S(1)} %get-tuple-element.42.refs_2_, ...), custom_call_target="tpu_custom_call" | custom-call | flops 2000000000 | bytes 1 | tf_op jit(solution)/shard_map/early/pallas_call | solution.py:731
  15.0 0.1 collective-permute-done.5.refs_2_
  15.1 0.9 %late.1.refs_14_ = f32[3,4,64,128]{3,2,1,0:T(8,128)S(1)} custom-call(f32[1,3,8,8,128]{4,3,2,1,0:T(8,128)S(1)} %collective-permute-done.refs_3_.refs_0_, f32[1,3,8,8,128]{4,3,2,1,0:T(8,128)S(1)} %collective-permute-done.1.refs_0_.refs_1_, f32[1,4,12,8,128]{4,3,2,1,0:T(8,128)S(1)} %collective-permute-done.5.refs_2_, ...), custom_call_target="tpu_custom_call" | custom-call | flops 2000000000 | bytes 1 | tf_op jit(solution)/shard_map/late/pallas_call | solution.py:751
  16.0 1.0 %collective-permute-done.2.refs_2_ = f32[1,2,12,8,128]{4,3,2,1,0:T(8,128)S(1)} collective-permute-done((f32[1,2,12,8,128]{4,3,2,1,0:T(8,128)S(1)}, f32[1,2,12,8,128]{4,3,2,1,0:T(8,128)S(1)}, u32[]{:S(2)}, u32[]{:S(2)}) %collective-permute-start.2) | collective-permute-done | bytes 98336 | tf_op jit(solution)/shard_map/ppermute | solution.py:714
  17.0 1.2 %late_rest.1 = f32[3,6,64,128]{3,2,1,0:T(8,128)} custom-call(f32[1,3,8,8,128]{4,3,2,1,0:T(8,128)S(1)} %collective-permute-done.refs_3_.refs_0_, f32[1,3,8,8,128]{4,3,2,1,0:T(8,128)S(1)} %collective-permute-done.1.refs_0_.refs_1_, f32[1,2,12,8,128]{4,3,2,1,0:T(8,128)S(1)} %collective-permute-done.2.refs_2_, ...), custom_call_target="tpu_custom_call" | custom-call | flops 2000000000 | bytes 1 | tf_op jit(solution)/shard_map/late_rest/pallas_call | solution.py:751
  (2 shorter events, 0.0 us)
Async XLA Ops:
  0.0 1.1 %copy-start = (f32[3,6,8,1024]{3,2,1,0:T(8,128)S(1)}, f32[3,6,8,1024]{3,2,1,0:T(8,128)}, u32[]{:S(2)}) copy-start(f32[3,6,8,1024]{3,2,1,0:T(8,128)} %param.4) | copy-start | bytes 1769476
  1.2 6.5 %collective-permute-start.3 = (f32[1,6,6,8,128]{4,3,2,1,0:T(8,128)S(1)}, f32[1,6,6,8,128]{4,3,2,1,0:T(8,128)S(1)}, u32[]{:S(2)}, u32[]{:S(2)}) collective-permute-start(f32[1,6,6,8,128]{4,3,2,1,0:T(8,128)S(1)} %get-tuple-element.40), channel_id=1, source_target_pairs={{0,1},{1,0},{2,3},{3,2},{4,5},{5,4},{6,7},{7,6},{8,9},{9,8},{10,11... | collective-permute-start | bytes 442376 | tf_op jit(solution)/shard_map/ppermute | solution.py:666
  3.8 8.9 %collective-permute-start.4 = (f32[1,6,6,8,128]{4,3,2,1,0:T(8,128)S(1)}, f32[1,6,6,8,128]{4,3,2,1,0:T(8,128)S(1)}, u32[]{:S(2)}, u32[]{:S(2)}) collective-permute-start(f32[1,6,6,8,128]{4,3,2,1,0:T(8,128)S(1)} %get-tuple-element.41), channel_id=1, source_target_pairs={{0,1},{1,0},{2,3},{3,2},{4,5},{5,4},{6,7},{7,6},{8,9},{9,8},{10,11... | collective-permute-start | bytes 442376 | tf_op jit(solution)/shard_map/ppermute | solution.py:677
  4.4 5.1 %collective-permute-start = (f32[1,3,8,8,128]{4,3,2,1,0:T(8,128)S(1)}, f32[1,3,8,8,128]{4,3,2,1,0:T(8,128)S(1)}, u32[]{:S(2)}, u32[]{:S(2)}) collective-permute-start(f32[1,3,8,8,128]{4,3,2,1,0:T(8,128)S(1)} %get-tuple-element.26), channel_id=1, source_target_pairs={{0,8},{8,0},{16,24},{24,16},{1,9},{9,1},{17,25},{25,17},{2,10},{10... | collective-permute-start | bytes 294920 | tf_op jit(solution)/shard_map/ppermute | solution.py:679
  4.4 6.0 %collective-permute-start.1 = (f32[1,3,8,8,128]{4,3,2,1,0:T(8,128)S(1)}, f32[1,3,8,8,128]{4,3,2,1,0:T(8,128)S(1)}, u32[]{:S(2)}, u32[]{:S(2)}) collective-permute-start(f32[1,3,8,8,128]{4,3,2,1,0:T(8,128)S(1)} %get-tuple-element.27), channel_id=1, source_target_pairs={{8,16},{16,8},{0,24},{24,0},{9,17},{17,9},{1,25},{25,1},{10,18},{1... | collective-permute-start | bytes 294920 | tf_op jit(solution)/shard_map/ppermute | solution.py:678
  6.0 3.5 %copy-start.1 = (f32[4,14]{1,0:T(4,128)S(1)}, f32[4,14]{1,0:T(4,128)}, u32[]{:S(2)}) copy-start(f32[4,14]{1,0:T(4,128)} %refs_1_.1) | copy-start | bytes 676
  6.0 3.5 %copy-start.2 = (s32[6]{0:T(128)S(1)}, s32[6]{0:T(128)}, u32[]{:S(2)}) copy-start(s32[6]{0:T(128)} %refs_0_.1) | copy-start | bytes 76
  6.0 3.5 %copy-start.3 = (f32[23]{0:T(128)S(1)}, f32[23]{0:T(128)}, u32[]{:S(2)}) copy-start(f32[23]{0:T(128)} %refs_2_.1) | copy-start | bytes 280
  7.7 7.4 %collective-permute-start.5 = (f32[1,4,12,8,128]{4,3,2,1,0:T(8,128)S(1)}, f32[1,4,12,8,128]{4,3,2,1,0:T(8,128)S(1)}, u32[]{:S(2)}, u32[]{:S(2)}) collective-permute-start(f32[1,4,12,8,128]{4,3,2,1,0:T(8,128)S(1)} %send.1), channel_id=1, source_target_pairs={{0,8},{1,2},{2,1},{3,4},{4,3},{5,6},{6,5},{7,15},{8,0},{9,10},{10,... | collective-permute-start | bytes 589832 | tf_op jit(solution)/shard_map/ppermute | solution.py:714
  11.4 5.6 %collective-permute-start.2 = (f32[1,2,12,8,128]{4,3,2,1,0:T(8,128)S(1)}, f32[1,2,12,8,128]{4,3,2,1,0:T(8,128)S(1)}, u32[]{:S(2)}, u32[]{:S(2)}) collective-permute-start(f32[1,2,12,8,128]{4,3,2,1,0:T(8,128)S(1)} %send_rest.1.refs_0_), channel_id=1, source_target_pairs={{0,8},{1,2},{2,1},{3,4},{4,3},{5,6},{6,5},{7,15},{8,0},{9,10},{10,... | collective-permute-start | bytes 294920 | tf_op jit(solution)/shard_map/ppermute | solution.py:714

commit v5 on v4

--- a/solution.py
+++ b/solution.py
@@ -198,29 +198,35 @@
     lax.fori_loop(0, plies // count, step, 0)
 
 
-def pack_kernel(plan, u_ref, rows_ref, message):
-    comps, plies, depth, _ = u_ref.shape
+def own_row(plan, u_ref, odd, sign, p, c, column):
+    x = column - REACH
+    at = jnp.where(odd, plan.cols - 1 - x, x)
+    row = u_ref[c, p, pl.ds(at, u_ref.shape[2] // plan.cols, stride=plan.cols), :]
+    return row * sign if c == 0 else row
+
+
+def pack_kernel(plan, u_ref, message):
     odd, sign = frame()
-    for p in range(plies):
-        for x in range(plan.cols):
-            at = jnp.where(odd, plan.cols - 1 - x, x)
-            for c in range(comps):
-                row = u_ref[c, p, pl.ds(at, depth // plan.cols, stride=plan.cols), :]
-                row = row * sign if c == 0 else row
-                rows_ref[p, c, x] = row
-                if x + REACH in plan.near_a and c < 2:
-                    message[0, p, c * REACH + x + REACH - plan.near_a.start] = row
-
-
-def near_a_kernel(plan, base_ref, message, rows_ref, sums_ref, inverse_ref, first_ref, second_ref):
+    for p in range(u_ref.shape[1]):
+        for c in range(2):
+            for n, column in enumerate(plan.near_a):
+                message[0, p, c * REACH + n] = own_row(plan, u_ref, odd, sign, p, c, column)
+
+
+def near_a_kernel(plan, after_ref, u_ref, message, base_ref, rows_ref, sums_ref, inverse_ref, first_ref, second_ref):
     plies = base_ref.shape[0]
+    odd, sign = frame()
     grid = Grid(base_ref.shape[-2])
     slots = {key: n for n, key in enumerate(plan.inner_a)}
 
     def ply(p):
         rows = Store((rows_ref, plan.start_a, range(plan.start_a, plan.own.stop), (p,)))
-        for x in rows.parts[0][2]:
-            keep_row(grid, rows, x, [base_ref[p, c, x - REACH] for c in range(3)])
+        for x in plan.own:
+            row = [own_row(plan, u_ref, odd, sign, p, c, x) for c in range(3)]
+            for c in range(3):
+                base_ref[p, c, x - REACH] = row[c]
+            if x >= plan.start_a:
+                keep_row(grid, rows, x, row)
 
         def keep(key, r):
             inverse_ref[p, slots[key]] = r
@@ -657,23 +663,23 @@
     tall = plan.own.stop - plan.start_a
     short = plan.start_a - REACH
 
-    base, message_a = call(
+    (message_a,) = call(
         lambda *refs: pack_kernel(plan, *refs),
         "pack",
         [whole],
-        [array(plies, 3, cols), array(1, plies, 2 * REACH)],
+        [array(1, plies, 2 * REACH)],
     )(view)
     got_a = lax.ppermute(message_a, "tile", swap_a)
 
-    more_a, rows_a, sums_a, inverse_a, first, second = call(
+    more_a, base, rows_a, sums_a, inverse_a, first, second = call(
         lambda *refs: near_a_kernel(plan, *refs),
         "near_a",
-        [whole],
+        [whole] * 2,
         [
-            array(1, plies, 2 * REACH), array(plies, REACH + 1, 3, tall), array(plies, tall),
+            array(1, plies, 2 * REACH), array(plies, 3, cols), array(plies, REACH + 1, 3, tall), array(plies, tall),
             array(plies, len(plan.inner_a)), array(1, 3, cols), array(1, 3, cols),
         ],
-    )(base)
+    )(message_a, view)
     got_more_a = lax.ppermute(more_a, "tile", swap_a)
     got_second = lax.ppermute(second, "ply", swap_second)
     got_first = lax.ppermute(first, "ply", swap_first)

time: 18.3 us -> 18.2 us (level)
  transfers between devices with their start and end apart: 6 -> 6, of which waited for: 3 -> 3; matrix products, arithmetic and copies ran while one was open for 0% -> 0% of each run, Pallas kernels for 38% -> 39%
where the time goes in v5:
time: 18.2 us; the launch traced here: 18 us
  Pallas kernels  8.18 us (45%)
  starting transfers between devices  6.82 us (37%)
  waiting for transfers between devices  1.89 us (10%)
  local copies, waits for them, and re-layouts  1.07 us (6%)
    ppermute x2, starting transfers between devices, send_part(): return (message, lax.ppermute(message, ('ply', 'tile'), swap_b))  3.06 us
    pallas_call x2, Pallas kernels, local(): call(lambda *refs: late_kernel(plan, tiles, part, final, *refs), 'late_re...  2.06 us
    ppermute x1, starting transfers between devices, local(): got_second = lax.ppermute(second, 'ply', swap_second)  1.6 us
    ppermute x1, starting transfers between devices, local(): got_a = lax.ppermute(message_a, 'tile', swap_a)  1.58 us
    pallas_call x1, Pallas kernels, local(): call(lambda *refs: early_kernel(plan, tiles, *refs), 'early', [whole] * 1...  1.5 us
    ppermute x2, waiting for transfers between devices, send_part(): return (message, lax.ppermute(message, ('ply', 'tile'), swap_b))  1.15 us
    unnamed x8, local copies, waits for them, and re-layouts  1.07 us
    pallas_call x1, Pallas kernels, local(): call(lambda *refs: near_a_kernel(plan, *refs), 'near_a', [whole] * 2, [ar...  1.05 us
  transfers between devices with their start and end apart: 6, of which 3 were waited for; matrix products, arithmetic and copies ran while one was open for 0% of the time, Pallas kernels for 39%

profile of v5, /device:TPU:8, one launch (start us, length us, event | category | flops | bytes accessed | tf_op | source)
XLA Modules:
  0.0 18.0 jit_solution(11399938923617683525)
XLA Ops:
  0.0 0.0 copy-start
  0.0 1.1 %copy-done = f32[3,6,8,1024]{3,2,1,0:T(8,128)S(1)} copy-done((f32[3,6,8,1024]{3,2,1,0:T(8,128)S(1)}, f32[3,6,8,1024]{3,2,1,0:T(8,128)}, u32[]{:S(2)}) %copy-start) | copy-done | bytes 589848
  1.1 1.6 %collective-permute-start.3 = (f32[1,6,6,8,128]{4,3,2,1,0:T(8,128)S(1)}, f32[1,6,6,8,128]{4,3,2,1,0:T(8,128)S(1)}, u32[]{:S(2)}, u32[]{:S(2)}) collective-permute-start(f32[1,6,6,8,128]{4,3,2,1,0:T(8,128)S(1)} %pack.1.refs_0_), channel_id=1, source_target_pairs={{0,1},{1,0},{2,3},{3,2},{4,5},{5,4},{6,7},{7,6},{8,9},{9,8},{10,11... | collective-permute-start | bytes 442376 | tf_op jit(solution)/shard_map/ppermute | solution.py:672
  2.7 1.0 %near_a.1 = (f32[1,6,6,8,128]{4,3,2,1,0:T(8,128)S(1)}, f32[6,3,8,8,128]{4,3,2,1,0:T(8,128)S(1)}, f32[6,4,3,6,8,128]{5,4,3,2,1,0:T(8,128)S(1)}, f32[6,6,8,128]{3,...) custom-call(f32[1,6,6,8,128]{4,3,2,1,0:T(8,128)S(1)} %pack.1.refs_0_, ...), custom_call_target="tpu_custom_call" | custom-call | flops 1 | bytes 1 | tf_op jit(solution)/shard_map/near_a/pallas_call | solution.py:674
  3.7 0.6 %collective-permute-start.4 = (f32[1,6,6,8,128]{4,3,2,1,0:T(8,128)S(1)}, f32[1,6,6,8,128]{4,3,2,1,0:T(8,128)S(1)}, u32[]{:S(2)}, u32[]{:S(2)}) collective-permute-start(f32[1,6,6,8,128]{4,3,2,1,0:T(8,128)S(1)} %get-tuple-element.39), channel_id=1, source_target_pairs={{0,1},{1,0},{2,3},{3,2},{4,5},{5,4},{6,7},{7,6},{8,9},{9,8},{10,11... | collective-permute-start | bytes 442376 | tf_op jit(solution)/shard_map/ppermute | solution.py:683
  4.3 0.0 collective-permute-start
  4.3 1.6 %collective-permute-start.1 = (f32[1,3,8,8,128]{4,3,2,1,0:T(8,128)S(1)}, f32[1,3,8,8,128]{4,3,2,1,0:T(8,128)S(1)}, u32[]{:S(2)}, u32[]{:S(2)}) collective-permute-start(f32[1,3,8,8,128]{4,3,2,1,0:T(8,128)S(1)} %get-tuple-element.25), channel_id=1, source_target_pairs={{8,16},{16,8},{0,24},{24,0},{9,17},{17,9},{1,25},{25,1},{10,18},{1... | collective-permute-start | bytes 294920 | tf_op jit(solution)/shard_map/ppermute | solution.py:684
  5.9 0.0 copy-start.1
  5.9 0.0 copy-start.2
  5.9 0.0 copy-start.3
  5.9 0.9 %near_b.1 = (f32[6,4,3,2,8,128]{5,4,3,2,1,0:T(8,128)S(1)}, f32[6,5,8,128]{3,2,1,0:T(8,128)S(1)}, f32[6,52,8,128]{3,2,1,0:T(8,128)S(1)}) custom-call(f32[6,3,8,8,128]{4,3,2,1,0:T(8,128)S(1)} %get-tuple-element.28.refs_0_.refs_1_, f32[6,4,3,6,8,128]{5,4,3,2,1,0:T(8,128)S(1)} %get-tuple-element.27.refs_1_.refs_2_.refs_3_.refs_0_, ...), custom_call_target="tpu_custom_call" | custom-call | flops 1 | bytes 1 | tf_op jit(solution)/shard_map/near_b/pallas_call | solution.py:687
  6.8 0.7 %collective-permute-done.3.refs_1_.refs_0_ = f32[1,6,6,8,128]{4,3,2,1,0:T(8,128)S(1)} collective-permute-done((f32[1,6,6,8,128]{4,3,2,1,0:T(8,128)S(1)}, f32[1,6,6,8,128]{4,3,2,1,0:T(8,128)S(1)}, u32[]{:S(2)}, u32[]{:S(2)}) %collective-permute-start.3) | collective-permute-done | bytes 147488 | tf_op jit(solution)/shard_map/ppermute | solution.py:672
  7.6 1.8 %collective-permute-start.5 = (f32[1,4,12,8,128]{4,3,2,1,0:T(8,128)S(1)}, f32[1,4,12,8,128]{4,3,2,1,0:T(8,128)S(1)}, u32[]{:S(2)}, u32[]{:S(2)}) collective-permute-start(f32[1,4,12,8,128]{4,3,2,1,0:T(8,128)S(1)} %send.1), channel_id=1, source_target_pairs={{0,8},{1,2},{2,1},{3,4},{4,3},{5,6},{6,5},{7,15},{8,0},{9,10},{10,... | collective-permute-start | bytes 589832 | tf_op jit(solution)/shard_map/ppermute | solution.py:720
  9.4 0.0 collective-permute-done.refs_3_.refs_0_
  9.4 0.0 copy-done.1
  9.4 0.0 copy-done.2
  9.4 0.0 copy-done.3
  9.4 0.8 %weights.1 = (f32[14,8,128]{2,1,0:T(8,128)S(1)}, f32[130,8,128]{2,1,0:T(8,128)S(1)}, f32[6,28,8,128]{3,2,1,0:T(8,128)S(1)}, f32[6,4,8,128]{3,2,1,0:T(8,128)S(1)}) custom-call(s32[6]{0:T(128)S(1)} %copy-done.2, f32[4,14]{1,0:T(4,128)S(1)} %copy-done.1, f32[23]{0:T(128)S(1)} %copy-done.3, f32[1,3,8,8,128]{4,3,2,1,0:T(8,128)S(1)} %collective-permute-done.refs_3_.refs_0_), custom_call_target="tpu_custom_call" | custom-call | flops 1 | bytes 1 | tf_op jit(solution)/shard_map/weights/pallas_call | solution.py:697
  10.2 0.0 collective-permute-done.1.refs_0_.refs_1_
  10.3 1.0 %inner.1 = (f32[6,42,3,8,128]{4,3,2,1,0:T(8,128)S(1)}, f32[6,3,6,8,128]{4,3,2,1,0:T(8,128)S(1)}) custom-call(f32[1,3,8,8,128]{4,3,2,1,0:T(8,128)S(1)} %collective-permute-done.1.refs_0_.refs_1_, f32[6,28,8,128]{3,2,1,0:T(8,128)S(1)} %get-tuple-element.26.refs_1_.refs_8_, f32[6,4,3,6,8,128]{5,4,3,2,1,0:T(8,128)S(1)} %get-tuple-element.27.refs_1_.refs_2_.refs_3_.refs_0_, ...), custom_call_target="tpu_custom_call" | custom-call | flops 1 | bytes 1 | tf_op jit(solution)/shard_map/inner/pallas_call | solution.py:707
  11.3 1.2 %collective-permute-start.2 = (f32[1,2,12,8,128]{4,3,2,1,0:T(8,128)S(1)}, f32[1,2,12,8,128]{4,3,2,1,0:T(8,128)S(1)}, u32[]{:S(2)}, u32[]{:S(2)}) collective-permute-start(f32[1,2,12,8,128]{4,3,2,1,0:T(8,128)S(1)} %send_rest.1.refs_0_), channel_id=1, source_target_pairs={{0,8},{1,2},{2,1},{3,4},{4,3},{5,6},{6,5},{7,15},{8,0},{9,10},{10,... | collective-permute-start | bytes 294920 | tf_op jit(solution)/shard_map/ppermute | solution.py:720
  12.5 0.0 collective-permute-done.4.refs_2_
  12.5 0.8 %strain.1 = (f32[6,4,3,3,8,128]{5,4,3,2,1,0:T(8,128)S(1)}, f32[6,4,8,8,128]{4,3,2,1,0:T(8,128)S(1)}, f32[6,18,8,128]{3,2,1,0:T(8,128)S(1)}) custom-call(f32[1,2,12,8,128]{4,3,2,1,0:T(8,128)S(1)} %send_rest.1.refs_0_, f32[1,6,6,8,128]{4,3,2,1,0:T(8,128)S(1)} %collective-permute-done.3.refs_1_.refs_0_, ...), custom_call_target="tpu_custom_call" | custom-call | flops 1 | bytes 1 | tf_op jit(solution)/shard_map/strain/pallas_call | solution.py:727
  13.3 1.5 %early.1.refs_12_ = f32[6,3,8,8,128]{4,3,2,1,0:T(8,128)S(1)} custom-call(f32[6,4,3,6,8,128]{5,4,3,2,1,0:T(8,128)S(1)} %get-tuple-element.27.refs_1_.refs_2_.refs_3_.refs_0_, f32[6,4,3,2,8,128]{5,4,3,2,1,0:T(8,128)S(1)} %get-tuple-element.30.refs_3_.refs_4_.refs_1_, f32[6,4,3,3,8,128]{5,4,3,2,1,0:T(8,128)S(1)} %get-tuple-element.40.refs_2_, ...), custom_call_target="tpu_custom_call" | custom-call | flops 2000000000 | bytes 1 | tf_op jit(solution)/shard_map/early/pallas_call | solution.py:737
  14.8 0.2 %collective-permute-done.5.refs_2_ = f32[1,4,12,8,128]{4,3,2,1,0:T(8,128)S(1)} collective-permute-done((f32[1,4,12,8,128]{4,3,2,1,0:T(8,128)S(1)}, f32[1,4,12,8,128]{4,3,2,1,0:T(8,128)S(1)}, u32[]{:S(2)}, u32[]{:S(2)}) %collective-permute-start.5) | collective-permute-done | bytes 196640 | tf_op jit(solution)/shard_map/ppermute | solution.py:720
  15.0 0.9 %late.1.refs_14_ = f32[3,4,64,128]{3,2,1,0:T(8,128)S(1)} custom-call(f32[1,3,8,8,128]{4,3,2,1,0:T(8,128)S(1)} %collective-permute-done.refs_3_.refs_0_, f32[1,3,8,8,128]{4,3,2,1,0:T(8,128)S(1)} %collective-permute-done.1.refs_0_.refs_1_, f32[1,4,12,8,128]{4,3,2,1,0:T(8,128)S(1)} %collective-permute-done.5.refs_2_, ...), custom_call_target="tpu_custom_call" | custom-call | flops 2000000000 | bytes 1 | tf_op jit(solution)/shard_map/late/pallas_call | solution.py:757
  15.9 0.9 %collective-permute-done.2.refs_2_ = f32[1,2,12,8,128]{4,3,2,1,0:T(8,128)S(1)} collective-permute-done((f32[1,2,12,8,128]{4,3,2,1,0:T(8,128)S(1)}, f32[1,2,12,8,128]{4,3,2,1,0:T(8,128)S(1)}, u32[]{:S(2)}, u32[]{:S(2)}) %collective-permute-start.2) | collective-permute-done | bytes 98336 | tf_op jit(solution)/shard_map/ppermute | solution.py:720
  16.9 1.2 %late_rest.1 = f32[3,6,64,128]{3,2,1,0:T(8,128)} custom-call(f32[1,3,8,8,128]{4,3,2,1,0:T(8,128)S(1)} %collective-permute-done.refs_3_.refs_0_, f32[1,3,8,8,128]{4,3,2,1,0:T(8,128)S(1)} %collective-permute-done.1.refs_0_.refs_1_, f32[1,2,12,8,128]{4,3,2,1,0:T(8,128)S(1)} %collective-permute-done.2.refs_2_, ...), custom_call_target="tpu_custom_call" | custom-call | flops 2000000000 | bytes 1 | tf_op jit(solution)/shard_map/late_rest/pallas_call | solution.py:757
  (3 shorter events, 0.1 us)
Async XLA Ops:
  0.0 1.1 %copy-start = (f32[3,6,8,1024]{3,2,1,0:T(8,128)S(1)}, f32[3,6,8,1024]{3,2,1,0:T(8,128)}, u32[]{:S(2)}) copy-start(f32[3,6,8,1024]{3,2,1,0:T(8,128)} %param.4) | copy-start | bytes 1769476
  1.1 6.4 %collective-permute-start.3 = (f32[1,6,6,8,128]{4,3,2,1,0:T(8,128)S(1)}, f32[1,6,6,8,128]{4,3,2,1,0:T(8,128)S(1)}, u32[]{:S(2)}, u32[]{:S(2)}) collective-permute-start(f32[1,6,6,8,128]{4,3,2,1,0:T(8,128)S(1)} %pack.1.refs_0_), channel_id=1, source_target_pairs={{0,1},{1,0},{2,3},{3,2},{4,5},{5,4},{6,7},{7,6},{8,9},{9,8},{10,11... | collective-permute-start | bytes 442376 | tf_op jit(solution)/shard_map/ppermute | solution.py:672
  3.7 8.8 %collective-permute-start.4 = (f32[1,6,6,8,128]{4,3,2,1,0:T(8,128)S(1)}, f32[1,6,6,8,128]{4,3,2,1,0:T(8,128)S(1)}, u32[]{:S(2)}, u32[]{:S(2)}) collective-permute-start(f32[1,6,6,8,128]{4,3,2,1,0:T(8,128)S(1)} %get-tuple-element.39), channel_id=1, source_target_pairs={{0,1},{1,0},{2,3},{3,2},{4,5},{5,4},{6,7},{7,6},{8,9},{9,8},{10,11... | collective-permute-start | bytes 442376 | tf_op jit(solution)/shard_map/ppermute | solution.py:683
  4.3 5.1 %collective-permute-start = (f32[1,3,8,8,128]{4,3,2,1,0:T(8,128)S(1)}, f32[1,3,8,8,128]{4,3,2,1,0:T(8,128)S(1)}, u32[]{:S(2)}, u32[]{:S(2)}) collective-permute-start(f32[1,3,8,8,128]{4,3,2,1,0:T(8,128)S(1)} %get-tuple-element.24), channel_id=1, source_target_pairs={{0,8},{8,0},{16,24},{24,16},{1,9},{9,1},{17,25},{25,17},{2,10},{10... | collective-permute-start | bytes 294920 | tf_op jit(solution)/shard_map/ppermute | solution.py:685
  4.3 5.9 %collective-permute-start.1 = (f32[1,3,8,8,128]{4,3,2,1,0:T(8,128)S(1)}, f32[1,3,8,8,128]{4,3,2,1,0:T(8,128)S(1)}, u32[]{:S(2)}, u32[]{:S(2)}) collective-permute-start(f32[1,3,8,8,128]{4,3,2,1,0:T(8,128)S(1)} %get-tuple-element.25), channel_id=1, source_target_pairs={{8,16},{16,8},{0,24},{24,0},{9,17},{17,9},{1,25},{25,1},{10,18},{1... | collective-permute-start | bytes 294920 | tf_op jit(solution)/shard_map/ppermute | solution.py:684
  5.9 3.5 %copy-start.1 = (f32[4,14]{1,0:T(4,128)S(1)}, f32[4,14]{1,0:T(4,128)}, u32[]{:S(2)}) copy-start(f32[4,14]{1,0:T(4,128)} %refs_1_.1) | copy-start | bytes 676
  5.9 3.5 %copy-start.2 = (s32[6]{0:T(128)S(1)}, s32[6]{0:T(128)}, u32[]{:S(2)}) copy-start(s32[6]{0:T(128)} %refs_0_.1) | copy-start | bytes 76
  5.9 3.5 %copy-start.3 = (f32[23]{0:T(128)S(1)}, f32[23]{0:T(128)}, u32[]{:S(2)}) copy-start(f32[23]{0:T(128)} %refs_2_.1) | copy-start | bytes 280
  7.6 7.5 %collective-permute-start.5 = (f32[1,4,12,8,128]{4,3,2,1,0:T(8,128)S(1)}, f32[1,4,12,8,128]{4,3,2,1,0:T(8,128)S(1)}, u32[]{:S(2)}, u32[]{:S(2)}) collective-permute-start(f32[1,4,12,8,128]{4,3,2,1,0:T(8,128)S(1)} %send.1), channel_id=1, source_target_pairs={{0,8},{1,2},{2,1},{3,4},{4,3},{5,6},{6,5},{7,15},{8,0},{9,10},{10,... | collective-permute-start | bytes 589832 | tf_op jit(solution)/shard_map/ppermute | solution.py:720
  11.3 5.6 %collective-permute-start.2 = (f32[1,2,12,8,128]{4,3,2,1,0:T(8,128)S(1)}, f32[1,2,12,8,128]{4,3,2,1,0:T(8,128)S(1)}, u32[]{:S(2)}, u32[]{:S(2)}) collective-permute-start(f32[1,2,12,8,128]{4,3,2,1,0:T(8,128)S(1)} %send_rest.1.refs_0_), channel_id=1, source_target_pairs={{0,8},{1,2},{2,1},{3,4},{4,3},{5,6},{6,5},{7,15},{8,0},{9,10},{10,... | collective-permute-start | bytes 294920 | tf_op jit(solution)/shard_map/ppermute | solution.py:720

commit v6 on v5

--- a/solution.py
+++ b/solution.py
@@ -30,8 +30,6 @@
 
 COLUMNS = bond_columns()
 BONDS = {0: (1, 2, 3), 1: (-2, -1, 0, 1, 2), 2: (-2, -1, 0, 1, 2), 3: (0,)}
-
-
 OFFSETS = [(a, b) for b, offsets in BONDS.items() for a in offsets]
 
 
@@ -238,7 +236,7 @@
                 message[0, p, x - plan.near_a.start] = base_ref[p, 2, x - REACH]
                 message[0, p, REACH + x - plan.near_a.start] = sums[x]
 
-    for_plies(plies, 2, ply)
+    for_plies(plies, 3, ply)
     upper = lax.axis_index("ply") % 2 == 1
     for c in range(3):
         for x in range(plan.cols):
@@ -453,7 +451,7 @@
             for b, moved in grid.ahead(strain).items():
                 strains.put(x, moved, b)
 
-    for_plies(plies, 2, ply)
+    for_plies(plies, 3, ply)
 
 
 def cross_mask_a(grid, tiles):

time: 18.2 us -> 18.2 us (level)
  transfers between devices with their start and end apart: 6 -> 6, of which waited for: 3 -> 3; matrix products, arithmetic and copies ran while one was open for 0% -> 0% of each run, Pallas kernels for 39% -> 38%
where the time goes in v6:
time: 18.2 us; the launch traced here: 18 us
  Pallas kernels  8.01 us (44%)
  starting transfers between devices  6.82 us (37%)
  waiting for transfers between devices  2.06 us (11%)
  local copies, waits for them, and re-layouts  1.07 us (6%)
    ppermute x2, starting transfers between devices, send_part(): return (message, lax.ppermute(message, ('ply', 'tile'), swap_b))  3.06 us
    pallas_call x2, Pallas kernels, local(): call(lambda *refs: late_kernel(plan, tiles, part, final, *refs), 'late_re...  2.06 us
    ppermute x1, starting transfers between devices, local(): got_second = lax.ppermute(second, 'ply', swap_second)  1.6 us
    ppermute x1, starting transfers between devices, local(): got_a = lax.ppermute(message_a, 'tile', swap_a)  1.58 us
    pallas_call x1, Pallas kernels, local(): call(lambda *refs: early_kernel(plan, tiles, *refs), 'early', [whole] * 1...  1.5 us
    ppermute x2, waiting for transfers between devices, send_part(): return (message, lax.ppermute(message, ('ply', 'tile'), swap_b))  1.25 us
    unnamed x8, local copies, waits for them, and re-layouts  1.07 us
    pallas_call x1, Pallas kernels, local(): call(lambda *refs: inner_kernel(plan, *refs), 'inner', [whole] * 7, [arra...  1.04 us
  transfers between devices with their start and end apart: 6, of which 3 were waited for; matrix products, arithmetic and copies ran while one was open for 0% of the time, Pallas kernels for 38%

profile of v6, /device:TPU:8, one launch (start us, length us, event | category | flops | bytes accessed | tf_op | source)
XLA Modules:
  0.0 18.0 jit_solution(13991204698884690254)
XLA Ops:
  0.0 0.0 copy-start
  0.0 1.1 %copy-done = f32[3,6,8,1024]{3,2,1,0:T(8,128)S(1)} copy-done((f32[3,6,8,1024]{3,2,1,0:T(8,128)S(1)}, f32[3,6,8,1024]{3,2,1,0:T(8,128)}, u32[]{:S(2)}) %copy-start) | copy-done | bytes 589848
  1.1 1.6 %collective-permute-start.3 = (f32[1,6,6,8,128]{4,3,2,1,0:T(8,128)S(1)}, f32[1,6,6,8,128]{4,3,2,1,0:T(8,128)S(1)}, u32[]{:S(2)}, u32[]{:S(2)}) collective-permute-start(f32[1,6,6,8,128]{4,3,2,1,0:T(8,128)S(1)} %pack.1.refs_0_), channel_id=1, source_target_pairs={{0,1},{1,0},{2,3},{3,2},{4,5},{5,4},{6,7},{7,6},{8,9},{9,8},{10,11... | collective-permute-start | bytes 442376 | tf_op jit(solution)/shard_map/ppermute | solution.py:670
  2.7 1.0 %near_a.1 = (f32[1,6,6,8,128]{4,3,2,1,0:T(8,128)S(1)}, f32[6,3,8,8,128]{4,3,2,1,0:T(8,128)S(1)}, f32[6,4,3,6,8,128]{5,4,3,2,1,0:T(8,128)S(1)}, f32[6,6,8,128]{3,...) custom-call(f32[1,6,6,8,128]{4,3,2,1,0:T(8,128)S(1)} %pack.1.refs_0_, ...), custom_call_target="tpu_custom_call" | custom-call | flops 1 | bytes 1 | tf_op jit(solution)/shard_map/near_a/pallas_call | solution.py:672
  3.7 0.6 %collective-permute-start.4 = (f32[1,6,6,8,128]{4,3,2,1,0:T(8,128)S(1)}, f32[1,6,6,8,128]{4,3,2,1,0:T(8,128)S(1)}, u32[]{:S(2)}, u32[]{:S(2)}) collective-permute-start(f32[1,6,6,8,128]{4,3,2,1,0:T(8,128)S(1)} %get-tuple-element.39), channel_id=1, source_target_pairs={{0,1},{1,0},{2,3},{3,2},{4,5},{5,4},{6,7},{7,6},{8,9},{9,8},{10,11... | collective-permute-start | bytes 442376 | tf_op jit(solution)/shard_map/ppermute | solution.py:681
  4.3 0.0 collective-permute-start
  4.3 1.6 %collective-permute-start.1 = (f32[1,3,8,8,128]{4,3,2,1,0:T(8,128)S(1)}, f32[1,3,8,8,128]{4,3,2,1,0:T(8,128)S(1)}, u32[]{:S(2)}, u32[]{:S(2)}) collective-permute-start(f32[1,3,8,8,128]{4,3,2,1,0:T(8,128)S(1)} %get-tuple-element.25), channel_id=1, source_target_pairs={{8,16},{16,8},{0,24},{24,0},{9,17},{17,9},{1,25},{25,1},{10,18},{1... | collective-permute-start | bytes 294920 | tf_op jit(solution)/shard_map/ppermute | solution.py:682
  5.9 0.0 copy-start.1
  5.9 0.0 copy-start.2
  5.9 0.0 copy-start.3
  5.9 0.9 %near_b.1 = (f32[6,4,3,2,8,128]{5,4,3,2,1,0:T(8,128)S(1)}, f32[6,5,8,128]{3,2,1,0:T(8,128)S(1)}, f32[6,52,8,128]{3,2,1,0:T(8,128)S(1)}) custom-call(f32[6,3,8,8,128]{4,3,2,1,0:T(8,128)S(1)} %get-tuple-element.28.refs_0_.refs_1_, f32[6,4,3,6,8,128]{5,4,3,2,1,0:T(8,128)S(1)} %get-tuple-element.27.refs_1_.refs_2_.refs_3_.refs_0_, ...), custom_call_target="tpu_custom_call" | custom-call | flops 1 | bytes 1 | tf_op jit(solution)/shard_map/near_b/pallas_call | solution.py:685
  6.8 0.8 %collective-permute-done.3.refs_1_.refs_0_ = f32[1,6,6,8,128]{4,3,2,1,0:T(8,128)S(1)} collective-permute-done((f32[1,6,6,8,128]{4,3,2,1,0:T(8,128)S(1)}, f32[1,6,6,8,128]{4,3,2,1,0:T(8,128)S(1)}, u32[]{:S(2)}, u32[]{:S(2)}) %collective-permute-start.3) | collective-permute-done | bytes 147488 | tf_op jit(solution)/shard_map/ppermute | solution.py:670
  7.6 1.8 %collective-permute-start.5 = (f32[1,4,12,8,128]{4,3,2,1,0:T(8,128)S(1)}, f32[1,4,12,8,128]{4,3,2,1,0:T(8,128)S(1)}, u32[]{:S(2)}, u32[]{:S(2)}) collective-permute-start(f32[1,4,12,8,128]{4,3,2,1,0:T(8,128)S(1)} %send.1), channel_id=1, source_target_pairs={{0,8},{1,2},{2,1},{3,4},{4,3},{5,6},{6,5},{7,15},{8,0},{9,10},{10,... | collective-permute-start | bytes 589832 | tf_op jit(solution)/shard_map/ppermute | solution.py:718
  9.4 0.0 collective-permute-done.refs_3_.refs_0_
  9.4 0.0 copy-done.1
  9.4 0.0 copy-done.2
  9.4 0.0 copy-done.3
  9.4 0.8 %weights.1 = (f32[14,8,128]{2,1,0:T(8,128)S(1)}, f32[130,8,128]{2,1,0:T(8,128)S(1)}, f32[6,28,8,128]{3,2,1,0:T(8,128)S(1)}, f32[6,4,8,128]{3,2,1,0:T(8,128)S(1)}) custom-call(s32[6]{0:T(128)S(1)} %copy-done.2, f32[4,14]{1,0:T(4,128)S(1)} %copy-done.1, f32[23]{0:T(128)S(1)} %copy-done.3, f32[1,3,8,8,128]{4,3,2,1,0:T(8,128)S(1)} %collective-permute-done.refs_3_.refs_0_), custom_call_target="tpu_custom_call" | custom-call | flops 1 | bytes 1 | tf_op jit(solution)/shard_map/weights/pallas_call | solution.py:695
  10.2 0.0 collective-permute-done.1.refs_0_.refs_1_
  10.3 1.0 %inner.1 = (f32[6,42,3,8,128]{4,3,2,1,0:T(8,128)S(1)}, f32[6,3,6,8,128]{4,3,2,1,0:T(8,128)S(1)}) custom-call(f32[1,3,8,8,128]{4,3,2,1,0:T(8,128)S(1)} %collective-permute-done.1.refs_0_.refs_1_, f32[6,28,8,128]{3,2,1,0:T(8,128)S(1)} %get-tuple-element.26.refs_1_.refs_8_, f32[6,4,3,6,8,128]{5,4,3,2,1,0:T(8,128)S(1)} %get-tuple-element.27.refs_1_.refs_2_.refs_3_.refs_0_, ...), custom_call_target="tpu_custom_call" | custom-call | flops 1 | bytes 1 | tf_op jit(solution)/shard_map/inner/pallas_call | solution.py:705
  11.3 1.3 %collective-permute-start.2 = (f32[1,2,12,8,128]{4,3,2,1,0:T(8,128)S(1)}, f32[1,2,12,8,128]{4,3,2,1,0:T(8,128)S(1)}, u32[]{:S(2)}, u32[]{:S(2)}) collective-permute-start(f32[1,2,12,8,128]{4,3,2,1,0:T(8,128)S(1)} %send_rest.1.refs_0_), channel_id=1, source_target_pairs={{0,8},{1,2},{2,1},{3,4},{4,3},{5,6},{6,5},{7,15},{8,0},{9,10},{10,... | collective-permute-start | bytes 294920 | tf_op jit(solution)/shard_map/ppermute | solution.py:718
  12.6 0.0 collective-permute-done.4.refs_2_
  12.6 0.7 %strain.1 = (f32[6,4,3,3,8,128]{5,4,3,2,1,0:T(8,128)S(1)}, f32[6,4,8,8,128]{4,3,2,1,0:T(8,128)S(1)}, f32[6,18,8,128]{3,2,1,0:T(8,128)S(1)}) custom-call(f32[1,2,12,8,128]{4,3,2,1,0:T(8,128)S(1)} %send_rest.1.refs_0_, f32[1,6,6,8,128]{4,3,2,1,0:T(8,128)S(1)} %collective-permute-done.3.refs_1_.refs_0_, ...), custom_call_target="tpu_custom_call" | custom-call | flops 1 | bytes 1 | tf_op jit(solution)/shard_map/strain/pallas_call | solution.py:725
  13.2 1.5 %early.1.refs_12_ = f32[6,3,8,8,128]{4,3,2,1,0:T(8,128)S(1)} custom-call(f32[6,4,3,6,8,128]{5,4,3,2,1,0:T(8,128)S(1)} %get-tuple-element.27.refs_1_.refs_2_.refs_3_.refs_0_, f32[6,4,3,2,8,128]{5,4,3,2,1,0:T(8,128)S(1)} %get-tuple-element.30.refs_3_.refs_4_.refs_1_, f32[6,4,3,3,8,128]{5,4,3,2,1,0:T(8,128)S(1)} %get-tuple-element.40.refs_2_, ...), custom_call_target="tpu_custom_call" | custom-call | flops 2000000000 | bytes 1 | tf_op jit(solution)/shard_map/early/pallas_call | solution.py:735
  14.7 0.3 %collective-permute-done.5.refs_2_ = f32[1,4,12,8,128]{4,3,2,1,0:T(8,128)S(1)} collective-permute-done((f32[1,4,12,8,128]{4,3,2,1,0:T(8,128)S(1)}, f32[1,4,12,8,128]{4,3,2,1,0:T(8,128)S(1)}, u32[]{:S(2)}, u32[]{:S(2)}) %collective-permute-start.5) | collective-permute-done | bytes 196640 | tf_op jit(solution)/shard_map/ppermute | solution.py:718
  15.0 0.9 %late.1.refs_14_ = f32[3,4,64,128]{3,2,1,0:T(8,128)S(1)} custom-call(f32[1,3,8,8,128]{4,3,2,1,0:T(8,128)S(1)} %collective-permute-done.refs_3_.refs_0_, f32[1,3,8,8,128]{4,3,2,1,0:T(8,128)S(1)} %collective-permute-done.1.refs_0_.refs_1_, f32[1,4,12,8,128]{4,3,2,1,0:T(8,128)S(1)} %collective-permute-done.5.refs_2_, ...), custom_call_target="tpu_custom_call" | custom-call | flops 2000000000 | bytes 1 | tf_op jit(solution)/shard_map/late/pallas_call | solution.py:755
  15.9 1.0 %collective-permute-done.2.refs_2_ = f32[1,2,12,8,128]{4,3,2,1,0:T(8,128)S(1)} collective-permute-done((f32[1,2,12,8,128]{4,3,2,1,0:T(8,128)S(1)}, f32[1,2,12,8,128]{4,3,2,1,0:T(8,128)S(1)}, u32[]{:S(2)}, u32[]{:S(2)}) %collective-permute-start.2) | collective-permute-done | bytes 98336 | tf_op jit(solution)/shard_map/ppermute | solution.py:718
  16.9 1.2 %late_rest.1 = f32[3,6,64,128]{3,2,1,0:T(8,128)} custom-call(f32[1,3,8,8,128]{4,3,2,1,0:T(8,128)S(1)} %collective-permute-done.refs_3_.refs_0_, f32[1,3,8,8,128]{4,3,2,1,0:T(8,128)S(1)} %collective-permute-done.1.refs_0_.refs_1_, f32[1,2,12,8,128]{4,3,2,1,0:T(8,128)S(1)} %collective-permute-done.2.refs_2_, ...), custom_call_target="tpu_custom_call" | custom-call | flops 2000000000 | bytes 1 | tf_op jit(solution)/shard_map/late_rest/pallas_call | solution.py:755
  (3 shorter events, 0.1 us)
Async XLA Ops:
  0.0 1.1 %copy-start = (f32[3,6,8,1024]{3,2,1,0:T(8,128)S(1)}, f32[3,6,8,1024]{3,2,1,0:T(8,128)}, u32[]{:S(2)}) copy-start(f32[3,6,8,1024]{3,2,1,0:T(8,128)} %param.4) | copy-start | bytes 1769476
  1.1 6.5 %collective-permute-start.3 = (f32[1,6,6,8,128]{4,3,2,1,0:T(8,128)S(1)}, f32[1,6,6,8,128]{4,3,2,1,0:T(8,128)S(1)}, u32[]{:S(2)}, u32[]{:S(2)}) collective-permute-start(f32[1,6,6,8,128]{4,3,2,1,0:T(8,128)S(1)} %pack.1.refs_0_), channel_id=1, source_target_pairs={{0,1},{1,0},{2,3},{3,2},{4,5},{5,4},{6,7},{7,6},{8,9},{9,8},{10,11... | collective-permute-start | bytes 442376 | tf_op jit(solution)/shard_map/ppermute | solution.py:670
  3.7 8.9 %collective-permute-start.4 = (f32[1,6,6,8,128]{4,3,2,1,0:T(8,128)S(1)}, f32[1,6,6,8,128]{4,3,2,1,0:T(8,128)S(1)}, u32[]{:S(2)}, u32[]{:S(2)}) collective-permute-start(f32[1,6,6,8,128]{4,3,2,1,0:T(8,128)S(1)} %get-tuple-element.39), channel_id=1, source_target_pairs={{0,1},{1,0},{2,3},{3,2},{4,5},{5,4},{6,7},{7,6},{8,9},{9,8},{10,11... | collective-permute-start | bytes 442376 | tf_op jit(solution)/shard_map/ppermute | solution.py:681
  4.3 5.1 %collective-permute-start = (f32[1,3,8,8,128]{4,3,2,1,0:T(8,128)S(1)}, f32[1,3,8,8,128]{4,3,2,1,0:T(8,128)S(1)}, u32[]{:S(2)}, u32[]{:S(2)}) collective-permute-start(f32[1,3,8,8,128]{4,3,2,1,0:T(8,128)S(1)} %get-tuple-element.24), channel_id=1, source_target_pairs={{0,8},{8,0},{16,24},{24,16},{1,9},{9,1},{17,25},{25,17},{2,10},{10... | collective-permute-start | bytes 294920 | tf_op jit(solution)/shard_map/ppermute | solution.py:683
  4.3 6.0 %collective-permute-start.1 = (f32[1,3,8,8,128]{4,3,2,1,0:T(8,128)S(1)}, f32[1,3,8,8,128]{4,3,2,1,0:T(8,128)S(1)}, u32[]{:S(2)}, u32[]{:S(2)}) collective-permute-start(f32[1,3,8,8,128]{4,3,2,1,0:T(8,128)S(1)} %get-tuple-element.25), channel_id=1, source_target_pairs={{8,16},{16,8},{0,24},{24,0},{9,17},{17,9},{1,25},{25,1},{10,18},{1... | collective-permute-start | bytes 294920 | tf_op jit(solution)/shard_map/ppermute | solution.py:682
  5.9 3.5 %copy-start.1 = (f32[4,14]{1,0:T(4,128)S(1)}, f32[4,14]{1,0:T(4,128)}, u32[]{:S(2)}) copy-start(f32[4,14]{1,0:T(4,128)} %refs_1_.1) | copy-start | bytes 676
  5.9 3.5 %copy-start.2 = (s32[6]{0:T(128)S(1)}, s32[6]{0:T(128)}, u32[]{:S(2)}) copy-start(s32[6]{0:T(128)} %refs_0_.1) | copy-start | bytes 76
  5.9 3.5 %copy-start.3 = (f32[23]{0:T(128)S(1)}, f32[23]{0:T(128)}, u32[]{:S(2)}) copy-start(f32[23]{0:T(128)} %refs_2_.1) | copy-start | bytes 280
  7.6 7.4 %collective-permute-start.5 = (f32[1,4,12,8,128]{4,3,2,1,0:T(8,128)S(1)}, f32[1,4,12,8,128]{4,3,2,1,0:T(8,128)S(1)}, u32[]{:S(2)}, u32[]{:S(2)}) collective-permute-start(f32[1,4,12,8,128]{4,3,2,1,0:T(8,128)S(1)} %send.1), channel_id=1, source_target_pairs={{0,8},{1,2},{2,1},{3,4},{4,3},{5,6},{6,5},{7,15},{8,0},{9,10},{10,... | collective-permute-start | bytes 589832 | tf_op jit(solution)/shard_map/ppermute | solution.py:718
  11.3 5.6 %collective-permute-start.2 = (f32[1,2,12,8,128]{4,3,2,1,0:T(8,128)S(1)}, f32[1,2,12,8,128]{4,3,2,1,0:T(8,128)S(1)}, u32[]{:S(2)}, u32[]{:S(2)}) collective-permute-start(f32[1,2,12,8,128]{4,3,2,1,0:T(8,128)S(1)} %send_rest.1.refs_0_), channel_id=1, source_target_pairs={{0,8},{1,2},{2,1},{3,4},{4,3},{5,6},{6,5},{7,15},{8,0},{9,10},{10,... | collective-permute-start | bytes 294920 | tf_op jit(solution)/shard_map/ppermute | solution.py:718

commit v7 on v6

--- a/solution.py
+++ b/solution.py
@@ -164,7 +164,7 @@
             sep = separation(rows, b, a, i, here)
             q = sep[0] * sep[0] + sep[1] * sep[1] + sep[2] * sep[2]
             r = lax.rsqrt(q)
-            keep((b, a, i), r)
+            keep((b, a, i), r, sep)
             e = q * r - length_of(a, b)
             mask = mask_of(b)
             if mask is not None:
@@ -226,7 +226,7 @@
             if x >= plan.start_a:
                 keep_row(grid, rows, x, row)
 
-        def keep(key, r):
+        def keep(key, r, sep):
             inverse_ref[p, slots[key]] = r
 
         sums = extension_sums(grid, rows, plan.inner_a, grid.exists.get, keep)
@@ -259,7 +259,7 @@
         for x in fresh:
             keep_row(grid, rows, x, [base_ref[p, c, x - REACH] for c in range(3)])
 
-        def keep(key, r):
+        def keep(key, r, sep):
             inverse_ref[p, slots[key]] = r
 
         sums = extension_sums(grid, rows, plan.inner_b, grid.exists.get, keep)
@@ -349,9 +349,13 @@
 
 def whole_push(rows, strains, factors, inverse, pair, mask_of, key):
     b, a, i = key
+    sep = separation(rows, b, a, i, [rows.get(i, 0, c) for c in range(3)])
+    return push_from(strains, factors, inverse(key), sep, pair, mask_of, key)
+
+
+def push_from(strains, factors, r, sep, pair, mask_of, key):
+    b, a, i = key
     alpha, beta = factors(a, b)
-    sep = separation(rows, b, a, i, [rows.get(i, 0, c) for c in range(3)])
-    r = inverse(key)
     f = (alpha * r) * (strains.get(i, 0) + strains.get(i + a, b)) + (beta * pair(key)) * (1.0 - length_of(a, b) * r)
     mask = mask_of(b)
     if mask is not None:
@@ -433,7 +437,7 @@
             row = [got_ref[0, p, j], got_ref[0, p, REACH + j], got_more_ref[0, p, j]]
             keep_row(grid, rows, plan.wide - 1 - j, [-row[0], row[1], row[2]])
 
-        def keep(key, r):
+        def keep(key, r, sep):
             inverse_ref[p, in_cross[key]] = r
 
         sums = extension_sums(grid, rows, plan.cross_a, mask_of, keep)
@@ -463,7 +467,7 @@
 
 def early_kernel(
     plan, tiles, rows_a_ref, rows_b_ref, halo_ref, strain_ref, inverse_ref, inverse_a_ref, inverse_b_ref, pair_ref,
-    factor_ref, spring_ref, force_ref,
+    factor_ref, spring_ref, inner_ref, first_ref, second_ref, force_ref,
 ):
     plies = rows_a_ref.shape[0]
     grid = Grid(rows_a_ref.shape[-2])
@@ -473,6 +477,7 @@
     in_pair = {key: n for n, key in enumerate(plan.early + plan.late)}
     start = 2 * REACH
     cross_mask = cross_mask_a(grid, tiles)
+    late = plan.span(plan.inner_late)
 
     def ply(p):
         def rows_of(q, *more):
@@ -491,6 +496,8 @@
             for c in range(3):
                 here = rows.get(x, 0, c)
                 spring = up * (over.get(x, 0, c) - here) + down * (under.get(x, 0, c) - here)
+                if x in late:
+                    spring = spring + inner_ref[p, c, x - REACH]
                 force_ref[p, c, x - REACH] = spring
 
         def inverse(key):
@@ -509,34 +516,37 @@
         collect(plan, grid, plan.early, push_of, force)
 
     for_plies(plies, 2, ply)
+    upper = lax.axis_index("ply") % 2 == 1
+    for p, n, one, two in ((plies - 1, 0, second_ref, first_ref), (0, 1, first_ref, second_ref)):
+        rows = Store(
+            (rows_b_ref, REACH, range(REACH, plan.start_a), (p,)),
+            (rows_a_ref, plan.start_a, range(plan.start_a, plan.own.stop), (p,)),
+        )
+        for c in range(3):
+            for x in plan.own:
+                at = (p, c, x - REACH)
+                beyond = jnp.where(upper, one[0, c, x - REACH], two[0, c, x - REACH])
+                force_ref[at] = force_ref[at] + spring_ref[p, n] * (beyond - rows.get(x, 0, c))
 
 
 def late_kernel(
-    plan, tiles, part, final, first_ref, second_ref, got_ref, rows_a_ref, rows_b_ref, sums_b_ref, weight_ref, pair_ref,
-    factor_ref, spring_ref, vector_ref, inner_ref, force_in_ref, strain_a_ref, *rest,
+    plan, tiles, part, final, got_ref, rows_a_ref, rows_b_ref, sums_b_ref, weight_ref, pair_ref,
+    factor_ref, vector_ref, force_in_ref, strain_a_ref, *rest,
 ):
     if final:
-        before_ref, out_hbm, halo_ref, cross_ref, strain_ref, force_ref, out_ref, sems, before_sem = rest
+        before_ref, out_hbm, halo_ref, strain_ref, force_ref, out_ref, out_sem, before_sem = rest
         copy_before = pltpu.make_async_copy(before_ref, out_hbm.at[:, pl.ds(0, part.start)], before_sem)
         copy_before.start()
     else:
-        out_ref, halo_ref, cross_ref, strain_ref, force_ref = rest
+        out_ref, halo_ref, strain_ref, force_ref = rest
     plies = rows_a_ref.shape[0]
     grid = Grid(rows_a_ref.shape[-2])
     odd, sign = frame()
-    upper = lax.axis_index("ply") % 2 == 1
-    in_cross = {key: n for n, key in enumerate(plan.cross_b)}
     in_pair = {key: n for n, key in enumerate(plan.early + plan.late)}
     in_vector = {key: n for n, key in enumerate(plan.inner_late)}
     start = 2 * REACH
     has_b = jnp.ones((grid.subs, LANES), jnp.int32) * sides(tiles)[1].astype(jnp.int32) > 0
     cross_masks = {b: grid.exists[b] & has_b if b else has_b for b in range(REACH + 1)}
-    late = plan.span(plan.inner_late)
-
-    def copy_out(p):
-        return pltpu.make_async_copy(
-            out_ref.at[:, pl.ds(p - part.start, 1)], out_hbm.at[:, pl.ds(p, 1)], sems.at[p - part.start]
-        )
 
     def ply(p):
         n = p - part.start
@@ -553,8 +563,10 @@
             row = [got_ref[0, n, c * REACH + j] for c in range(3)]
             keep_row(grid, rows, REACH - 1 - j, [-row[0], row[1], row[2]])
 
-        def keep(key, r):
-            cross_ref[n, in_cross[key]] = r
+        crossed = {}
+
+        def keep(key, r, sep):
+            crossed[key] = r, sep
 
         sums = extension_sums(grid, rows, plan.cross_b, cross_masks.get, keep)
         for x in range(start):
@@ -563,27 +575,14 @@
             strains.put(x, strain, 0)
             for b, moved in grid.ahead(strain).items():
                 strains.put(x, moved, b)
-        faces = []
-        if p == plies - 1:
-            faces.append((spring_ref[p, 0], second_ref, first_ref))
-        if p == 0:
-            faces.append((spring_ref[p, 1], first_ref, second_ref))
         for c in range(3):
             for x in plan.own:
-                value = force_in_ref[p, c, x - REACH]
-                if x in late:
-                    value = value + inner_ref[p, c, x - REACH]
-                for factor, one, two in faces:
-                    beyond = jnp.where(upper, one[0, c, x - REACH], two[0, c, x - REACH])
-                    value = value + factor * (beyond - rows.get(x, 0, c))
-                force_ref[n, c, x - REACH] = value
+                force_ref[n, c, x - REACH] = force_in_ref[p, c, x - REACH]
 
         def push_of(key):
-            if key in in_cross:
-                return whole_push(
-                    rows, strains, factors, lambda k: cross_ref[n, in_cross[k]], lambda k: pair_ref[in_pair[k]],
-                    cross_masks.get, key,
-                )
+            if key in crossed:
+                r, sep = crossed[key]
+                return push_from(strains, factors, r, sep, lambda k: pair_ref[in_pair[k]], cross_masks.get, key)
             b, a, i = key
             total = strains.get(i, 0) + strains.get(i + a, b)
             return [vector_ref[p, in_vector[key], c] * total for c in range(3)]
@@ -599,17 +598,13 @@
                 value = force_ref[n, c, x - REACH]
                 out_ref[c, n, pl.ds(at, grid.subs, stride=plan.cols), :] = value * sign if c == 0 else value
 
-    for first in range(part.start, part.stop, 2):
-        group = range(first, min(first + 2, part.stop))
-        for p in group:
-            ply(p)
-        if final:
-            for p in group:
-                copy_out(p).start()
+    for p in part:
+        ply(p)
     if final:
+        copy_out = pltpu.make_async_copy(out_ref, out_hbm.at[:, pl.ds(part.start, len(part))], out_sem)
+        copy_out.start()
         copy_before.wait()
-        for p in part:
-            copy_out(p).wait()
+        copy_out.wait()
 
 
 def local(displacement, angle_index, bond_table, interface_stiffness):
@@ -735,34 +730,36 @@
     (force,) = call(
         lambda *refs: early_kernel(plan, tiles, *refs),
         "early",
-        [whole] * 10,
+        [whole] * 13,
         [array(plies, 3, cols)],
         cost=EARLY_COST,
-    )(rows_a, rows_b, halo_a, strain, inverse_cross, inverse_a, inverse_b, pair, factor, spring)
+    )(
+        rows_a, rows_b, halo_a, strain, inverse_cross, inverse_a, inverse_b, pair, factor, spring, inner_late,
+        got_first, got_second,
+    )
 
     out = []
     for part, got in zip(parts, got_b):
         final = part.stop == plies
         result = jax.ShapeDtypeStruct((comps, len(part), *view.shape[2:]), jnp.float32)
         scratches = [
-            scratch(len(part), REACH + 1, 3, REACH), scratch(len(part), len(plan.cross_b)),
-            scratch(len(part), REACH + 1, 2 * REACH), scratch(len(part), 3, cols),
+            scratch(len(part), REACH + 1, 3, REACH), scratch(len(part), REACH + 1, 2 * REACH),
+            scratch(len(part), 3, cols),
         ]
         if final:
             scratches += [
-                pltpu.VMEM(result.shape, jnp.float32), pltpu.SemaphoreType.DMA((len(part),)), pltpu.SemaphoreType.DMA,
+                pltpu.VMEM(result.shape, jnp.float32), pltpu.SemaphoreType.DMA, pltpu.SemaphoreType.DMA,
             ]
         out = call(
             lambda *refs: late_kernel(plan, tiles, part, final, *refs),
             "late_rest" if final else "late",
-            [whole] * (14 + len(out)),
+            [whole] * (10 + len(out)),
             [jax.ShapeDtypeStruct(view.shape, jnp.float32) if final else result],
             out_specs=[pl.BlockSpec(memory_space=pltpu.HBM)] if final else None,
             scratches=scratches,
             cost=LATE_COST,
         )(
-            got_first, got_second, got, rows_a, rows_b, sums_b, weight, pair, factor, spring, vector_late, inner_late,
-            force, strain, *out,
+            got, rows_a, rows_b, sums_b, weight, pair, factor, vector_late, force, strain, *out,
         )
     (out,) = out
     return (

time: 18.2 us -> 18.2 us (level)
  no operation moved by 1% of the time
where the time goes in v7:
time: 18.2 us; the launch traced here: 18 us
  Pallas kernels  8.02 us (44%)
  starting transfers between devices  6.82 us (37%)
  waiting for transfers between devices  2.04 us (11%)
  local copies, waits for them, and re-layouts  1.07 us (6%)
    ppermute x2, starting transfers between devices, send_part(): return (message, lax.ppermute(message, ('ply', 'tile'), swap_b))  3.06 us
    pallas_call x2, Pallas kernels, local(): call(lambda *refs: late_kernel(plan, tiles, part, final, *refs), 'late_re...  1.97 us
    ppermute x1, starting transfers between devices, local(): got_second = lax.ppermute(second, 'ply', swap_second)  1.6 us
    pallas_call x1, Pallas kernels, local(): call(lambda *refs: early_kernel(plan, tiles, *refs), 'early', [whole] * 1...  1.6 us
    ppermute x1, starting transfers between devices, local(): got_a = lax.ppermute(message_a, 'tile', swap_a)  1.58 us
    ppermute x2, waiting for transfers between devices, send_part(): return (message, lax.ppermute(message, ('ply', 'tile'), swap_b))  1.22 us
    unnamed x8, local copies, waits for them, and re-layouts  1.07 us
    pallas_call x1, Pallas kernels, local(): call(lambda *refs: inner_kernel(plan, *refs), 'inner', [whole] * 7, [arra...  1.04 us
  transfers between devices with their start and end apart: 6, of which 3 were waited for; matrix products, arithmetic and copies ran while one was open for 0% of the time, Pallas kernels for 38%

profile of v7, /device:TPU:8, one launch (start us, length us, event | category | flops | bytes accessed | tf_op | source)
XLA Modules:
  0.0 18.0 jit_solution(17401535094409045351)
XLA Ops:
  0.0 0.0 copy-start
  0.0 1.1 %copy-done = f32[3,6,8,1024]{3,2,1,0:T(8,128)S(1)} copy-done((f32[3,6,8,1024]{3,2,1,0:T(8,128)S(1)}, f32[3,6,8,1024]{3,2,1,0:T(8,128)}, u32[]{:S(2)}) %copy-start) | copy-done | bytes 589848
  1.1 1.6 %collective-permute-start.3 = (f32[1,6,6,8,128]{4,3,2,1,0:T(8,128)S(1)}, f32[1,6,6,8,128]{4,3,2,1,0:T(8,128)S(1)}, u32[]{:S(2)}, u32[]{:S(2)}) collective-permute-start(f32[1,6,6,8,128]{4,3,2,1,0:T(8,128)S(1)} %pack.1.refs_0_), channel_id=1, source_target_pairs={{0,1},{1,0},{2,3},{3,2},{4,5},{5,4},{6,7},{7,6},{8,9},{9,8},{10,11... | collective-permute-start | bytes 442376 | tf_op jit(solution)/shard_map/ppermute | solution.py:665
  2.7 1.0 %near_a.1 = (f32[1,6,6,8,128]{4,3,2,1,0:T(8,128)S(1)}, f32[6,3,8,8,128]{4,3,2,1,0:T(8,128)S(1)}, f32[6,4,3,6,8,128]{5,4,3,2,1,0:T(8,128)S(1)}, f32[6,6,8,128]{3,...) custom-call(f32[1,6,6,8,128]{4,3,2,1,0:T(8,128)S(1)} %pack.1.refs_0_, ...), custom_call_target="tpu_custom_call" | custom-call | flops 1 | bytes 1 | tf_op jit(solution)/shard_map/near_a/pallas_call | solution.py:667
  3.7 0.6 %collective-permute-start.4 = (f32[1,6,6,8,128]{4,3,2,1,0:T(8,128)S(1)}, f32[1,6,6,8,128]{4,3,2,1,0:T(8,128)S(1)}, u32[]{:S(2)}, u32[]{:S(2)}) collective-permute-start(f32[1,6,6,8,128]{4,3,2,1,0:T(8,128)S(1)} %get-tuple-element.38), channel_id=1, source_target_pairs={{0,1},{1,0},{2,3},{3,2},{4,5},{5,4},{6,7},{7,6},{8,9},{9,8},{10,11... | collective-permute-start | bytes 442376 | tf_op jit(solution)/shard_map/ppermute | solution.py:676
  4.3 0.0 collective-permute-start.1
  4.3 1.6 %collective-permute-start = (f32[1,3,8,8,128]{4,3,2,1,0:T(8,128)S(1)}, f32[1,3,8,8,128]{4,3,2,1,0:T(8,128)S(1)}, u32[]{:S(2)}, u32[]{:S(2)}) collective-permute-start(f32[1,3,8,8,128]{4,3,2,1,0:T(8,128)S(1)} %get-tuple-element.24), channel_id=1, source_target_pairs={{8,16},{16,8},{0,24},{24,0},{9,17},{17,9},{1,25},{25,1},{10,18},{1... | collective-permute-start | bytes 294920 | tf_op jit(solution)/shard_map/ppermute | solution.py:677
  5.9 0.0 copy-start.1
  5.9 0.0 copy-start.2
  5.9 0.0 copy-start.3
  5.9 0.9 %near_b.1 = (f32[6,4,3,2,8,128]{5,4,3,2,1,0:T(8,128)S(1)}, f32[6,5,8,128]{3,2,1,0:T(8,128)S(1)}, f32[6,52,8,128]{3,2,1,0:T(8,128)S(1)}) custom-call(f32[6,3,8,8,128]{4,3,2,1,0:T(8,128)S(1)} %get-tuple-element.28.refs_0_.refs_1_, f32[6,4,3,6,8,128]{5,4,3,2,1,0:T(8,128)S(1)} %get-tuple-element.27.refs_1_.refs_2_.refs_3_.refs_0_, ...), custom_call_target="tpu_custom_call" | custom-call | flops 1 | bytes 1 | tf_op jit(solution)/shard_map/near_b/pallas_call | solution.py:680
  6.8 0.8 %collective-permute-done.3.refs_1_.refs_0_ = f32[1,6,6,8,128]{4,3,2,1,0:T(8,128)S(1)} collective-permute-done((f32[1,6,6,8,128]{4,3,2,1,0:T(8,128)S(1)}, f32[1,6,6,8,128]{4,3,2,1,0:T(8,128)S(1)}, u32[]{:S(2)}, u32[]{:S(2)}) %collective-permute-start.3) | collective-permute-done | bytes 147488 | tf_op jit(solution)/shard_map/ppermute | solution.py:665
  7.6 1.8 %collective-permute-start.5 = (f32[1,4,12,8,128]{4,3,2,1,0:T(8,128)S(1)}, f32[1,4,12,8,128]{4,3,2,1,0:T(8,128)S(1)}, u32[]{:S(2)}, u32[]{:S(2)}) collective-permute-start(f32[1,4,12,8,128]{4,3,2,1,0:T(8,128)S(1)} %send.1), channel_id=1, source_target_pairs={{0,8},{1,2},{2,1},{3,4},{4,3},{5,6},{6,5},{7,15},{8,0},{9,10},{10,... | collective-permute-start | bytes 589832 | tf_op jit(solution)/shard_map/ppermute | solution.py:713
  9.4 0.0 collective-permute-done.1.refs_3_.refs_11_
  9.4 0.0 copy-done.1
  9.4 0.0 copy-done.2
  9.4 0.0 copy-done.3
  9.4 0.8 %weights.1 = (f32[14,8,128]{2,1,0:T(8,128)S(1)}, f32[130,8,128]{2,1,0:T(8,128)S(1)}, f32[6,28,8,128]{3,2,1,0:T(8,128)S(1)}, f32[6,4,8,128]{3,2,1,0:T(8,128)S(1)}) custom-call(s32[6]{0:T(128)S(1)} %copy-done.2, f32[4,14]{1,0:T(4,128)S(1)} %copy-done.1, f32[23]{0:T(128)S(1)} %copy-done.3, f32[1,3,8,8,128]{4,3,2,1,0:T(8,128)S(1)} %collective-permute-done.1.refs_3_.refs_11_), custom_call_target="tpu_custom_call" | custom-call | flops 1 | bytes 1 | tf_op jit(solution)/shard_map/weights/pallas_call | solution.py:690
  10.2 0.0 collective-permute-done.refs_0_.refs_12_
  10.3 1.0 %inner.1 = (f32[6,42,3,8,128]{4,3,2,1,0:T(8,128)S(1)}, f32[6,3,6,8,128]{4,3,2,1,0:T(8,128)S(1)}) custom-call(f32[1,3,8,8,128]{4,3,2,1,0:T(8,128)S(1)} %collective-permute-done.refs_0_.refs_12_, f32[6,28,8,128]{3,2,1,0:T(8,128)S(1)} %get-tuple-element.26.refs_1_.refs_8_.refs_6_, ...), custom_call_target="tpu_custom_call" | custom-call | flops 1 | bytes 1 | tf_op jit(solution)/shard_map/inner/pallas_call | solution.py:700
  11.3 1.3 %collective-permute-start.2 = (f32[1,2,12,8,128]{4,3,2,1,0:T(8,128)S(1)}, f32[1,2,12,8,128]{4,3,2,1,0:T(8,128)S(1)}, u32[]{:S(2)}, u32[]{:S(2)}) collective-permute-start(f32[1,2,12,8,128]{4,3,2,1,0:T(8,128)S(1)} %send_rest.1.refs_0_), channel_id=1, source_target_pairs={{0,8},{1,2},{2,1},{3,4},{4,3},{5,6},{6,5},{7,15},{8,0},{9,10},{10,... | collective-permute-start | bytes 294920 | tf_op jit(solution)/shard_map/ppermute | solution.py:713
  12.6 0.0 collective-permute-done.4.refs_2_
  12.6 0.7 %strain.1 = (f32[6,4,3,3,8,128]{5,4,3,2,1,0:T(8,128)S(1)}, f32[6,4,8,8,128]{4,3,2,1,0:T(8,128)S(1)}, f32[6,18,8,128]{3,2,1,0:T(8,128)S(1)}) custom-call(f32[1,2,12,8,128]{4,3,2,1,0:T(8,128)S(1)} %send_rest.1.refs_0_, f32[1,6,6,8,128]{4,3,2,1,0:T(8,128)S(1)} %collective-permute-done.3.refs_1_.refs_0_, ...), custom_call_target="tpu_custom_call" | custom-call | flops 1 | bytes 1 | tf_op jit(solution)/shard_map/strain/pallas_call | solution.py:720
  13.2 1.6 %early.1.refs_8_ = f32[6,3,8,8,128]{4,3,2,1,0:T(8,128)S(1)} custom-call(f32[6,4,3,6,8,128]{5,4,3,2,1,0:T(8,128)S(1)} %get-tuple-element.27.refs_1_.refs_2_.refs_3_.refs_0_, f32[6,4,3,2,8,128]{5,4,3,2,1,0:T(8,128)S(1)} %get-tuple-element.30.refs_3_.refs_4_.refs_1_.refs_2_, f32[6,4,3,3,8,128]{5,4,3,2,1,0:T(8,128)S(1)} %get-tuple-element.39.refs_2_, ...), custom_call_target="tpu_custom_call" | custom-call | flops 2000000000 | bytes 1 | tf_op jit(solution)/shard_map/early/pallas_call | solution.py:730
  14.8 0.2 collective-permute-done.5.refs_0_
  15.0 0.8 %late.1.refs_10_ = f32[3,4,64,128]{3,2,1,0:T(8,128)S(1)} custom-call(f32[1,4,12,8,128]{4,3,2,1,0:T(8,128)S(1)} %collective-permute-done.5.refs_0_, f32[6,4,3,6,8,128]{5,4,3,2,1,0:T(8,128)S(1)} %get-tuple-element.27.refs_1_.refs_2_.refs_3_.refs_0_, f32[6,4,3,2,8,128]{5,4,3,2,1,0:T(8,128)S(1)} %get-tuple-element.30.refs_3_.refs_4_.refs_1_.refs_2_, ...), custom_call_target="tpu_custom_call" | custom-call | flops 2000000000 | bytes 1 | tf_op jit(solution)/shard_map/late/pallas_call | solution.py:753
  15.8 1.1 %collective-permute-done.2.refs_0_ = f32[1,2,12,8,128]{4,3,2,1,0:T(8,128)S(1)} collective-permute-done((f32[1,2,12,8,128]{4,3,2,1,0:T(8,128)S(1)}, f32[1,2,12,8,128]{4,3,2,1,0:T(8,128)S(1)}, u32[]{:S(2)}, u32[]{:S(2)}) %collective-permute-start.2) | collective-permute-done | bytes 98336 | tf_op jit(solution)/shard_map/ppermute | solution.py:713
  16.9 1.1 %late_rest.1 = f32[3,6,64,128]{3,2,1,0:T(8,128)} custom-call(f32[1,2,12,8,128]{4,3,2,1,0:T(8,128)S(1)} %collective-permute-done.2.refs_0_, f32[6,4,3,6,8,128]{5,4,3,2,1,0:T(8,128)S(1)} %get-tuple-element.27.refs_1_.refs_2_.refs_3_.refs_0_, f32[6,4,3,2,8,128]{5,4,3,2,1,0:T(8,128)S(1)} %get-tuple-element.30.refs_3_.refs_4_.refs_1_.refs_2_, ...), custom_call_target="tpu_custom_call" | custom-call | flops 2000000000 | bytes 1 | tf_op jit(solution)/shard_map/late_rest/pallas_call | solution.py:753
  (3 shorter events, 0.1 us)
Async XLA Ops:
  0.0 1.1 %copy-start = (f32[3,6,8,1024]{3,2,1,0:T(8,128)S(1)}, f32[3,6,8,1024]{3,2,1,0:T(8,128)}, u32[]{:S(2)}) copy-start(f32[3,6,8,1024]{3,2,1,0:T(8,128)} %param.4) | copy-start | bytes 1769476
  1.1 6.5 %collective-permute-start.3 = (f32[1,6,6,8,128]{4,3,2,1,0:T(8,128)S(1)}, f32[1,6,6,8,128]{4,3,2,1,0:T(8,128)S(1)}, u32[]{:S(2)}, u32[]{:S(2)}) collective-permute-start(f32[1,6,6,8,128]{4,3,2,1,0:T(8,128)S(1)} %pack.1.refs_0_), channel_id=1, source_target_pairs={{0,1},{1,0},{2,3},{3,2},{4,5},{5,4},{6,7},{7,6},{8,9},{9,8},{10,11... | collective-permute-start | bytes 442376 | tf_op jit(solution)/shard_map/ppermute | solution.py:665
  3.7 8.9 %collective-permute-start.4 = (f32[1,6,6,8,128]{4,3,2,1,0:T(8,128)S(1)}, f32[1,6,6,8,128]{4,3,2,1,0:T(8,128)S(1)}, u32[]{:S(2)}, u32[]{:S(2)}) collective-permute-start(f32[1,6,6,8,128]{4,3,2,1,0:T(8,128)S(1)} %get-tuple-element.38), channel_id=1, source_target_pairs={{0,1},{1,0},{2,3},{3,2},{4,5},{5,4},{6,7},{7,6},{8,9},{9,8},{10,11... | collective-permute-start | bytes 442376 | tf_op jit(solution)/shard_map/ppermute | solution.py:676
  4.3 5.1 %collective-permute-start.1 = (f32[1,3,8,8,128]{4,3,2,1,0:T(8,128)S(1)}, f32[1,3,8,8,128]{4,3,2,1,0:T(8,128)S(1)}, u32[]{:S(2)}, u32[]{:S(2)}) collective-permute-start(f32[1,3,8,8,128]{4,3,2,1,0:T(8,128)S(1)} %get-tuple-element.25), channel_id=1, source_target_pairs={{0,8},{8,0},{16,24},{24,16},{1,9},{9,1},{17,25},{25,17},{2,10},{10... | collective-permute-start | bytes 294920 | tf_op jit(solution)/shard_map/ppermute | solution.py:678
  4.3 6.0 %collective-permute-start = (f32[1,3,8,8,128]{4,3,2,1,0:T(8,128)S(1)}, f32[1,3,8,8,128]{4,3,2,1,0:T(8,128)S(1)}, u32[]{:S(2)}, u32[]{:S(2)}) collective-permute-start(f32[1,3,8,8,128]{4,3,2,1,0:T(8,128)S(1)} %get-tuple-element.24), channel_id=1, source_target_pairs={{8,16},{16,8},{0,24},{24,0},{9,17},{17,9},{1,25},{25,1},{10,18},{1... | collective-permute-start | bytes 294920 | tf_op jit(solution)/shard_map/ppermute | solution.py:677
  5.9 3.5 %copy-start.1 = (f32[4,14]{1,0:T(4,128)S(1)}, f32[4,14]{1,0:T(4,128)}, u32[]{:S(2)}) copy-start(f32[4,14]{1,0:T(4,128)} %refs_1_.1) | copy-start | bytes 676
  5.9 3.5 %copy-start.2 = (s32[6]{0:T(128)S(1)}, s32[6]{0:T(128)}, u32[]{:S(2)}) copy-start(s32[6]{0:T(128)} %refs_0_.1) | copy-start | bytes 76
  5.9 3.5 %copy-start.3 = (f32[23]{0:T(128)S(1)}, f32[23]{0:T(128)}, u32[]{:S(2)}) copy-start(f32[23]{0:T(128)} %refs_2_.1) | copy-start | bytes 280
  7.6 7.4 %collective-permute-start.5 = (f32[1,4,12,8,128]{4,3,2,1,0:T(8,128)S(1)}, f32[1,4,12,8,128]{4,3,2,1,0:T(8,128)S(1)}, u32[]{:S(2)}, u32[]{:S(2)}) collective-permute-start(f32[1,4,12,8,128]{4,3,2,1,0:T(8,128)S(1)} %send.1), channel_id=1, source_target_pairs={{0,8},{1,2},{2,1},{3,4},{4,3},{5,6},{6,5},{7,15},{8,0},{9,10},{10,... | collective-permute-start | bytes 589832 | tf_op jit(solution)/shard_map/ppermute | solution.py:713
  11.3 5.6 %collective-permute-start.2 = (f32[1,2,12,8,128]{4,3,2,1,0:T(8,128)S(1)}, f32[1,2,12,8,128]{4,3,2,1,0:T(8,128)S(1)}, u32[]{:S(2)}, u32[]{:S(2)}) collective-permute-start(f32[1,2,12,8,128]{4,3,2,1,0:T(8,128)S(1)} %send_rest.1.refs_0_), channel_id=1, source_target_pairs={{0,8},{1,2},{2,1},{3,4},{4,3},{5,6},{6,5},{7,15},{8,0},{9,10},{10,... | collective-permute-start | bytes 294920 | tf_op jit(solution)/shard_map/ppermute | solution.py:713

commit v8 on v7

--- a/solution.py
+++ b/solution.py
@@ -11,6 +11,7 @@
 REACH = 3
 LANES = 128
 VMEM_LIMIT = 24 * 1024 * 1024
+EXTRA = 1
 EARLY_COST = 2 * 10**9
 LATE_COST = 2 * 10**9
 
@@ -408,12 +409,10 @@
     for_plies(plies, 2, ply)
 
 
-def send_kernel(plan, part, after_ref, base_ref, sums_b_ref, message):
-    for p in part:
-        for x in range(REACH):
-            message[0, p - part.start, 3 * REACH + x] = sums_b_ref[p, x]
-            for c in range(3):
-                message[0, p - part.start, c * REACH + x] = base_ref[p, c, x]
+def send_kernel(plan, wanted, after_ref, base_ref, sums_b_ref, message):
+    for at, (p, n) in enumerate(wanted):
+        x = n % REACH
+        message[0, at] = sums_b_ref[p, x] if n >= 3 * REACH else base_ref[p, n // REACH, x]
 
 
 def strain_kernel(
@@ -530,7 +529,7 @@
 
 
 def late_kernel(
-    plan, tiles, part, final, got_ref, rows_a_ref, rows_b_ref, sums_b_ref, weight_ref, pair_ref,
+    plan, tiles, part, final, wanted, got_ref, more_ref, rows_a_ref, rows_b_ref, sums_b_ref, weight_ref, pair_ref,
     factor_ref, vector_ref, force_in_ref, strain_a_ref, *rest,
 ):
     if final:
@@ -548,6 +547,11 @@
     has_b = jnp.ones((grid.subs, LANES), jnp.int32) * sides(tiles)[1].astype(jnp.int32) > 0
     cross_masks = {b: grid.exists[b] & has_b if b else has_b for b in range(REACH + 1)}
 
+    def got_row(p, n):
+        for ref, places in zip((got_ref, more_ref), wanted):
+            if (p, n) in places:
+                return ref[0, places.index((p, n))]
+
     def ply(p):
         n = p - part.start
         rows = Store(
@@ -560,7 +564,7 @@
         )
         factors = factors_of(factor_ref, p)
         for j in range(REACH):
-            row = [got_ref[0, n, c * REACH + j] for c in range(3)]
+            row = [got_row(p, c * REACH + j) for c in range(3)]
             keep_row(grid, rows, REACH - 1 - j, [-row[0], row[1], row[2]])
 
         crossed = {}
@@ -570,7 +574,7 @@
 
         sums = extension_sums(grid, rows, plan.cross_b, cross_masks.get, keep)
         for x in range(start):
-            total = got_ref[0, n, 3 * REACH + REACH - 1 - x] if x in plan.low else sums_b_ref[p, x - REACH]
+            total = got_row(p, 3 * REACH + REACH - 1 - x) if x in plan.low else sums_b_ref[p, x - REACH]
             strain = 3.0 * (total + sums[x]) * (weight_ref[x] * weight_ref[x])
             strains.put(x, strain, 0)
             for b, moved in grid.ahead(strain).items():
@@ -706,16 +710,20 @@
 
     count = plies - plies // 3
     parts = [range(count), range(count, plies)]
-    def send_part(part, name, after):
+    width = 4 * REACH
+    wanted = [
+        [(p, n) for p in parts[0] for n in range(width)] + [(p, n) for p in parts[1] for n in range(EXTRA)],
+        [(p, n) for p in parts[1] for n in range(EXTRA, width)],
+    ]
+
+    def send_part(places, name, after):
         (message,) = call(
-            lambda *refs: send_kernel(plan, part, *refs), name, [whole] * 3, [array(1, len(part), 4 * REACH)]
+            lambda *refs: send_kernel(plan, places, *refs), name, [whole] * 3, [array(1, len(places))]
         )(after, base, sums_b)
         return message, lax.ppermute(message, ("ply", "tile"), swap_b)
 
-    message_b, got = send_part(parts[0], "send", got_a)
-    got_b = [got]
-    message_b, got = send_part(parts[1], "send_rest", inner_late)
-    got_b.append(got)
+    _, got_b = send_part(wanted[0], "send", got_a)
+    message_b, got_rest = send_part(wanted[1], "send_rest", inner_late)
 
     halo_a, strain, inverse_cross = call(
         lambda *refs: strain_kernel(plan, tiles, *refs),
@@ -739,7 +747,7 @@
     )
 
     out = []
-    for part, got in zip(parts, got_b):
+    for part in parts:
         final = part.stop == plies
         result = jax.ShapeDtypeStruct((comps, len(part), *view.shape[2:]), jnp.float32)
         scratches = [
@@ -751,15 +759,15 @@
                 pltpu.VMEM(result.shape, jnp.float32), pltpu.SemaphoreType.DMA, pltpu.SemaphoreType.DMA,
             ]
         out = call(
-            lambda *refs: late_kernel(plan, tiles, part, final, *refs),
+            lambda *refs: late_kernel(plan, tiles, part, final, wanted, *refs),
             "late_rest" if final else "late",
-            [whole] * (10 + len(out)),
+            [whole] * (11 + len(out)),
             [jax.ShapeDtypeStruct(view.shape, jnp.float32) if final else result],
             out_specs=[pl.BlockSpec(memory_space=pltpu.HBM)] if final else None,
             scratches=scratches,
             cost=LATE_COST,
         )(
-            got, rows_a, rows_b, sums_b, weight, pair, factor, vector_late, force, strain, *out,
+            got_b, got_rest if final else got_b, rows_a, rows_b, sums_b, weight, pair, factor, vector_late, force, strain, *out,
         )
     (out,) = out
     return (

time: 18.2 us -> 18.1 us (level)
  no operation moved by 1% of the time
where the time goes in v8:
time: 18.1 us; the launch traced here: 17.9 us
  Pallas kernels  7.96 us (44%)
  starting transfers between devices  6.82 us (38%)
  waiting for transfers between devices  1.99 us (11%)
  local copies, waits for them, and re-layouts  1.07 us (6%)
    ppermute x2, starting transfers between devices, send_part(): return (message, lax.ppermute(message, ('ply', 'tile'), swap_b))  3.06 us
    pallas_call x2, Pallas kernels, local(): call(lambda *refs: late_kernel(plan, tiles, part, final, wanted, *refs),...  1.96 us
    ppermute x1, starting transfers between devices, local(): got_second = lax.ppermute(second, 'ply', swap_second)  1.6 us
    ppermute x1, starting transfers between devices, local(): got_a = lax.ppermute(message_a, 'tile', swap_a)  1.58 us
    pallas_call x1, Pallas kernels, local(): call(lambda *refs: early_kernel(plan, tiles, *refs), 'early', [whole] * 1...  1.57 us
    ppermute x2, waiting for transfers between devices, send_part(): return (message, lax.ppermute(message, ('ply', 'tile'), swap_b))  1.17 us
    unnamed x8, local copies, waits for them, and re-layouts  1.07 us
    pallas_call x1, Pallas kernels, local(): call(lambda *refs: inner_kernel(plan, *refs), 'inner', [whole] * 7, [arra...  1.02 us
  transfers between devices with their start and end apart: 6, of which 3 were waited for; matrix products, arithmetic and copies ran while one was open for 0% of the time, Pallas kernels for 38%

profile of v8, /device:TPU:8, one launch (start us, length us, event | category | flops | bytes accessed | tf_op | source)
XLA Modules:
  0.0 17.9 jit_solution(10528516579898368599)
XLA Ops:
  0.0 0.0 copy-start
  0.0 1.1 %copy-done = f32[3,6,8,1024]{3,2,1,0:T(8,128)S(1)} copy-done((f32[3,6,8,1024]{3,2,1,0:T(8,128)S(1)}, f32[3,6,8,1024]{3,2,1,0:T(8,128)}, u32[]{:S(2)}) %copy-start) | copy-done | bytes 589848
  1.1 1.6 %collective-permute-start = (f32[1,6,6,8,128]{4,3,2,1,0:T(8,128)S(1)}, f32[1,6,6,8,128]{4,3,2,1,0:T(8,128)S(1)}, u32[]{:S(2)}, u32[]{:S(2)}) collective-permute-start(f32[1,6,6,8,128]{4,3,2,1,0:T(8,128)S(1)} %pack.1.refs_0_), channel_id=1, source_target_pairs={{0,1},{1,0},{2,3},{3,2},{4,5},{5,4},{6,7},{7,6},{8,9},{9,8},{10,11... | collective-permute-start | bytes 442376 | tf_op jit(solution)/shard_map/ppermute | solution.py:669
  2.7 1.0 %near_a.1 = (f32[1,6,6,8,128]{4,3,2,1,0:T(8,128)S(1)}, f32[6,3,8,8,128]{4,3,2,1,0:T(8,128)S(1)}, f32[6,4,3,6,8,128]{5,4,3,2,1,0:T(8,128)S(1)}, f32[6,6,8,128]{3,...) custom-call(f32[1,6,6,8,128]{4,3,2,1,0:T(8,128)S(1)} %pack.1.refs_0_, ...), custom_call_target="tpu_custom_call" | custom-call | flops 1 | bytes 1 | tf_op jit(solution)/shard_map/near_a/pallas_call | solution.py:671
  3.7 0.6 %collective-permute-start.5 = (f32[1,6,6,8,128]{4,3,2,1,0:T(8,128)S(1)}, f32[1,6,6,8,128]{4,3,2,1,0:T(8,128)S(1)}, u32[]{:S(2)}, u32[]{:S(2)}) collective-permute-start(f32[1,6,6,8,128]{4,3,2,1,0:T(8,128)S(1)} %get-tuple-element.38), channel_id=1, source_target_pairs={{0,1},{1,0},{2,3},{3,2},{4,5},{5,4},{6,7},{7,6},{8,9},{9,8},{10,11... | collective-permute-start | bytes 442376 | tf_op jit(solution)/shard_map/ppermute | solution.py:680
  4.3 0.0 collective-permute-start.3
  4.3 1.6 %collective-permute-start.2 = (f32[1,3,8,8,128]{4,3,2,1,0:T(8,128)S(1)}, f32[1,3,8,8,128]{4,3,2,1,0:T(8,128)S(1)}, u32[]{:S(2)}, u32[]{:S(2)}) collective-permute-start(f32[1,3,8,8,128]{4,3,2,1,0:T(8,128)S(1)} %get-tuple-element.28), channel_id=1, source_target_pairs={{8,16},{16,8},{0,24},{24,0},{9,17},{17,9},{1,25},{25,1},{10,18},{1... | collective-permute-start | bytes 294920 | tf_op jit(solution)/shard_map/ppermute | solution.py:681
  5.9 0.0 copy-start.1
  5.9 0.0 copy-start.2
  5.9 0.0 copy-start.3
  5.9 0.9 %near_b.1 = (f32[6,4,3,2,8,128]{5,4,3,2,1,0:T(8,128)S(1)}, f32[6,5,8,128]{3,2,1,0:T(8,128)S(1)}, f32[6,52,8,128]{3,2,1,0:T(8,128)S(1)}) custom-call(f32[6,3,8,8,128]{4,3,2,1,0:T(8,128)S(1)} %get-tuple-element.24.refs_0_.refs_1_, f32[6,4,3,6,8,128]{5,4,3,2,1,0:T(8,128)S(1)} %get-tuple-element.25.refs_1_.refs_2_.refs_3_.refs_0_, ...), custom_call_target="tpu_custom_call" | custom-call | flops 1 | bytes 1 | tf_op jit(solution)/shard_map/near_b/pallas_call | solution.py:684
  6.8 0.8 %collective-permute-done.refs_0_.refs_1_ = f32[1,6,6,8,128]{4,3,2,1,0:T(8,128)S(1)} collective-permute-done((f32[1,6,6,8,128]{4,3,2,1,0:T(8,128)S(1)}, f32[1,6,6,8,128]{4,3,2,1,0:T(8,128)S(1)}, u32[]{:S(2)}, u32[]{:S(2)}) %collective-permute-start) | collective-permute-done | bytes 147488 | tf_op jit(solution)/shard_map/ppermute | solution.py:669
  7.6 1.8 %collective-permute-start.1 = (f32[1,50,8,128]{3,2,1,0:T(8,128)S(1)}, f32[1,50,8,128]{3,2,1,0:T(8,128)S(1)}, u32[]{:S(2)}, u32[]{:S(2)}) collective-permute-start(f32[1,50,8,128]{3,2,1,0:T(8,128)S(1)} %send.1), channel_id=1, source_target_pairs={{0,8},{1,2},{2,1},{3,4},{4,3},{5,6},{6,5},{7,15},{8,0},{9,10},{10,... | collective-permute-start | bytes 614408 | tf_op jit(solution)/shard_map/ppermute | solution.py:723
  9.4 0.0 collective-permute-done.3.refs_3_.refs_11_
  9.4 0.0 copy-done.1
  9.4 0.0 copy-done.2
  9.4 0.0 copy-done.3
  9.4 0.8 %weights.1 = (f32[14,8,128]{2,1,0:T(8,128)S(1)}, f32[130,8,128]{2,1,0:T(8,128)S(1)}, f32[6,28,8,128]{3,2,1,0:T(8,128)S(1)}, f32[6,4,8,128]{3,2,1,0:T(8,128)S(1)}) custom-call(s32[6]{0:T(128)S(1)} %copy-done.2, f32[4,14]{1,0:T(4,128)S(1)} %copy-done.1, f32[23]{0:T(128)S(1)} %copy-done.3, f32[1,3,8,8,128]{4,3,2,1,0:T(8,128)S(1)} %collective-permute-done.3.refs_3_.refs_11_), custom_call_target="tpu_custom_call" | custom-call | flops 1 | bytes 1 | tf_op jit(solution)/shard_map/weights/pallas_call | solution.py:694
  10.2 0.0 collective-permute-done.2.refs_0_.refs_12_
  10.3 1.0 %inner.1 = (f32[6,42,3,8,128]{4,3,2,1,0:T(8,128)S(1)}, f32[6,3,6,8,128]{4,3,2,1,0:T(8,128)S(1)}) custom-call(f32[1,3,8,8,128]{4,3,2,1,0:T(8,128)S(1)} %collective-permute-done.2.refs_0_.refs_12_, f32[6,28,8,128]{3,2,1,0:T(8,128)S(1)} %get-tuple-element.30.refs_1_.refs_8_.refs_7_, ...), custom_call_target="tpu_custom_call" | custom-call | flops 1 | bytes 1 | tf_op jit(solution)/shard_map/inner/pallas_call | solution.py:704
  11.3 1.3 %collective-permute-start.4 = (f32[1,22,8,128]{3,2,1,0:T(8,128)S(1)}, f32[1,22,8,128]{3,2,1,0:T(8,128)S(1)}, u32[]{:S(2)}, u32[]{:S(2)}) collective-permute-start(f32[1,22,8,128]{3,2,1,0:T(8,128)S(1)} %send_rest.1.refs_0_), channel_id=1, source_target_pairs={{0,8},{1,2},{2,1},{3,4},{4,3},{5,6},{6,5},{7,15},{8,0},{9,10},{10,... | collective-permute-start | bytes 270344 | tf_op jit(solution)/shard_map/ppermute | solution.py:723
  12.6 0.0 collective-permute-done.5.refs_2_
  12.6 0.7 %strain.1 = (f32[6,4,3,3,8,128]{5,4,3,2,1,0:T(8,128)S(1)}, f32[6,4,8,8,128]{4,3,2,1,0:T(8,128)S(1)}, f32[6,18,8,128]{3,2,1,0:T(8,128)S(1)}) custom-call(f32[1,22,8,128]{3,2,1,0:T(8,128)S(1)} %send_rest.1.refs_0_, f32[1,6,6,8,128]{4,3,2,1,0:T(8,128)S(1)} %collective-permute-done.refs_0_.refs_1_, f32[1,6,6,8,128]{4,3,2,1,0:T(8,128)S(1)} %collective-permute-done.5.refs_2_, ...), custom_call_target="tpu_custom_call" | custom-call | flops 1 | bytes 1 | tf_op jit(solution)/shard_map/strain/pallas_call | solution.py:728
  13.2 1.6 %early.1.refs_9_ = f32[6,3,8,8,128]{4,3,2,1,0:T(8,128)S(1)} custom-call(f32[6,4,3,6,8,128]{5,4,3,2,1,0:T(8,128)S(1)} %get-tuple-element.25.refs_1_.refs_2_.refs_3_.refs_0_, f32[6,4,3,2,8,128]{5,4,3,2,1,0:T(8,128)S(1)} %get-tuple-element.31.refs_3_.refs_4_.refs_1_, f32[6,4,3,3,8,128]{5,4,3,2,1,0:T(8,128)S(1)} %get-tuple-element.39.refs_2_, ...), custom_call_target="tpu_custom_call" | custom-call | flops 2000000000 | bytes 1 | tf_op jit(solution)/shard_map/early/pallas_call | solution.py:738
  14.8 0.6 %collective-permute-done.1.refs_0_.refs_1_ = f32[1,50,8,128]{3,2,1,0:T(8,128)S(1)} collective-permute-done((f32[1,50,8,128]{3,2,1,0:T(8,128)S(1)}, f32[1,50,8,128]{3,2,1,0:T(8,128)S(1)}, u32[]{:S(2)}, u32[]{:S(2)}) %collective-permute-start.1) | collective-permute-done | bytes 204832 | tf_op jit(solution)/shard_map/ppermute | solution.py:723
  15.4 0.8 %late.1.refs_11_ = f32[3,4,64,128]{3,2,1,0:T(8,128)S(1)} custom-call(f32[1,50,8,128]{3,2,1,0:T(8,128)S(1)} %collective-permute-done.1.refs_0_.refs_1_, f32[1,50,8,128]{3,2,1,0:T(8,128)S(1)} %collective-permute-done.1.refs_0_.refs_1_, f32[6,4,3,6,8,128]{5,4,3,2,1,0:T(8,128)S(1)} %get-tuple-element.25.refs_1_.refs_2_.refs_3_.refs_0_, ...), custom_call_target="tpu_custom_call" | custom-call | flops 2000000000 | bytes 1 | tf_op jit(solution)/shard_map/late/pallas_call | solution.py:761
  16.2 0.6 %collective-permute-done.4.refs_1_ = f32[1,22,8,128]{3,2,1,0:T(8,128)S(1)} collective-permute-done((f32[1,22,8,128]{3,2,1,0:T(8,128)S(1)}, f32[1,22,8,128]{3,2,1,0:T(8,128)S(1)}, u32[]{:S(2)}, u32[]{:S(2)}) %collective-permute-start.4) | collective-permute-done | bytes 90144 | tf_op jit(solution)/shard_map/ppermute | solution.py:723
  16.8 1.1 %late_rest.1 = f32[3,6,64,128]{3,2,1,0:T(8,128)} custom-call(f32[1,50,8,128]{3,2,1,0:T(8,128)S(1)} %collective-permute-done.1.refs_0_.refs_1_, f32[1,22,8,128]{3,2,1,0:T(8,128)S(1)} %collective-permute-done.4.refs_1_, f32[6,4,3,6,8,128]{5,4,3,2,1,0:T(8,128)S(1)} %get-tuple-element.25.refs_1_.refs_2_.refs_3_.refs_0_, ...), custom_call_target="tpu_custom_call" | custom-call | flops 2000000000 | bytes 1 | tf_op jit(solution)/shard_map/late_rest/pallas_call | solution.py:761
  (3 shorter events, 0.1 us)
Async XLA Ops:
  0.0 1.1 %copy-start = (f32[3,6,8,1024]{3,2,1,0:T(8,128)S(1)}, f32[3,6,8,1024]{3,2,1,0:T(8,128)}, u32[]{:S(2)}) copy-start(f32[3,6,8,1024]{3,2,1,0:T(8,128)} %param.4) | copy-start | bytes 1769476
  1.1 6.5 %collective-permute-start = (f32[1,6,6,8,128]{4,3,2,1,0:T(8,128)S(1)}, f32[1,6,6,8,128]{4,3,2,1,0:T(8,128)S(1)}, u32[]{:S(2)}, u32[]{:S(2)}) collective-permute-start(f32[1,6,6,8,128]{4,3,2,1,0:T(8,128)S(1)} %pack.1.refs_0_), channel_id=1, source_target_pairs={{0,1},{1,0},{2,3},{3,2},{4,5},{5,4},{6,7},{7,6},{8,9},{9,8},{10,11... | collective-permute-start | bytes 442376 | tf_op jit(solution)/shard_map/ppermute | solution.py:669
  3.7 8.8 %collective-permute-start.5 = (f32[1,6,6,8,128]{4,3,2,1,0:T(8,128)S(1)}, f32[1,6,6,8,128]{4,3,2,1,0:T(8,128)S(1)}, u32[]{:S(2)}, u32[]{:S(2)}) collective-permute-start(f32[1,6,6,8,128]{4,3,2,1,0:T(8,128)S(1)} %get-tuple-element.38), channel_id=1, source_target_pairs={{0,1},{1,0},{2,3},{3,2},{4,5},{5,4},{6,7},{7,6},{8,9},{9,8},{10,11... | collective-permute-start | bytes 442376 | tf_op jit(solution)/shard_map/ppermute | solution.py:680
  4.3 5.1 %collective-permute-start.3 = (f32[1,3,8,8,128]{4,3,2,1,0:T(8,128)S(1)}, f32[1,3,8,8,128]{4,3,2,1,0:T(8,128)S(1)}, u32[]{:S(2)}, u32[]{:S(2)}) collective-permute-start(f32[1,3,8,8,128]{4,3,2,1,0:T(8,128)S(1)} %get-tuple-element.29), channel_id=1, source_target_pairs={{0,8},{8,0},{16,24},{24,16},{1,9},{9,1},{17,25},{25,17},{2,10},{10... | collective-permute-start | bytes 294920 | tf_op jit(solution)/shard_map/ppermute | solution.py:682
  4.3 6.0 %collective-permute-start.2 = (f32[1,3,8,8,128]{4,3,2,1,0:T(8,128)S(1)}, f32[1,3,8,8,128]{4,3,2,1,0:T(8,128)S(1)}, u32[]{:S(2)}, u32[]{:S(2)}) collective-permute-start(f32[1,3,8,8,128]{4,3,2,1,0:T(8,128)S(1)} %get-tuple-element.28), channel_id=1, source_target_pairs={{8,16},{16,8},{0,24},{24,0},{9,17},{17,9},{1,25},{25,1},{10,18},{1... | collective-permute-start | bytes 294920 | tf_op jit(solution)/shard_map/ppermute | solution.py:681
  5.9 3.5 %copy-start.1 = (f32[4,14]{1,0:T(4,128)S(1)}, f32[4,14]{1,0:T(4,128)}, u32[]{:S(2)}) copy-start(f32[4,14]{1,0:T(4,128)} %refs_1_.1) | copy-start | bytes 676
  5.9 3.5 %copy-start.2 = (s32[6]{0:T(128)S(1)}, s32[6]{0:T(128)}, u32[]{:S(2)}) copy-start(s32[6]{0:T(128)} %refs_0_.1) | copy-start | bytes 76
  5.9 3.5 %copy-start.3 = (f32[23]{0:T(128)S(1)}, f32[23]{0:T(128)}, u32[]{:S(2)}) copy-start(f32[23]{0:T(128)} %refs_2_.1) | copy-start | bytes 280
  7.6 7.8 %collective-permute-start.1 = (f32[1,50,8,128]{3,2,1,0:T(8,128)S(1)}, f32[1,50,8,128]{3,2,1,0:T(8,128)S(1)}, u32[]{:S(2)}, u32[]{:S(2)}) collective-permute-start(f32[1,50,8,128]{3,2,1,0:T(8,128)S(1)} %send.1), channel_id=1, source_target_pairs={{0,8},{1,2},{2,1},{3,4},{4,3},{5,6},{6,5},{7,15},{8,0},{9,10},{10,... | collective-permute-start | bytes 614408 | tf_op jit(solution)/shard_map/ppermute | solution.py:723
  11.3 5.5 %collective-permute-start.4 = (f32[1,22,8,128]{3,2,1,0:T(8,128)S(1)}, f32[1,22,8,128]{3,2,1,0:T(8,128)S(1)}, u32[]{:S(2)}, u32[]{:S(2)}) collective-permute-start(f32[1,22,8,128]{3,2,1,0:T(8,128)S(1)} %send_rest.1.refs_0_), channel_id=1, source_target_pairs={{0,8},{1,2},{2,1},{3,4},{4,3},{5,6},{6,5},{7,15},{8,0},{9,10},{10,... | collective-permute-start | bytes 270344 | tf_op jit(solution)/shard_map/ppermute | solution.py:723

commit v9 on v8

--- a/solution.py
+++ b/solution.py
@@ -312,7 +312,7 @@
             if a:
                 mass = mass + term
         weight[x] = 1.0 / mass
-        weight_ref[x] = weight[x]
+        weight_ref[x] = 3.0 * (weight[x] * weight[x])
     moved = {x: {0: weight[x], **grid.ahead(weight[x])} for x in range(plan.wide)}
     for n, (b, a, i) in enumerate(plan.early + plan.late):
         pair_ref[n] = weight[i] + moved[i + a][b]
@@ -449,7 +449,7 @@
                 total = sums_b_ref[p, x - REACH]
             if x in sums:
                 total = total + sums[x]
-            strain = 3.0 * total * (weight_ref[x] * weight_ref[x])
+            strain = total * weight_ref[x]
             strains.put(x, strain, 0)
             for b, moved in grid.ahead(strain).items():
                 strains.put(x, moved, b)
@@ -575,7 +575,7 @@
         sums = extension_sums(grid, rows, plan.cross_b, cross_masks.get, keep)
         for x in range(start):
             total = got_row(p, 3 * REACH + REACH - 1 - x) if x in plan.low else sums_b_ref[p, x - REACH]
-            strain = 3.0 * (total + sums[x]) * (weight_ref[x] * weight_ref[x])
+            strain = (total + sums[x]) * weight_ref[x]
             strains.put(x, strain, 0)
             for b, moved in grid.ahead(strain).items():
                 strains.put(x, moved, b)

time: 18.1 us -> 18.1 us (level)
  no operation moved by 1% of the time
where the time goes in v9:
time: 18.1 us; the launch traced here: 17.9 us
  Pallas kernels  7.97 us (44%)
  starting transfers between devices  6.82 us (38%)
  waiting for transfers between devices  1.99 us (11%)
  local copies, waits for them, and re-layouts  1.07 us (6%)
    ppermute x2, starting transfers between devices, send_part(): return (message, lax.ppermute(message, ('ply', 'tile'), swap_b))  3.06 us
    pallas_call x2, Pallas kernels, local(): call(lambda *refs: late_kernel(plan, tiles, part, final, wanted, *refs),...  1.97 us
    ppermute x1, starting transfers between devices, local(): got_second = lax.ppermute(second, 'ply', swap_second)  1.6 us
    ppermute x1, starting transfers between devices, local(): got_a = lax.ppermute(message_a, 'tile', swap_a)  1.58 us
    pallas_call x1, Pallas kernels, local(): call(lambda *refs: early_kernel(plan, tiles, *refs), 'early', [whole] * 1...  1.57 us
    ppermute x2, waiting for transfers between devices, send_part(): return (message, lax.ppermute(message, ('ply', 'tile'), swap_b))  1.17 us
    unnamed x8, local copies, waits for them, and re-layouts  1.07 us
    pallas_call x1, Pallas kernels, local(): call(lambda *refs: inner_kernel(plan, *refs), 'inner', [whole] * 7, [arra...  1.02 us
  transfers between devices with their start and end apart: 6, of which 3 were waited for; matrix products, arithmetic and copies ran while one was open for 0% of the time, Pallas kernels for 38%

profile of v9, /device:TPU:8, one launch (start us, length us, event | category | flops | bytes accessed | tf_op | source)
XLA Modules:
  0.0 17.9 jit_solution(17154839983572278645)
XLA Ops:
  0.0 0.0 copy-start
  0.0 1.1 %copy-done = f32[3,6,8,1024]{3,2,1,0:T(8,128)S(1)} copy-done((f32[3,6,8,1024]{3,2,1,0:T(8,128)S(1)}, f32[3,6,8,1024]{3,2,1,0:T(8,128)}, u32[]{:S(2)}) %copy-start) | copy-done | bytes 589848
  1.1 1.6 %collective-permute-start = (f32[1,6,6,8,128]{4,3,2,1,0:T(8,128)S(1)}, f32[1,6,6,8,128]{4,3,2,1,0:T(8,128)S(1)}, u32[]{:S(2)}, u32[]{:S(2)}) collective-permute-start(f32[1,6,6,8,128]{4,3,2,1,0:T(8,128)S(1)} %pack.1.refs_0_), channel_id=1, source_target_pairs={{0,1},{1,0},{2,3},{3,2},{4,5},{5,4},{6,7},{7,6},{8,9},{9,8},{10,11... | collective-permute-start | bytes 442376 | tf_op jit(solution)/shard_map/ppermute | solution.py:669
  2.7 1.0 %near_a.1 = (f32[1,6,6,8,128]{4,3,2,1,0:T(8,128)S(1)}, f32[6,3,8,8,128]{4,3,2,1,0:T(8,128)S(1)}, f32[6,4,3,6,8,128]{5,4,3,2,1,0:T(8,128)S(1)}, f32[6,6,8,128]{3,...) custom-call(f32[1,6,6,8,128]{4,3,2,1,0:T(8,128)S(1)} %pack.1.refs_0_, ...), custom_call_target="tpu_custom_call" | custom-call | flops 1 | bytes 1 | tf_op jit(solution)/shard_map/near_a/pallas_call | solution.py:671
  3.7 0.6 %collective-permute-start.5 = (f32[1,6,6,8,128]{4,3,2,1,0:T(8,128)S(1)}, f32[1,6,6,8,128]{4,3,2,1,0:T(8,128)S(1)}, u32[]{:S(2)}, u32[]{:S(2)}) collective-permute-start(f32[1,6,6,8,128]{4,3,2,1,0:T(8,128)S(1)} %get-tuple-element.38), channel_id=1, source_target_pairs={{0,1},{1,0},{2,3},{3,2},{4,5},{5,4},{6,7},{7,6},{8,9},{9,8},{10,11... | collective-permute-start | bytes 442376 | tf_op jit(solution)/shard_map/ppermute | solution.py:680
  4.3 0.0 collective-permute-start.3
  4.3 1.6 %collective-permute-start.2 = (f32[1,3,8,8,128]{4,3,2,1,0:T(8,128)S(1)}, f32[1,3,8,8,128]{4,3,2,1,0:T(8,128)S(1)}, u32[]{:S(2)}, u32[]{:S(2)}) collective-permute-start(f32[1,3,8,8,128]{4,3,2,1,0:T(8,128)S(1)} %get-tuple-element.28), channel_id=1, source_target_pairs={{8,16},{16,8},{0,24},{24,0},{9,17},{17,9},{1,25},{25,1},{10,18},{1... | collective-permute-start | bytes 294920 | tf_op jit(solution)/shard_map/ppermute | solution.py:681
  5.9 0.0 copy-start.1
  5.9 0.0 copy-start.2
  5.9 0.0 copy-start.3
  5.9 0.9 %near_b.1 = (f32[6,4,3,2,8,128]{5,4,3,2,1,0:T(8,128)S(1)}, f32[6,5,8,128]{3,2,1,0:T(8,128)S(1)}, f32[6,52,8,128]{3,2,1,0:T(8,128)S(1)}) custom-call(f32[6,3,8,8,128]{4,3,2,1,0:T(8,128)S(1)} %get-tuple-element.24.refs_0_.refs_1_, f32[6,4,3,6,8,128]{5,4,3,2,1,0:T(8,128)S(1)} %get-tuple-element.25.refs_1_.refs_2_.refs_3_.refs_0_, ...), custom_call_target="tpu_custom_call" | custom-call | flops 1 | bytes 1 | tf_op jit(solution)/shard_map/near_b/pallas_call | solution.py:684
  6.8 0.8 %collective-permute-done.refs_0_.refs_1_ = f32[1,6,6,8,128]{4,3,2,1,0:T(8,128)S(1)} collective-permute-done((f32[1,6,6,8,128]{4,3,2,1,0:T(8,128)S(1)}, f32[1,6,6,8,128]{4,3,2,1,0:T(8,128)S(1)}, u32[]{:S(2)}, u32[]{:S(2)}) %collective-permute-start) | collective-permute-done | bytes 147488 | tf_op jit(solution)/shard_map/ppermute | solution.py:669
  7.6 1.8 %collective-permute-start.1 = (f32[1,50,8,128]{3,2,1,0:T(8,128)S(1)}, f32[1,50,8,128]{3,2,1,0:T(8,128)S(1)}, u32[]{:S(2)}, u32[]{:S(2)}) collective-permute-start(f32[1,50,8,128]{3,2,1,0:T(8,128)S(1)} %send.1), channel_id=1, source_target_pairs={{0,8},{1,2},{2,1},{3,4},{4,3},{5,6},{6,5},{7,15},{8,0},{9,10},{10,... | collective-permute-start | bytes 614408 | tf_op jit(solution)/shard_map/ppermute | solution.py:723
  9.4 0.0 collective-permute-done.3.refs_3_.refs_11_
  9.4 0.0 copy-done.1
  9.4 0.0 copy-done.2
  9.4 0.0 copy-done.3
  9.4 0.8 %weights.1 = (f32[14,8,128]{2,1,0:T(8,128)S(1)}, f32[130,8,128]{2,1,0:T(8,128)S(1)}, f32[6,28,8,128]{3,2,1,0:T(8,128)S(1)}, f32[6,4,8,128]{3,2,1,0:T(8,128)S(1)}) custom-call(s32[6]{0:T(128)S(1)} %copy-done.2, f32[4,14]{1,0:T(4,128)S(1)} %copy-done.1, f32[23]{0:T(128)S(1)} %copy-done.3, f32[1,3,8,8,128]{4,3,2,1,0:T(8,128)S(1)} %collective-permute-done.3.refs_3_.refs_11_), custom_call_target="tpu_custom_call" | custom-call | flops 1 | bytes 1 | tf_op jit(solution)/shard_map/weights/pallas_call | solution.py:694
  10.2 0.0 collective-permute-done.2.refs_0_.refs_12_
  10.3 1.0 %inner.1 = (f32[6,42,3,8,128]{4,3,2,1,0:T(8,128)S(1)}, f32[6,3,6,8,128]{4,3,2,1,0:T(8,128)S(1)}) custom-call(f32[1,3,8,8,128]{4,3,2,1,0:T(8,128)S(1)} %collective-permute-done.2.refs_0_.refs_12_, f32[6,28,8,128]{3,2,1,0:T(8,128)S(1)} %get-tuple-element.30.refs_1_.refs_8_.refs_7_, ...), custom_call_target="tpu_custom_call" | custom-call | flops 1 | bytes 1 | tf_op jit(solution)/shard_map/inner/pallas_call | solution.py:704
  11.3 1.3 %collective-permute-start.4 = (f32[1,22,8,128]{3,2,1,0:T(8,128)S(1)}, f32[1,22,8,128]{3,2,1,0:T(8,128)S(1)}, u32[]{:S(2)}, u32[]{:S(2)}) collective-permute-start(f32[1,22,8,128]{3,2,1,0:T(8,128)S(1)} %send_rest.1.refs_0_), channel_id=1, source_target_pairs={{0,8},{1,2},{2,1},{3,4},{4,3},{5,6},{6,5},{7,15},{8,0},{9,10},{10,... | collective-permute-start | bytes 270344 | tf_op jit(solution)/shard_map/ppermute | solution.py:723
  12.6 0.0 collective-permute-done.5.refs_2_
  12.6 0.7 %strain.1 = (f32[6,4,3,3,8,128]{5,4,3,2,1,0:T(8,128)S(1)}, f32[6,4,8,8,128]{4,3,2,1,0:T(8,128)S(1)}, f32[6,18,8,128]{3,2,1,0:T(8,128)S(1)}) custom-call(f32[1,22,8,128]{3,2,1,0:T(8,128)S(1)} %send_rest.1.refs_0_, f32[1,6,6,8,128]{4,3,2,1,0:T(8,128)S(1)} %collective-permute-done.refs_0_.refs_1_, f32[1,6,6,8,128]{4,3,2,1,0:T(8,128)S(1)} %collective-permute-done.5.refs_2_, ...), custom_call_target="tpu_custom_call" | custom-call | flops 1 | bytes 1 | tf_op jit(solution)/shard_map/strain/pallas_call | solution.py:728
  13.2 1.6 %early.1.refs_9_ = f32[6,3,8,8,128]{4,3,2,1,0:T(8,128)S(1)} custom-call(f32[6,4,3,6,8,128]{5,4,3,2,1,0:T(8,128)S(1)} %get-tuple-element.25.refs_1_.refs_2_.refs_3_.refs_0_, f32[6,4,3,2,8,128]{5,4,3,2,1,0:T(8,128)S(1)} %get-tuple-element.31.refs_3_.refs_4_.refs_1_, f32[6,4,3,3,8,128]{5,4,3,2,1,0:T(8,128)S(1)} %get-tuple-element.39.refs_2_, ...), custom_call_target="tpu_custom_call" | custom-call | flops 2000000000 | bytes 1 | tf_op jit(solution)/shard_map/early/pallas_call | solution.py:738
  14.8 0.6 %collective-permute-done.1.refs_0_.refs_1_ = f32[1,50,8,128]{3,2,1,0:T(8,128)S(1)} collective-permute-done((f32[1,50,8,128]{3,2,1,0:T(8,128)S(1)}, f32[1,50,8,128]{3,2,1,0:T(8,128)S(1)}, u32[]{:S(2)}, u32[]{:S(2)}) %collective-permute-start.1) | collective-permute-done | bytes 204832 | tf_op jit(solution)/shard_map/ppermute | solution.py:723
  15.4 0.8 %late.1.refs_11_ = f32[3,4,64,128]{3,2,1,0:T(8,128)S(1)} custom-call(f32[1,50,8,128]{3,2,1,0:T(8,128)S(1)} %collective-permute-done.1.refs_0_.refs_1_, f32[1,50,8,128]{3,2,1,0:T(8,128)S(1)} %collective-permute-done.1.refs_0_.refs_1_, f32[6,4,3,6,8,128]{5,4,3,2,1,0:T(8,128)S(1)} %get-tuple-element.25.refs_1_.refs_2_.refs_3_.refs_0_, ...), custom_call_target="tpu_custom_call" | custom-call | flops 2000000000 | bytes 1 | tf_op jit(solution)/shard_map/late/pallas_call | solution.py:761
  16.2 0.6 %collective-permute-done.4.refs_1_ = f32[1,22,8,128]{3,2,1,0:T(8,128)S(1)} collective-permute-done((f32[1,22,8,128]{3,2,1,0:T(8,128)S(1)}, f32[1,22,8,128]{3,2,1,0:T(8,128)S(1)}, u32[]{:S(2)}, u32[]{:S(2)}) %collective-permute-start.4) | collective-permute-done | bytes 90144 | tf_op jit(solution)/shard_map/ppermute | solution.py:723
  16.8 1.1 %late_rest.1 = f32[3,6,64,128]{3,2,1,0:T(8,128)} custom-call(f32[1,50,8,128]{3,2,1,0:T(8,128)S(1)} %collective-permute-done.1.refs_0_.refs_1_, f32[1,22,8,128]{3,2,1,0:T(8,128)S(1)} %collective-permute-done.4.refs_1_, f32[6,4,3,6,8,128]{5,4,3,2,1,0:T(8,128)S(1)} %get-tuple-element.25.refs_1_.refs_2_.refs_3_.refs_0_, ...), custom_call_target="tpu_custom_call" | custom-call | flops 2000000000 | bytes 1 | tf_op jit(solution)/shard_map/late_rest/pallas_call | solution.py:761
  (3 shorter events, 0.1 us)
Async XLA Ops:
  0.0 1.1 %copy-start = (f32[3,6,8,1024]{3,2,1,0:T(8,128)S(1)}, f32[3,6,8,1024]{3,2,1,0:T(8,128)}, u32[]{:S(2)}) copy-start(f32[3,6,8,1024]{3,2,1,0:T(8,128)} %param.4) | copy-start | bytes 1769476
  1.1 6.5 %collective-permute-start = (f32[1,6,6,8,128]{4,3,2,1,0:T(8,128)S(1)}, f32[1,6,6,8,128]{4,3,2,1,0:T(8,128)S(1)}, u32[]{:S(2)}, u32[]{:S(2)}) collective-permute-start(f32[1,6,6,8,128]{4,3,2,1,0:T(8,128)S(1)} %pack.1.refs_0_), channel_id=1, source_target_pairs={{0,1},{1,0},{2,3},{3,2},{4,5},{5,4},{6,7},{7,6},{8,9},{9,8},{10,11... | collective-permute-start | bytes 442376 | tf_op jit(solution)/shard_map/ppermute | solution.py:669
  3.7 8.8 %collective-permute-start.5 = (f32[1,6,6,8,128]{4,3,2,1,0:T(8,128)S(1)}, f32[1,6,6,8,128]{4,3,2,1,0:T(8,128)S(1)}, u32[]{:S(2)}, u32[]{:S(2)}) collective-permute-start(f32[1,6,6,8,128]{4,3,2,1,0:T(8,128)S(1)} %get-tuple-element.38), channel_id=1, source_target_pairs={{0,1},{1,0},{2,3},{3,2},{4,5},{5,4},{6,7},{7,6},{8,9},{9,8},{10,11... | collective-permute-start | bytes 442376 | tf_op jit(solution)/shard_map/ppermute | solution.py:680
  4.3 5.1 %collective-permute-start.3 = (f32[1,3,8,8,128]{4,3,2,1,0:T(8,128)S(1)}, f32[1,3,8,8,128]{4,3,2,1,0:T(8,128)S(1)}, u32[]{:S(2)}, u32[]{:S(2)}) collective-permute-start(f32[1,3,8,8,128]{4,3,2,1,0:T(8,128)S(1)} %get-tuple-element.29), channel_id=1, source_target_pairs={{0,8},{8,0},{16,24},{24,16},{1,9},{9,1},{17,25},{25,17},{2,10},{10... | collective-permute-start | bytes 294920 | tf_op jit(solution)/shard_map/ppermute | solution.py:682
  4.3 6.0 %collective-permute-start.2 = (f32[1,3,8,8,128]{4,3,2,1,0:T(8,128)S(1)}, f32[1,3,8,8,128]{4,3,2,1,0:T(8,128)S(1)}, u32[]{:S(2)}, u32[]{:S(2)}) collective-permute-start(f32[1,3,8,8,128]{4,3,2,1,0:T(8,128)S(1)} %get-tuple-element.28), channel_id=1, source_target_pairs={{8,16},{16,8},{0,24},{24,0},{9,17},{17,9},{1,25},{25,1},{10,18},{1... | collective-permute-start | bytes 294920 | tf_op jit(solution)/shard_map/ppermute | solution.py:681
  5.9 3.5 %copy-start.1 = (f32[4,14]{1,0:T(4,128)S(1)}, f32[4,14]{1,0:T(4,128)}, u32[]{:S(2)}) copy-start(f32[4,14]{1,0:T(4,128)} %refs_1_.1) | copy-start | bytes 676
  5.9 3.5 %copy-start.2 = (s32[6]{0:T(128)S(1)}, s32[6]{0:T(128)}, u32[]{:S(2)}) copy-start(s32[6]{0:T(128)} %refs_0_.1) | copy-start | bytes 76
  5.9 3.5 %copy-start.3 = (f32[23]{0:T(128)S(1)}, f32[23]{0:T(128)}, u32[]{:S(2)}) copy-start(f32[23]{0:T(128)} %refs_2_.1) | copy-start | bytes 280
  7.6 7.8 %collective-permute-start.1 = (f32[1,50,8,128]{3,2,1,0:T(8,128)S(1)}, f32[1,50,8,128]{3,2,1,0:T(8,128)S(1)}, u32[]{:S(2)}, u32[]{:S(2)}) collective-permute-start(f32[1,50,8,128]{3,2,1,0:T(8,128)S(1)} %send.1), channel_id=1, source_target_pairs={{0,8},{1,2},{2,1},{3,4},{4,3},{5,6},{6,5},{7,15},{8,0},{9,10},{10,... | collective-permute-start | bytes 614408 | tf_op jit(solution)/shard_map/ppermute | solution.py:723
  11.3 5.5 %collective-permute-start.4 = (f32[1,22,8,128]{3,2,1,0:T(8,128)S(1)}, f32[1,22,8,128]{3,2,1,0:T(8,128)S(1)}, u32[]{:S(2)}, u32[]{:S(2)}) collective-permute-start(f32[1,22,8,128]{3,2,1,0:T(8,128)S(1)} %send_rest.1.refs_0_), channel_id=1, source_target_pairs={{0,8},{1,2},{2,1},{3,4},{4,3},{5,6},{6,5},{7,15},{8,0},{9,10},{10,... | collective-permute-start | bytes 270344 | tf_op jit(solution)/shard_map/ppermute | solution.py:723
